TPU v7x, 32 devices: a whole 2x2x4 slice. The times are simulated.
32 devices in a mesh: curve: 8 (over z, y), near: 4 (over x, core).
Axes of the slice: x: 2, y: 2, z: 4, core: 2. Of those that a mesh axis runs over, the one named last changes fastest.
Arguments:
- primitive: float32 [6, 16, 24576], P(None, 'near', 'curve'), may hold values from -2 to 2, as said below
- conductivity: float32 [16, 24576], P('near', 'curve'), may hold values from 0.05 to 0.5
- new_owner: int32 [24], P('curve'), may hold values from 0 to 7, as said below
Outputs:
- regridded: float32 [8, 6, 16, 4096], P('curve', None, 'near')
Inputs may be any that keep to these rules, and one draw needn't show every extreme that they name: `primitive`: fields in order: density and pressure within 0.5 to 2, three velocity components within -2 to 2, tracer concentration within 0 to 1. `new_owner`: before the regrid box column b lies on curve segment b // 3. Its new owner is that segment, except that the first box column of a segment c >= 1 may go to c - 1. Some segment ends with 4 box columns and some with 2.
All inputs are finite; a program needn't handle non-finite values.
Results may differ from a plain program's by a relative error of at most 0.0003.
Values sent between devices are 32-bit elements; how exact they have to be, the bound alone decides.
No kernel may reach another device: no remote copies, remote signals or barrier semaphores. Data moves between devices by JAX's collectives and lax.ppermute only.
A program may use at most 64 MiB of HBM per device.

v0:
```python
import jax
import jax.numpy as jnp
from jax import lax
from jax.sharding import PartitionSpec as P

BW = 32


GAMMA = 1.4
COURANT = 0.8


def extended_2(x, sides, width, wrap):
    for axis, dim in sides:
        devices, length = (lax.axis_size(axis), x.shape[dim])
        up = [(i, (i + 1) % devices) for i in range(devices if wrap else devices - 1)]
        down = [(j, i) for i, j in up]
        last = lax.slice_in_dim(x, length - width, length, axis=dim)
        first = lax.slice_in_dim(x, 0, width, axis=dim)
        before = lax.ppermute(last, axis, up)
        after = lax.ppermute(first, axis, down)
        x = jnp.concatenate([before, x, after], axis=dim)
    return x


def shifted(block, axis, distance):
    devices = range(lax.axis_size(axis))
    route = [(i - distance, i) for i in devices if i - distance in devices]
    return lax.ppermute(block, axis, route)


def to_conserved(prim):
    specific_weight_field = prim[0]
    velocity = prim[1:4]
    normal_stress_field = prim[4]
    momentum = specific_weight_field[None] * velocity
    energy = normal_stress_field / (GAMMA - 1.0) + 0.5 * specific_weight_field * jnp.sum(
        velocity * velocity, axis=0
    )
    tracer = specific_weight_field * prim[5]
    return jnp.concatenate(
        [specific_weight_field[None], momentum, energy[None], tracer[None]], axis=0
    )


def wave_bound(prim):
    sound = jnp.sqrt(GAMMA * prim[4] / prim[0])
    return jnp.abs(prim[1]) + jnp.abs(prim[2]) + jnp.abs(prim[3]) + 3.0 * sound


def roll_upper(values, ypos, ghost_layer_depth):
    return jnp.where(
        ypos == ghost_layer_depth - 1,
        jnp.roll(values, ghost_layer_depth - 1, axis=-1),
        jnp.roll(values, -1, axis=-1),
    )


def roll_lower(values, ypos, ghost_layer_depth):
    return jnp.where(
        ypos == 0, jnp.roll(values, 1 - ghost_layer_depth, axis=-1), jnp.roll(values, 1, axis=-1)
    )


def face_flux(
    lower_u, upper_u, lower_f, upper_f, lower_s, upper_s, lower_k, upper_k, lower_t, upper_t
):
    flux = 0.5 * (lower_f + upper_f) - 0.5 * jnp.maximum(lower_s, upper_s)[None] * (
        upper_u - lower_u
    )
    heat = 0.5 * (lower_k + upper_k) * (upper_t - lower_t)
    return flux.at[4].add(-heat)


def compute_rate(extended, ext_kappa, ghost_layer_depth):
    specific_weight_field = extended[0]
    velocity = extended[1:4] / specific_weight_field[None]
    kinetic = 0.5 * jnp.sum(extended[1:4] * velocity, axis=0)
    normal_stress_field = (GAMMA - 1.0) * (extended[4] - kinetic)
    sound = jnp.sqrt(GAMMA * normal_stress_field / specific_weight_field)
    thermal_state_kelvin = normal_stress_field / specific_weight_field

    def physical(direction):
        speed_dir = velocity[direction]
        fluxes = extended * speed_dir[None]
        fluxes = fluxes.at[1 + direction].add(normal_stress_field)
        fluxes = fluxes.at[4].add(normal_stress_field * speed_dir)
        return (fluxes, jnp.abs(speed_dir) + sound)

    fluxes, signal = physical(0)
    rows_u = extended[:, 1:-1]
    rows_f = fluxes[:, 1:-1]
    rows_s = signal[1:-1]
    rows_k = ext_kappa[1:-1]
    horizontal_line_number = thermal_state_kelvin[1:-1]
    faces = face_flux(
        rows_u[..., :-ghost_layer_depth],
        rows_u[..., ghost_layer_depth:],
        rows_f[..., :-ghost_layer_depth],
        rows_f[..., ghost_layer_depth:],
        rows_s[..., :-ghost_layer_depth],
        rows_s[..., ghost_layer_depth:],
        rows_k[..., :-ghost_layer_depth],
        rows_k[..., ghost_layer_depth:],
        horizontal_line_number[..., :-ghost_layer_depth],
        horizontal_line_number[..., ghost_layer_depth:],
    )
    total = faces[..., ghost_layer_depth:] - faces[..., :-ghost_layer_depth]
    fluxes, signal = physical(2)
    cols_u = extended[..., ghost_layer_depth:-ghost_layer_depth]
    cols_f = fluxes[..., ghost_layer_depth:-ghost_layer_depth]
    cols_s = signal[..., ghost_layer_depth:-ghost_layer_depth]
    cols_k = ext_kappa[..., ghost_layer_depth:-ghost_layer_depth]
    vertical_count_grid = thermal_state_kelvin[..., ghost_layer_depth:-ghost_layer_depth]
    faces = face_flux(
        cols_u[:, :-1],
        cols_u[:, 1:],
        cols_f[:, :-1],
        cols_f[:, 1:],
        cols_s[:-1],
        cols_s[1:],
        cols_k[:-1],
        cols_k[1:],
        vertical_count_grid[:-1],
        vertical_count_grid[1:],
    )
    total = total + faces[:, 1:] - faces[:, :-1]
    fluxes, signal = physical(1)
    inner_u = extended[:, 1:-1, ghost_layer_depth:-ghost_layer_depth]
    inner_f = fluxes[:, 1:-1, ghost_layer_depth:-ghost_layer_depth]
    inner_s = signal[1:-1, ghost_layer_depth:-ghost_layer_depth]
    inner_k = ext_kappa[1:-1, ghost_layer_depth:-ghost_layer_depth]
    core_cell_number = thermal_state_kelvin[1:-1, ghost_layer_depth:-ghost_layer_depth]
    ypos = jnp.arange(inner_u.shape[-1]) % ghost_layer_depth
    faces = face_flux(
        inner_u,
        roll_upper(inner_u, ypos, ghost_layer_depth),
        inner_f,
        roll_upper(inner_f, ypos, ghost_layer_depth),
        inner_s,
        roll_upper(inner_s, ypos, ghost_layer_depth),
        inner_k,
        roll_upper(inner_k, ypos, ghost_layer_depth),
        core_cell_number,
        roll_upper(core_cell_number, ypos, ghost_layer_depth),
    )
    total = total + faces - roll_lower(faces, ypos, ghost_layer_depth)
    return -total


def section_rate(state, kappa, box_count, segment, segments):
    ghost_layer_depth = BW
    box_cells = ghost_layer_depth * ghost_layer_depth
    depth = state.shape[1]
    joined = jnp.concatenate([state, kappa[None]], axis=0)
    first_plane = joined[:, :, :ghost_layer_depth]
    last_plane = lax.dynamic_slice_in_dim(
        joined, box_count * box_cells - ghost_layer_depth, ghost_layer_depth, 2
    )
    packet = jnp.stack([first_plane, last_plane]).reshape(2, 7, depth * ghost_layer_depth)
    framed = extended_2(packet, (("curve", 0),), 1, False)
    from_before = jnp.where(segment == 0, packet[0], framed[0]).reshape(7, depth, ghost_layer_depth)
    from_after = jnp.where(segment == segments - 1, packet[1], framed[3]).reshape(
        7, depth, ghost_layer_depth
    )
    z_edges = jnp.stack([joined[:, 0], joined[:, -1]])
    z_wrapped = extended_2(z_edges, (("near", 0),), 1, True)
    stacked = jnp.concatenate([z_wrapped[0][:, None], joined, z_wrapped[3][:, None]], axis=1)
    before_col = jnp.pad(from_before, ((0, 0), (1, 1), (0, 0)), mode="edge")
    after_col = jnp.pad(from_after, ((0, 0), (1, 1), (0, 0)), mode="edge")
    broad = jnp.concatenate([before_col, stacked, after_col], axis=2)
    broad = lax.dynamic_update_slice_in_dim(
        broad, after_col, ghost_layer_depth + box_count * box_cells, 2
    )
    return compute_rate(broad[:6], broad[6], ghost_layer_depth)


def advance(state, kappa, box_count, time_step, segment, segments):
    half = state + time_step * section_rate(state, kappa, box_count, segment, segments)
    return 0.5 * state + 0.5 * (
        half + time_step * section_rate(half, kappa, box_count, segment, segments)
    )


def regroup(block, incoming, leaving, arriving, box_cells):
    last_axis = block.ndim - 1
    stacked = jnp.concatenate(
        [block, incoming * arriving.astype(block.dtype), jnp.zeros_like(incoming)], axis=last_axis
    )
    return lax.dynamic_slice_in_dim(
        stacked, leaving * box_cells, block.shape[last_axis] + box_cells, last_axis
    )


def local(primitive, conductivity, new_owner):
    segment = lax.axis_index("curve")
    segments = lax.axis_size("curve")
    box_cells = BW * BW
    held_boxes = primitive.shape[2] // box_cells
    top_speed = jnp.max(wave_bound(primitive))
    top_kappa = jnp.max(conductivity)
    top_speed, top_kappa = lax.pmax((top_speed, top_kappa), ("curve", "near"))
    time_step = COURANT / (top_speed + 6.0 * top_kappa)
    leaving = (new_owner[0] != segment).astype(jnp.int32)
    cell_slot = jnp.arange((held_boxes + 1) * box_cells) // box_cells
    final = advance(to_conserved(primitive), conductivity, held_boxes, time_step, segment, segments)
    arrived = shifted((final[:, :, :box_cells], new_owner[0:1]), "curve", -1)
    arriving = ((arrived[1][0] == segment) & (segment < segments - 1)).astype(jnp.int32)
    box_count = held_boxes - leaving + arriving
    valid = cell_slot < box_count
    result = jnp.where(
        valid[None, None, :], regroup(final, arrived[0], leaving, arriving, box_cells), 0.0
    )
    return result[None]


def solution(mesh):
    in_specs = (P(None, "near", "curve"), P("near", "curve"), P("curve"))
    out_specs = P("curve", None, "near", None)
    return jax.shard_map(local, mesh=mesh, in_specs=in_specs, out_specs=out_specs, check_vma=False)
```

profile of v0, /device:TPU:0, one launch (start us, length us, event | category | flops | bytes accessed | tf_op | source)
XLA Modules:
  0.0 95.9 jit_solution(1617639988642084619)
XLA Ops:
  0.0 0.8 fusion.106
  0.8 1.0 %constant_dynamic-update-slice_fusion.3 = (f32[7,4,3072]{2,1,0:T(4,128)S(1)}, f32[3,4,3072]{2,1,0:T(4,128)S(1)}, f32[4,3072]{1,0:T(4,128)S(1)}) fusion(f32[7,4,3072]{2,1,0:T(4,128)S(1)} %get-tuple-element.279, f32[6,4,3072]{2,1,0:T(4,128)} %param.39, f32[4,3072]{1,0:T(4,128)S(1)} %get-tuple-element.278), kind=kLoop, calls=%fused_computation.230 | loop fusion | flops 98304 | bytes 540672
  2.0 0.8 copy-done
  2.9 1.3 %collective-permute-start.4 = (f32[1,7,128]{2,1,0:T(8,128)S(1)}, f32[1,7,128]{2,1,0:T(8,128)S(1)}, u32[]{:S(2)}, u32[]{:S(2)}) collective-permute-start(f32[1,7,128]{2,1,0:T(8,128)S(1)} %slice.1004), channel_id=1, source_target_pairs={{4,0},{8,4},{12,8},{16,12},{20,16},{24,20},{28,24},{5,1},{9,5},{13... | collective-permute-start | bytes 10760 | tf_op jit(solution)/shard_map/ppermute | solution.py:21
  4.3 5.5 %collective-permute-start.1 = (f32[1,7,128]{2,1,0:T(8,128)S(1)}, f32[1,7,128]{2,1,0:T(8,128)S(1)}, u32[]{:S(2)}, u32[]{:S(2)}) collective-permute-start(f32[1,7,128]{2,1,0:T(8,128)S(1)} %slice.999), channel_id=1, source_target_pairs={{0,4},{4,8},{8,12},{12,16},{16,20},{20,24},{24,28},{1,5},{5,9},{9,... | collective-permute-start | bytes 10760 | tf_op jit(solution)/shard_map/ppermute | solution.py:20
  9.9 0.9 collective-permute-start.3
  11.5 1.3 %collective-permute-start = (s32[1]{0:T(128)S(1)}, s32[1]{0:T(128)}, u32[]{:S(2)}, u32[]{:S(2)}) collective-permute-start(s32[1]{0:T(128)S(1)} %bitcast.158), channel_id=1, source_target_pairs={{4,0},{8,4},{12,8},{16,12},{20,16},{24,20},{28,24},{5,1},{9,5},{13... | collective-permute-start | bytes 20 | tf_op jit(solution)/shard_map/ppermute | solution.py:29
  12.8 0.7 fusion.91
  13.5 0.7 reduce_max.19
  14.2 42.8 %all-reduce = (f32[]{:T(128)}, f32[]{:T(128)}) all-reduce(f32[]{:T(128)} %fusion.91, f32[]{:T(128)} %reduce_max.19), channel_id=1, replica_groups=mesh['curve'=8,'near'=4] {'curve','near'}, use_global_device_ids=true, to_apply=%region_2.0 | all-reduce | flops 2 | bytes 16 | tf_op jit(solution)/shard_map/pmax | solution.py:202
  60.0 1.2 %dynamic_update_slice.6 = f32[7,6,3136]{2,1,0:T(8,128)S(1)} dynamic-update-slice(f32[7,6,3136]{2,1,0:T(8,128)S(1)} %concatenate.157, f32[7,6,32]{2,1,0:T(8,128)S(1)} %get-tuple-element.294, s32[]{:T(128)} %constant.455.clone.1, s32[]{:T(128)} %constant.455.clone.1, s32[]{:T(128)} %constant.470.clone.1) | dynamic-update-slice | bytes 10756 | tf_op jit(solution)/shard_map/dynamic_update_slice | solution.py:172
  64.1 0.7 fusion.27
  65.4 0.7 fusion.4
  67.5 1.3 %collective-permute-start.8 = (f32[1,7,128]{2,1,0:T(8,128)S(1)}, f32[1,7,128]{2,1,0:T(8,128)S(1)}, u32[]{:S(2)}, u32[]{:S(2)}) collective-permute-start(f32[1,7,128]{2,1,0:T(8,128)S(1)} %slice.1085), channel_id=1, source_target_pairs={{4,0},{8,4},{12,8},{16,12},{20,16},{24,20},{28,24},{5,1},{9,5},{13... | collective-permute-start | bytes 10760 | tf_op jit(solution)/shard_map/ppermute | solution.py:21
  68.9 0.9 collective-permute-start.7
  69.8 3.7 %collective-permute-done.8 = f32[1,7,128]{2,1,0:T(8,128)S(1)} collective-permute-done((f32[1,7,128]{2,1,0:T(8,128)S(1)}, f32[1,7,128]{2,1,0:T(8,128)S(1)}, u32[]{:S(2)}, u32[]{:S(2)}) %collective-permute-start.8) | collective-permute-done | bytes 3616 | tf_op jit(solution)/shard_map/ppermute | solution.py:21
  73.7 5.0 %collective-permute-start.5 = (f32[1,7,128]{2,1,0:T(8,128)S(1)}, f32[1,7,128]{2,1,0:T(8,128)S(1)}, u32[]{:S(2)}, u32[]{:S(2)}) collective-permute-start(f32[1,7,128]{2,1,0:T(8,128)S(1)} %slice.1080), channel_id=1, source_target_pairs={{0,4},{4,8},{8,12},{12,16},{16,20},{20,24},{24,28},{1,5},{5,9},{9,... | collective-permute-start | bytes 10760 | tf_op jit(solution)/shard_map/ppermute | solution.py:20
  78.8 1.1 %collective-permute-done.5 = f32[1,7,128]{2,1,0:T(8,128)S(1)} collective-permute-done((f32[1,7,128]{2,1,0:T(8,128)S(1)}, f32[1,7,128]{2,1,0:T(8,128)S(1)}, u32[]{:S(2)}, u32[]{:S(2)}) %collective-permute-start.5) | collective-permute-done | bytes 3616 | tf_op jit(solution)/shard_map/ppermute | solution.py:20
  80.7 1.2 %dynamic_update_slice.7 = f32[7,6,3136]{2,1,0:T(8,128)S(1)} dynamic-update-slice(f32[7,6,3136]{2,1,0:T(8,128)S(1)} %concatenate.174, f32[7,6,32]{2,1,0:T(8,128)S(1)} %pad_maximum_fusion.7, s32[]{:T(128)} %constant.455.clone.1, s32[]{:T(128)} %constant.455.clone.1, s32[]{:T(128)} %constant.470.clone.1) | dynamic-update-slice | bytes 10756 | tf_op jit(solution)/shard_map/dynamic_update_slice | solution.py:172
  84.7 0.7 fusion.17
  86.1 0.7 fusion.1
  88.1 1.3 %collective-permute-start.9 = (f32[6,4,1024]{2,1,0:T(4,128)S(1)}, f32[6,4,1024]{2,1,0:T(4,128)S(1)}, u32[]{:S(2)}, u32[]{:S(2)}) collective-permute-start(f32[6,4,1024]{2,1,0:T(4,128)S(1)} %slice.1314), channel_id=1, source_target_pairs={{4,0},{8,4},{12,8},{16,12},{20,16},{24,20},{28,24},{5,1},{9,5},{13... | collective-permute-start | bytes 294920 | tf_op jit(solution)/shard_map/ppermute | solution.py:29
  89.5 5.5 %collective-permute-done.9 = f32[6,4,1024]{2,1,0:T(4,128)S(1)} collective-permute-done((f32[6,4,1024]{2,1,0:T(4,128)S(1)}, f32[6,4,1024]{2,1,0:T(4,128)S(1)}, u32[]{:S(2)}, u32[]{:S(2)}) %collective-permute-start.9) | collective-permute-done | bytes 98336 | tf_op jit(solution)/shard_map/ppermute | solution.py:29
  94.9 0.9 fusion.9
  (132 shorter events, 12.8 us)
Async XLA Ops:
  0.8 1.1 %copy-start.1 = (f32[6,4,3072]{2,1,0:T(4,128)S(1)}, f32[6,4,3072]{2,1,0:T(4,128)}, u32[]{:S(2)}) copy-start(f32[6,4,3072]{2,1,0:T(4,128)} %param.39) | copy-start | bytes 884740
  1.9 0.8 copy-start
  2.9 56.1 %collective-permute-start.4 = (f32[1,7,128]{2,1,0:T(8,128)S(1)}, f32[1,7,128]{2,1,0:T(8,128)S(1)}, u32[]{:S(2)}, u32[]{:S(2)}) collective-permute-start(f32[1,7,128]{2,1,0:T(8,128)S(1)} %slice.1004), channel_id=1, source_target_pairs={{4,0},{8,4},{12,8},{16,12},{20,16},{24,20},{28,24},{5,1},{9,5},{13... | collective-permute-start | bytes 10760 | tf_op jit(solution)/shard_map/ppermute | solution.py:21
  4.3 54.8 %collective-permute-start.1 = (f32[1,7,128]{2,1,0:T(8,128)S(1)}, f32[1,7,128]{2,1,0:T(8,128)S(1)}, u32[]{:S(2)}, u32[]{:S(2)}) collective-permute-start(f32[1,7,128]{2,1,0:T(8,128)S(1)} %slice.999), channel_id=1, source_target_pairs={{0,4},{4,8},{8,12},{12,16},{16,20},{20,24},{24,28},{1,5},{5,9},{9,... | collective-permute-start | bytes 10760 | tf_op jit(solution)/shard_map/ppermute | solution.py:20
  9.9 49.4 %collective-permute-start.3 = (f32[1,7,3072]{2,0,1:T(1,128)S(1)}, f32[1,7,3072]{2,0,1:T(1,128)S(1)}, u32[]{:S(2)}, u32[]{:S(2)}) collective-permute-start(f32[1,7,3072]{2,0,1:T(1,128)S(1)} %get-tuple-element.270), channel_id=1, source_target_pairs={{1,0},{2,1},{3,2},{0,3},{5,4},{6,5},{7,6},{4,7},{9,8},{10,9},{11,1... | collective-permute-start | bytes 258056 | tf_op jit(solution)/shard_map/ppermute | solution.py:21
  10.8 0.7 copy-start.2
  10.8 48.5 %collective-permute-start.2 = (f32[1,7,3072]{2,0,1:T(1,128)S(1)}, f32[1,7,3072]{2,0,1:T(1,128)S(1)}, u32[]{:S(2)}, u32[]{:S(2)}) collective-permute-start(f32[1,7,3072]{2,0,1:T(1,128)S(1)} %get-tuple-element.269), channel_id=1, source_target_pairs={{0,1},{1,2},{2,3},{3,0},{4,5},{5,6},{6,7},{7,4},{8,9},{9,10},{10,1... | collective-permute-start | bytes 258056 | tf_op jit(solution)/shard_map/ppermute | solution.py:20
  11.5 47.0 %collective-permute-start = (s32[1]{0:T(128)S(1)}, s32[1]{0:T(128)}, u32[]{:S(2)}, u32[]{:S(2)}) collective-permute-start(s32[1]{0:T(128)S(1)} %bitcast.158), channel_id=1, source_target_pairs={{4,0},{8,4},{12,8},{16,12},{20,16},{24,20},{28,24},{5,1},{9,5},{13... | collective-permute-start | bytes 20 | tf_op jit(solution)/shard_map/ppermute | solution.py:29
  67.5 6.0 %collective-permute-start.8 = (f32[1,7,128]{2,1,0:T(8,128)S(1)}, f32[1,7,128]{2,1,0:T(8,128)S(1)}, u32[]{:S(2)}, u32[]{:S(2)}) collective-permute-start(f32[1,7,128]{2,1,0:T(8,128)S(1)} %slice.1085), channel_id=1, source_target_pairs={{4,0},{8,4},{12,8},{16,12},{20,16},{24,20},{28,24},{5,1},{9,5},{13... | collective-permute-start | bytes 10760 | tf_op jit(solution)/shard_map/ppermute | solution.py:21
  68.9 11.1 %collective-permute-start.7 = (f32[1,7,3072]{2,0,1:T(1,128)S(1)}, f32[1,7,3072]{2,0,1:T(1,128)S(1)}, u32[]{:S(2)}, u32[]{:S(2)}) collective-permute-start(f32[1,7,3072]{2,0,1:T(1,128)S(1)} %get-tuple-element.264), channel_id=1, source_target_pairs={{1,0},{2,1},{3,2},{0,3},{5,4},{6,5},{7,6},{4,7},{9,8},{10,9},{11,1... | collective-permute-start | bytes 258056 | tf_op jit(solution)/shard_map/ppermute | solution.py:21
  69.8 10.2 %collective-permute-start.6 = (f32[1,7,3072]{2,0,1:T(1,128)S(1)}, f32[1,7,3072]{2,0,1:T(1,128)S(1)}, u32[]{:S(2)}, u32[]{:S(2)}) collective-permute-start(f32[1,7,3072]{2,0,1:T(1,128)S(1)} %get-tuple-element.263), channel_id=1, source_target_pairs={{0,1},{1,2},{2,3},{3,0},{4,5},{5,6},{6,7},{7,4},{8,9},{9,10},{10,1... | collective-permute-start | bytes 258056 | tf_op jit(solution)/shard_map/ppermute | solution.py:20
  73.7 6.1 %collective-permute-start.5 = (f32[1,7,128]{2,1,0:T(8,128)S(1)}, f32[1,7,128]{2,1,0:T(8,128)S(1)}, u32[]{:S(2)}, u32[]{:S(2)}) collective-permute-start(f32[1,7,128]{2,1,0:T(8,128)S(1)} %slice.1080), channel_id=1, source_target_pairs={{0,4},{4,8},{8,12},{12,16},{16,20},{20,24},{24,28},{1,5},{5,9},{9,... | collective-permute-start | bytes 10760 | tf_op jit(solution)/shard_map/ppermute | solution.py:20
  88.1 6.8 %collective-permute-start.9 = (f32[6,4,1024]{2,1,0:T(4,128)S(1)}, f32[6,4,1024]{2,1,0:T(4,128)S(1)}, u32[]{:S(2)}, u32[]{:S(2)}) collective-permute-start(f32[6,4,1024]{2,1,0:T(4,128)S(1)} %slice.1314), channel_id=1, source_target_pairs={{4,0},{8,4},{12,8},{16,12},{20,16},{24,20},{28,24},{5,1},{9,5},{13... | collective-permute-start | bytes 294920 | tf_op jit(solution)/shard_map/ppermute | solution.py:29
where the time goes:
time: 96.3 us; the launch traced here: 95.9 us
  blocking collectives  42.8 us (44%)
  starting transfers between devices  17.4 us (18%)
  other arithmetic  11.5 us (12%)
  local copies, waits for them, and re-layouts  11.3 us (12%)
  waiting for transfers between devices  10.3 us (11%)
  between operations  2.63 us (3%)
    pmax x1, blocking collectives, local(): top_speed, top_kappa = lax.pmax((top_speed, top_kappa), ('curve', 'near'))  42.8 us
    ppermute x4, starting transfers between devices, extended_2(): before = lax.ppermute(last, axis, up)  10.5 us
    ppermute x2, waiting for transfers between devices, shifted(): return lax.ppermute(block, axis, route)  5.46 us
    ppermute x4, starting transfers between devices, extended_2(): after = lax.ppermute(first, axis, down)  4.35 us
    ppermute x4, waiting for transfers between devices, extended_2(): after = lax.ppermute(first, axis, down)  3.7 us
    sub x6, other arithmetic, face_flux(): 0.5 * (lower_f + upper_f)  3.54 us
    ppermute x2, starting transfers between devices, shifted(): return lax.ppermute(block, axis, route)  2.57 us
    dynamic_update_slice x2, local copies, waits for them, and re-layouts, section_rate(): lax.dynamic_update_slice_in_dim(broad, after_col, ghost_layer_depth + box...  2.33 us
  transfers between devices with their start and end apart: 10, of which 3 were waited for; matrix products, arithmetic and copies ran while one was open for 3% of the time, Pallas kernels for 0%

commit v1 on v0

v1 whole, which is shorter than its diff:
```python
import functools

import jax
import jax.numpy as jnp
from jax import lax
from jax.experimental import pallas as pl
from jax.experimental.pallas import tpu as pltpu
from jax.sharding import PartitionSpec as P

BW = 32
LANES = 128
PLANES = LANES // BW
GAMMA = 1.4
COURANT = 0.8
NQ = 13
VX, PR, SND, TMP, KAP = 6, 9, 10, 11, 12
VMEM = pl.BlockSpec(memory_space=pltpu.VMEM)
SMEM = pl.BlockSpec(memory_space=pltpu.SMEM)
PARAMS = pltpu.CompilerParams(vmem_limit_bytes=24 * 1024 * 1024)


def f32(*shape):
    return jax.ShapeDtypeStruct(shape, jnp.float32)


def lanes_of(shape):
    return lax.broadcasted_iota(jnp.int32, shape, 1)


def rows_of(shape):
    return lax.broadcasted_iota(jnp.int32, shape, 0)


def pack_kernel(prim, kappa, flags, to_before, to_after, msg_a, msg_b, peak):
    even = lax.axis_index("near") % 2 == 0
    blocks = prim.shape[1] // 4

    def source(f):
        return (prim, (f,)) if f < 6 else (kappa, ())

    for f in range(7):
        ref, at = source(f)
        to_before[f, 0:36, :] = ref[at + (pl.ds(0, 36), slice(None))]
        to_after[f] = ref[at + (pl.ds(4 * blocks - 4, 4), slice(None))]
        for msg, start in ((msg_a, jnp.where(even, 2, 0)), (msg_b, jnp.where(even, 0, 2))):
            for z in range(2):
                for g in range(blocks // 8):
                    msg[f, z * blocks + 8 * g : z * blocks + 8 * g + 8, :] = ref[
                        at + (pl.ds(start + z + 32 * g, 8, stride=4), slice(None))
                    ]
    leaving = flags[0].astype(jnp.float32)
    to_before[:, 36:40, :] = jnp.full((7, 4, LANES), leaving, jnp.float32)
    speed = top = None
    for g in range(prim.shape[1] // 8):
        rows = pl.ds(8 * g, 8)
        sound = jnp.sqrt(GAMMA * prim[4, rows, :] / prim[0, rows, :])
        s = jnp.abs(prim[1, rows, :]) + jnp.abs(prim[2, rows, :]) + jnp.abs(prim[3, rows, :]) + 3.0 * sound
        k = kappa[rows, :]
        speed = s if speed is None else jnp.maximum(speed, s)
        top = k if top is None else jnp.maximum(top, k)
    peak[0:1, :] = jnp.max(speed, axis=0, keepdims=True)
    peak[1:2, :] = jnp.max(top, axis=0, keepdims=True)


def corner_kernel(right, left, corner_a, corner_b):
    even = lax.axis_index("near") % 2 == 0
    for msg, start in ((corner_a, jnp.where(even, 2, 0)), (corner_b, jnp.where(even, 0, 2))):
        for f in range(7):
            for z in range(2):
                msg[f, 16 * z : 16 * z + 8, :] = right[f, pl.ds(start + z, 8, stride=4), :]
                msg[f, pl.ds(16 * z + 8, 1), :] = right[f, pl.ds(32 + start + z, 1), :]
                msg[f, pl.ds(16 * z + 9, 1), :] = left[f, pl.ds(start + z, 1), :]


def up_x(q, lane, ghost):
    w = [pltpu.roll(v, LANES - BW, 1) for v in q[:4]]
    w.append(pltpu.roll(w[0], 7, 0))
    out = [jnp.where(lane < LANES - BW, w[j], w[j + 1]) for j in range(4)]
    return out + ([pltpu.roll(q[4], LANES - BW, 1)] if ghost else [])


def up_y(v, low):
    return jnp.where(low == BW - 1, pltpu.roll(v, BW - 1, 1), pltpu.roll(v, LANES - 1, 1))


def down_y(v, low):
    return jnp.where(low == 0, pltpu.roll(v, LANES - BW + 1, 1), pltpu.roll(v, 1, 1))


def flux(u, v, pressure, k, f):
    if f == 0:
        return u[1 + k]
    if f == 4:
        return (u[4] + pressure) * v[k]
    out = u[f] * v[k]
    return out + pressure if f == 1 + k else out


def face(lower_u, upper_u, lower_f, upper_f, speed, heat):
    out = (lower_f + upper_f) - speed * (upper_u - lower_u)
    return out if heat is None else out - heat


def z_sides(q, z, j):
    lower, upper = ([q[i, zz, j] for i in range(NQ)] for zz in (z, z + 1))
    speed = jnp.maximum(jnp.abs(lower[VX + 2]) + lower[SND], jnp.abs(upper[VX + 2]) + upper[SND])
    heat = (lower[KAP] + upper[KAP]) * (upper[TMP] - lower[TMP])
    return lower, upper, speed, heat


def z_faces(q, zf, z, slots):
    for j in range(slots):
        lower, upper, speed, heat = z_sides(q, z, j)
        for f in range(6):
            zf[f, j] = face(
                lower[f],
                upper[f],
                flux(lower[:6], lower[6:9], lower[PR], 2, f),
                flux(upper[:6], upper[6:9], upper[PR], 2, f),
                speed,
                heat if f == 4 else None,
            )


def divergence(q, zf, z, slots, emit):
    shape = (8, LANES)
    lane, row = lanes_of(shape), rows_of(shape)
    low = lane % BW
    ghost = 4
    five = range(5)
    at = lambda i, j: q[i, z, j]
    sx = [jnp.abs(at(VX, j)) + at(SND, j) for j in five]
    ax = [jnp.maximum(a, b) for a, b in zip(sx, up_x(sx, lane, True), strict=True)]
    kx, tx = [at(KAP, j) for j in five], [at(TMP, j) for j in five]
    hx = [
        (k + ku) * (tu - t)
        for k, ku, t, tu in zip(kx, up_x(kx, lane, True), tx, up_x(tx, lane, True), strict=True)
    ]
    ay, hy, az, hz = [], [], [], []
    for j in range(slots):
        s = jnp.abs(at(VX + 1, j)) + at(SND, j)
        ay.append(jnp.maximum(s, up_y(s, low)))
        hy.append((kx[j] + up_y(kx[j], low)) * (up_y(tx[j], low) - tx[j]))
        s0 = jnp.abs(at(VX + 2, j)) + at(SND, j)
        s1 = jnp.abs(q[VX + 2, z + 1, j]) + q[SND, z + 1, j]
        az.append(jnp.maximum(s0, s1))
        hz.append((kx[j] + q[KAP, z + 1, j]) * (q[TMP, z + 1, j] - tx[j]))
    for f in range(6):

        def physical(j, k, zz):
            u = {i: q[i, zz, j] for i in {f, 1 + k}}
            return flux(u, {k: q[VX + k, zz, j]}, q[PR, zz, j], k, f)

        heat = lambda h: h if f == 4 else None
        u = [at(f, j) for j in five]
        fx = [physical(j, 0, z) for j in five]
        uu, fu = up_x(u, lane, True), up_x(fx, lane, True)
        gx = [face(u[j], uu[j], fx[j], fu[j], ax[j], heat(hx[j])) for j in five]
        gx[3] = jnp.where((lane >= LANES - BW) & (row == 7), gx[ghost], gx[3])
        d = [pltpu.roll(g, BW, 1) for g in gx]
        before = jnp.where(row == 0, d[ghost], pltpu.roll(d[3], 1, 0))
        dx = [jnp.where(lane >= BW, d[j], before if j == 0 else d[j - 1]) for j in range(4)] + [d[ghost]]
        for j in range(slots):
            fy = physical(j, 1, z)
            gy = face(u[j], up_y(u[j], low), fy, up_y(fy, low), ay[j], heat(hy[j]))
            gz = face(u[j], q[f, z + 1, j], physical(j, 2, z), physical(j, 2, z + 1), az[j], heat(hz[j]))
            total = (gx[j] - dx[j]) + (gy - down_y(gy, low)) + (gz - zf[f, j])
            zf[f, j] = gz
            emit(f, j, total)


def first_kernel(
    prim, kappa, right, left, rec_a, rec_b, cor_a, cor_b, state, total, conduct, arrival, ext, q, zf
):
    segment, segments = lax.axis_index("curve"), lax.axis_size("curve")
    even = lax.axis_index("near") % 2 == 0
    blocks = prim.shape[1] // 4
    shape = (8, LANES)
    lane, row = lanes_of(shape), rows_of(shape)
    first, last = segment == 0, segment == segments - 1
    base_a, base_b = jnp.where(even, 6, 0), jnp.where(even, 0, 6)
    spread = lambda x: jnp.broadcast_to(x, shape)

    arrival[...] = jnp.where(last, 0.0, spread(right[0, 36:37, :]))

    def fill(f, z, own, box, beyond, behind):
        edge = spread(own[-1][7:8])
        box = jnp.where(last, pltpu.roll(edge, BW, 1), box)
        for g, rows in enumerate(own + [box]):
            ext[f, z, 8 * g : 8 * g + 8, :] = rows
        start, end = spread(own[0][0:1]), spread(box[7:8])
        behind = jnp.where(first, pltpu.roll(start, LANES - BW, 1), spread(behind))
        low_side = jnp.where(lane < BW, start, behind)
        high_side = jnp.where(lane >= LANES - BW, end, spread(beyond))
        ext[f, z, 32:40, :] = jnp.where(row == 7, high_side, low_side)

    for f in range(7):
        ref, at = (prim, (f,)) if f < 6 else (kappa, ())
        for z in range(4):
            own = [ref[at + (pl.ds(z + 32 * g, 8, stride=4), slice(None))] for g in range(blocks // 8)]
            fill(
                f, z + 2, own, right[f, pl.ds(z, 8, stride=4), :], right[f, 32 + z : 33 + z, :], left[f, z : z + 1, :]
            )
        for rec, cor, base in ((rec_a, cor_a, base_a), (rec_b, cor_b, base_b)):
            for z in range(2):
                own = [rec[f, z * blocks + 8 * g : z * blocks + 8 * g + 8, :] for g in range(blocks // 8)]
                c = 16 * z
                fill(
                    f, base + z, own, cor[f, c : c + 8, :], cor[f, c + 8 : c + 9, :], cor[f, c + 9 : c + 10, :]
                )

    @pl.loop(0, 8)
    def _(z):
        for j in range(5):
            rows = pl.ds(j, 8, stride=4) if j < 4 else pl.ds(32, 8)
            r, vx, vy, vz, p, s, k = (ext[f, z, rows, :] for f in range(7))
            t = p / r
            u = (r, r * vx, r * vy, r * vz, p / (GAMMA - 1.0) + 0.5 * r * (vx * vx + vy * vy + vz * vz), r * s)
            for i, value in enumerate(u + (vx, vy, vz, p, jnp.sqrt(GAMMA * t), t, k)):
                q[i, z, j] = value

    z_faces(q, zf, 0, 5)

    @pl.loop(1, 7)
    def _(z):
        def emit(f, j, value):
            total[f, z - 1, j] = value
            state[f, z - 1, j] = q[f, z, j]

        divergence(q, zf, z, 5, emit)
        for j in range(5):
            conduct[z - 1, j] = q[KAP, z, j]


def second_kernel(state, total, conduct, arrival, peak, flags, out, q, zf, final, sem):
    segment, segments = lax.axis_index("curve"), lax.axis_size("curve")
    shape = (8, LANES)
    lane, row = lanes_of(shape), rows_of(shape)
    first, last = segment == 0, segment == segments - 1
    speed, top = jnp.max(peak[0:1, :]), jnp.max(peak[1:2, :])
    step = COURANT / (speed + 6.0 * top)
    own_boxes = 3 * LANES

    @pl.loop(0, 6)
    def _(z):
        half = [[state[f, z, j] - (0.5 * step) * total[f, z, j] for j in range(5)] for f in range(6)]
        kap = [conduct[z, j] for j in range(5)]
        for u in half + [kap]:
            edge = pltpu.roll(pltpu.roll(u[3], BW, 1), 1, 0)
            u[0] = jnp.where(last & (row == 6) & (lane < BW), edge, u[0])
            g = jnp.where((row == 0) & (lane < BW), u[0], u[4])
            g = jnp.where((row == 7) & (lane >= LANES - BW), u[3], g)
            u[4] = jnp.where(first & (row == 0) & (lane >= BW), pltpu.roll(g, LANES - BW, 1), g)
        for j in range(5):
            r, mx, my, mz, e, s = (half[f][j] for f in range(6))
            inv = 1.0 / r
            vx, vy, vz = mx * inv, my * inv, mz * inv
            p = (GAMMA - 1.0) * (e - 0.5 * (mx * vx + my * vy + mz * vz))
            t = p * inv
            values = (r, mx, my, mz, e, s, vx, vy, vz, p, jnp.sqrt(GAMMA * t), t, kap[j])
            for i, value in enumerate(values):
                q[i, z, j] = value

    z_faces(q, zf, 0, 4)
    keep = (row < 6) | (arrival[...] > 0.5)
    final[:, 128:160, :] = jnp.zeros((6, 32, LANES), jnp.float32)

    @pl.loop(1, 5)
    def _(z):
        def emit(f, j, value):
            done = 0.5 * (state[f, z, j] + q[f, z, j]) - (0.25 * step) * value
            final[f, pl.ds(4 * j + z - 1, 8, stride=16), :] = jnp.where(keep, done, 0.0)

        divergence(q, zf, z, 4, emit)

    copy = pltpu.make_async_copy(final.at[:, pl.ds(pl.multiple_of(flags[0] * 32, 32), 128), :], out, sem)
    copy.start()
    copy.wait()


def swap(x, partner):
    m, n = lax.axis_size("curve"), lax.axis_size("near")
    route = []
    for c in range(m):
        for i in range(n):
            to_c, to_i = partner(c, i)
            route.append((c * n + i, to_c * n + to_i))
    return lax.ppermute(x, ("curve", "near"), route)


def largest(x):
    m, n = lax.axis_size("curve"), lax.axis_size("near")
    x = jnp.maximum(x, swap(x, lambda c, i: (c, i ^ 1)))
    x = jnp.maximum(x, swap(x, lambda c, i: (c, ((i + 1) ^ 1) - 1 if 0 < i < n - 1 else n - 1 - i)))
    reach = 4
    while reach < n:
        x = jnp.maximum(x, swap(x, lambda c, i, d=reach: (c, (i + d) % n)))
        reach *= 2
    reach = 1
    while reach < m:
        if m % (2 * reach) == 0:
            x = jnp.maximum(x, swap(x, lambda c, i, d=reach: (c ^ d, i ^ 1)))
        else:
            x = jnp.maximum(x, swap(x, lambda c, i, d=reach: ((c + d) % m, i ^ 1)))
        reach *= 2
    return x


def rows_view(x):
    lead, cells = x.shape[:-2], x.shape[-1]
    x = x.reshape(lead + (4, cells // LANES, LANES))
    return jnp.swapaxes(x, -3, -2).reshape(lead + (4 * (cells // LANES), LANES))


def local(primitive, conductivity, new_owner):
    segment = lax.axis_index("curve")
    m = lax.axis_size("curve")
    rows = primitive.shape[2] // LANES * 4
    half = rows // 2
    prim, kappa = rows_view(primitive), rows_view(conductivity)
    flags = (new_owner[0:1] != segment).astype(jnp.int32)

    to_before, to_after, msg_a, msg_b, peak = pl.pallas_call(
        pack_kernel,
        out_shape=(f32(7, 40, LANES), f32(7, 4, LANES), f32(7, half, LANES), f32(7, half, LANES), f32(2, LANES)),
        in_specs=[VMEM, VMEM, SMEM],
        out_specs=(VMEM,) * 5,
        compiler_params=PARAMS,
        name="pack",
    )(prim, kappa, flags)

    right = lax.ppermute(to_before, "curve", [(c, (c - 1) % m) for c in range(m)])
    left = lax.ppermute(to_after, "curve", [(c, (c + 1) % m) for c in range(m)])
    n = lax.axis_size("near")
    with_a = lambda c, i: (c, i ^ 1)
    with_b = lambda c, i: (c, ((i + 1) ^ 1) - 1 if 0 < i < n - 1 else n - 1 - i)
    rec_a, rec_b = swap(msg_a, with_a), swap(msg_b, with_b)
    cor_a, cor_b = pl.pallas_call(
        corner_kernel,
        out_shape=(f32(7, 32, LANES), f32(7, 32, LANES)),
        in_specs=[VMEM, VMEM],
        out_specs=(VMEM, VMEM),
        compiler_params=PARAMS,
        name="corners",
    )(right, left)
    cor_a, cor_b = swap(cor_a, with_a), swap(cor_b, with_b)
    peak = largest(peak)

    state, total, conduct, arrival = pl.pallas_call(
        first_kernel,
        out_shape=(f32(6, 6, 5, 8, LANES), f32(6, 6, 5, 8, LANES), f32(6, 5, 8, LANES), f32(8, LANES)),
        in_specs=[VMEM] * 8,
        out_specs=(VMEM,) * 4,
        scratch_shapes=[
            pltpu.VMEM((7, 8, 40, LANES), jnp.float32),
            pltpu.VMEM((NQ, 8, 5, 8, LANES), jnp.float32),
            pltpu.VMEM((6, 5, 8, LANES), jnp.float32),
        ],
        compiler_params=PARAMS,
        name="first_section",
    )(prim, kappa, right, left, rec_a, rec_b, cor_a, cor_b)

    out = pl.pallas_call(
        second_kernel,
        out_shape=f32(6, rows + 32, LANES),
        in_specs=[VMEM] * 5 + [SMEM],
        out_specs=pl.BlockSpec(memory_space=pl.ANY),
        scratch_shapes=[
            pltpu.VMEM((NQ, 6, 5, 8, LANES), jnp.float32),
            pltpu.VMEM((6, 5, 8, LANES), jnp.float32),
            pltpu.VMEM((6, rows + 64, LANES), jnp.float32),
            pltpu.SemaphoreType.DMA,
        ],
        compiler_params=PARAMS,
        name="second_section",
    )(state, total, conduct, arrival, peak, flags)
    out = jnp.swapaxes(out.reshape(6, (rows + 32) // 4, 4, LANES), 1, 2)
    return out.reshape(1, 6, 4, (rows + 32) // 4 * LANES)


def solution(mesh):
    in_specs = (P(None, "near", "curve"), P("near", "curve"), P("curve"))
    out_specs = P("curve", None, "near", None)
    return jax.shard_map(local, mesh=mesh, in_specs=in_specs, out_specs=out_specs, check_vma=False)
```

time: 96.3 us -> 52.7 us (0.55)
  blocking collectives: 42.8 us -> 0 us
  Pallas kernels: 0 us -> 20.9 us
  other arithmetic: 11.5 us -> 0.02 us
  waiting for transfers between devices: 10.3 us -> 19.3 us
  local copies, waits for them, and re-layouts: 11.3 us -> 2.41 us
  starting transfers between devices: 17.4 us -> 9.74 us
  between operations: 2.63 us -> 0.12 us
    pmax x1 -> x0, blocking collectives: 42.8 us -> none  [local(): top_speed, top_kappa = lax.pmax((top_speed, top_kappa), ('curve', 'near'))]
    pallas_call x0 -> x4, Pallas kernels: none -> 20.9 us  [the longest x1 12.6 us: local(): pl.pallas_call(first_kernel, out_shape=(f32(6, 6, 5, 8, LANES), f32(6, 6,...]
    ppermute x10 -> x11, waiting for transfers between devices: 10.3 us -> 19.3 us  [the longest x9 12.9 us: swap(): return lax.ppermute(x, ('curve', 'near'), route)]
    ppermute x10 -> x11, starting transfers between devices: 17.4 us -> 9.74 us  [the longest x1 6.06 us: local(): lax.ppermute(to_before, 'curve', [(c, (c - 1) % m) for c in range(m)])]
    slice x59 -> x0, local copies, waits for them, and re-layouts: 6.16 us -> none  [the longest x20 2.14 us: roll_upper(): jnp.roll(values, ghost_layer_depth - 1, axis=-1)]
    sub x6 -> x0, other arithmetic: 3.54 us -> none  [face_flux(): 0.5 * (lower_f + upper_f)]
    dynamic_update_slice x2 -> x0, local copies, waits for them, and re-layouts: 2.33 us -> none  [section_rate(): lax.dynamic_update_slice_in_dim(broad, after_col, ghost_layer_depth + box...]
    scatter-add x12 -> x0, other arithmetic: 1.39 us -> none  [the longest x6 1.06 us: face_flux(): return flux.at[4].add(-heat)]
  transfers between devices with their start and end apart: 10 -> 11, of which waited for: 3 -> 6; matrix products, arithmetic and copies ran while one was open for 3% -> 0% of each run, Pallas kernels for 0% -> 0%
where the time goes in v1:
time: 52.7 us; the launch traced here: 52.5 us
  Pallas kernels  20.9 us (40%)
  waiting for transfers between devices  19.3 us (37%)
  starting transfers between devices  9.74 us (18%)
  local copies, waits for them, and re-layouts  2.41 us (5%)
    ppermute x9, waiting for transfers between devices, swap(): return lax.ppermute(x, ('curve', 'near'), route)  12.9 us
    pallas_call x1, Pallas kernels, local(): pl.pallas_call(first_kernel, out_shape=(f32(6, 6, 5, 8, LANES), f32(6, 6,...  12.6 us
    pallas_call x1, Pallas kernels, local(): pl.pallas_call(second_kernel, out_shape=f32(6, rows + 32, LANES), in_spec...  8.17 us
    ppermute x1, waiting for transfers between devices, local(): left = lax.ppermute(to_after, 'curve', [(c, (c + 1) % m) for c in range(m)])  6.41 us
    ppermute x1, starting transfers between devices, local(): lax.ppermute(to_before, 'curve', [(c, (c - 1) % m) for c in range(m)])  6.06 us
    ppermute x9, starting transfers between devices, swap(): return lax.ppermute(x, ('curve', 'near'), route)  3.69 us
    unnamed x10, local copies, waits for them, and re-layouts  2.41 us
  transfers between devices with their start and end apart: 11, of which 6 were waited for; matrix products, arithmetic and copies ran while one was open for 0% of the time, Pallas kernels for 0%

profile of v1, /device:TPU:0, one launch (start us, length us, event | category | flops | bytes accessed | tf_op | source)
XLA Modules:
  0.0 52.5 jit_solution(15189175721373402312)
XLA Ops:
  0.0 0.7 %copy-done.4 = s32[3]{0:T(128)S(1)} copy-done((s32[3]{0:T(128)S(1)}, s32[3]{0:T(128)}, u32[]{:S(2)}) %copy-start.4) | copy-done | bytes 36
  0.7 1.0 %copy-done = f32[6,4,3072]{2,1,0:T(4,128)S(1)} copy-done((f32[6,4,3072]{2,1,0:T(4,128)S(1)}, f32[6,4,3072]{2,1,0:T(4,128)}, u32[]{:S(2)}) %copy-start) | copy-done | bytes 294936
  1.7 0.8 %copy-done.2 = f32[4,3072]{1,0:T(4,128)S(1)} copy-done((f32[4,3072]{1,0:T(4,128)S(1)}, f32[4,3072]{1,0:T(4,128)}, u32[]{:S(2)}) %copy-start.2) | copy-done | bytes 49176
  2.5 0.1 pack.1
  2.5 6.1 %collective-permute-start = (f32[7,40,128]{2,1,0:T(8,128)S(1)}, f32[7,40,128]{2,1,0:T(8,128)S(1)}, u32[]{:S(2)}, u32[]{:S(2)}) collective-permute-start(f32[7,40,128]{2,1,0:T(8,128)S(1)} %get-tuple-element.16), channel_id=1, source_target_pairs={{0,28},{4,0},{8,4},{12,8},{16,12},{20,16},{24,20},{28,24},{1,29},{... | collective-permute-start | bytes 430088 | tf_op jit(solution)/shard_map/ppermute | solution.py:332
  8.6 0.0 collective-permute-start.2
  8.6 1.6 %collective-permute-start.3 = (f32[7,48,128]{2,1,0:T(8,128)S(1)}, f32[7,48,128]{2,1,0:T(8,128)S(1)}, u32[]{:S(2)}, u32[]{:S(2)}) collective-permute-start(f32[7,48,128]{2,1,0:T(8,128)S(1)} %get-tuple-element.19), channel_id=1, source_target_pairs={{0,3},{1,2},{2,1},{3,0},{4,7},{5,6},{6,5},{7,4},{8,11},{9,10},{10,... | collective-permute-start | bytes 516104 | tf_op jit(solution)/shard_map/ppermute | solution.py:288
  10.2 0.0 collective-permute-start.1
  10.2 6.4 %collective-permute-done.1.left = f32[7,4,128]{2,1,0:T(4,128)S(1)} collective-permute-done((f32[7,4,128]{2,1,0:T(4,128)S(1)}, f32[7,4,128]{2,1,0:T(4,128)S(1)}, u32[]{:S(2)}, u32[]{:S(2)}) %collective-permute-start.1) | collective-permute-done | bytes 14368 | tf_op jit(solution)/shard_map/ppermute | solution.py:333
  16.6 0.0 collective-permute-done.right
  16.7 0.1 collective-permute-start.4
  16.7 0.7 %collective-permute-start.5 = (f32[7,32,128]{2,1,0:T(8,128)S(1)}, f32[7,32,128]{2,1,0:T(8,128)S(1)}, u32[]{:S(2)}, u32[]{:S(2)}) collective-permute-start(f32[7,32,128]{2,1,0:T(8,128)S(1)} %get-tuple-element.21), channel_id=1, source_target_pairs={{0,3},{1,2},{2,1},{3,0},{4,7},{5,6},{6,5},{7,4},{8,11},{9,10},{10,... | collective-permute-start | bytes 344072 | tf_op jit(solution)/shard_map/ppermute | solution.py:288
  17.4 0.1 collective-permute-start.6
  17.5 1.1 %collective-permute-done.6 = f32[2,128]{1,0:T(2,128)S(1)} collective-permute-done((f32[2,128]{1,0:T(2,128)S(1)}, f32[2,128]{1,0:T(2,128)S(1)}, u32[]{:S(2)}, u32[]{:S(2)}) %collective-permute-start.6) | collective-permute-done | bytes 1056 | tf_op jit(solution)/shard_map/ppermute | solution.py:288
  18.5 1.3 %collective-permute-start.7 = (f32[2,128]{1,0:T(2,128)S(1)}, f32[2,128]{1,0:T(2,128)S(1)}, u32[]{:S(2)}, u32[]{:S(2)}) collective-permute-start(f32[2,128]{1,0:T(2,128)S(1)} %max.15), channel_id=1, source_target_pairs={{0,3},{1,2},{2,1},{3,0},{4,7},{5,6},{6,5},{7,4},{8,11},{9,10},{10,... | collective-permute-start | bytes 3080 | tf_op jit(solution)/shard_map/ppermute | solution.py:288
  19.8 1.9 %collective-permute-done.7 = f32[2,128]{1,0:T(2,128)S(1)} collective-permute-done((f32[2,128]{1,0:T(2,128)S(1)}, f32[2,128]{1,0:T(2,128)S(1)}, u32[]{:S(2)}, u32[]{:S(2)}) %collective-permute-start.7) | collective-permute-done | bytes 1056 | tf_op jit(solution)/shard_map/ppermute | solution.py:288
  21.7 3.0 %collective-permute-done.8 = f32[2,128]{1,0:T(2,128)S(1)} collective-permute-done((f32[2,128]{1,0:T(2,128)S(1)}, f32[2,128]{1,0:T(2,128)S(1)}, u32[]{:S(2)}, u32[]{:S(2)}) %collective-permute-start.8) | collective-permute-done | bytes 1056 | tf_op jit(solution)/shard_map/ppermute | solution.py:288
  24.8 3.0 %collective-permute-done.9 = f32[2,128]{1,0:T(2,128)S(1)} collective-permute-done((f32[2,128]{1,0:T(2,128)S(1)}, f32[2,128]{1,0:T(2,128)S(1)}, u32[]{:S(2)}, u32[]{:S(2)}) %collective-permute-start.9) | collective-permute-done | bytes 1056 | tf_op jit(solution)/shard_map/ppermute | solution.py:288
  27.8 0.0 collective-permute-start.10
  27.8 3.9 %collective-permute-done.10 = f32[2,128]{1,0:T(2,128)S(1)} collective-permute-done((f32[2,128]{1,0:T(2,128)S(1)}, f32[2,128]{1,0:T(2,128)S(1)}, u32[]{:S(2)}, u32[]{:S(2)}) %collective-permute-start.10) | collective-permute-done | bytes 1056 | tf_op jit(solution)/shard_map/ppermute | solution.py:288
  31.7 0.0 collective-permute-done.2.rec_a
  31.7 0.0 collective-permute-done.3.rec_b
  31.7 12.6 %first_section.1 = (f32[6,6,5,8,128]{4,3,2,1,0:T(8,128)S(1)}, f32[6,6,5,8,128]{4,3,2,1,0:T(8,128)S(1)}, f32[6,5,8,128]{3,2,1,0:T(8,128)S(1)}, f32[8,128]{1,0:T(8,128)S(1)}) custom-call(f32[6,96,128]{2,1,0:T(8,128)S(1)} %bitcast.18, f32[96,128]{1,0:T(8,128)S(1)} %bitcast.20, f32[7,40,128]{2,1,0:T(8,128)S(1)} %collective-permute-done.right, ...), custom_call_target="tpu_custom_call" | custom-call | tf_op jit(solution)/shard_map/first_section/pallas_call | solution.py:349
  44.3 8.2 %second_section.1 = f32[6,128,128]{2,1,0:T(8,128)} custom-call(f32[6,6,5,8,128]{4,3,2,1,0:T(8,128)S(1)} %get-tuple-element.22.state, f32[6,6,5,8,128]{4,3,2,1,0:T(8,128)S(1)} %get-tuple-element.23.total, f32[6,5,8,128]{3,2,1,0:T(8,128)S(1)} %get-tuple-element.24.conduct, f32[8,128]{1,0:T(8,128)S(1)} %get-tuple-element.25.arrival, f32[2,128]{1,0:T(2,128)S(1)} %max.19.peak, ...), custom_call_target="tpu_custom_call" | custom-call | tf_op jit(solution)/shard_map/second_section/pallas_call | solution.py:363
  (17 shorter events, 0.1 us)
Async XLA Ops:
  0.0 0.7 %copy-start.4 = (s32[3]{0:T(128)S(1)}, s32[3]{0:T(128)}, u32[]{:S(2)}) copy-start(s32[3]{0:T(128)} %param.5) | copy-start | bytes 40
  0.7 1.0 %copy-start = (f32[6,4,3072]{2,1,0:T(4,128)S(1)}, f32[6,4,3072]{2,1,0:T(4,128)}, u32[]{:S(2)}) copy-start(f32[6,4,3072]{2,1,0:T(4,128)} %param.3) | copy-start | bytes 884740
  1.7 0.8 %copy-start.2 = (f32[4,3072]{1,0:T(4,128)S(1)}, f32[4,3072]{1,0:T(4,128)}, u32[]{:S(2)}) copy-start(f32[4,3072]{1,0:T(4,128)} %param.4) | copy-start | bytes 147460
  2.5 29.3 %copy-start.1 = (f32[6,4,3072]{2,1,0:T(4,128)S(1)}, f32[6,4,3072]{2,1,0:T(4,128)}, u32[]{:S(2)}) copy-start(f32[6,4,3072]{2,1,0:T(4,128)} %param.3) | copy-start | bytes 884740
  2.5 14.1 %collective-permute-start = (f32[7,40,128]{2,1,0:T(8,128)S(1)}, f32[7,40,128]{2,1,0:T(8,128)S(1)}, u32[]{:S(2)}, u32[]{:S(2)}) collective-permute-start(f32[7,40,128]{2,1,0:T(8,128)S(1)} %get-tuple-element.16), channel_id=1, source_target_pairs={{0,28},{4,0},{8,4},{12,8},{16,12},{20,16},{24,20},{28,24},{1,29},{... | collective-permute-start | bytes 430088 | tf_op jit(solution)/shard_map/ppermute | solution.py:332
  8.6 23.1 %collective-permute-start.2 = (f32[7,48,128]{2,1,0:T(8,128)S(1)}, f32[7,48,128]{2,1,0:T(8,128)S(1)}, u32[]{:S(2)}, u32[]{:S(2)}) collective-permute-start(f32[7,48,128]{2,1,0:T(8,128)S(1)} %get-tuple-element.18), channel_id=1, source_target_pairs={{0,1},{1,0},{2,3},{3,2},{4,5},{5,4},{6,7},{7,6},{8,9},{9,8},{10,11... | collective-permute-start | bytes 516104 | tf_op jit(solution)/shard_map/ppermute | solution.py:288
  8.6 23.1 %collective-permute-start.3 = (f32[7,48,128]{2,1,0:T(8,128)S(1)}, f32[7,48,128]{2,1,0:T(8,128)S(1)}, u32[]{:S(2)}, u32[]{:S(2)}) collective-permute-start(f32[7,48,128]{2,1,0:T(8,128)S(1)} %get-tuple-element.19), channel_id=1, source_target_pairs={{0,3},{1,2},{2,1},{3,0},{4,7},{5,6},{6,5},{7,4},{8,11},{9,10},{10,... | collective-permute-start | bytes 516104 | tf_op jit(solution)/shard_map/ppermute | solution.py:288
  10.2 6.4 %collective-permute-start.1 = (f32[7,4,128]{2,1,0:T(4,128)S(1)}, f32[7,4,128]{2,1,0:T(4,128)S(1)}, u32[]{:S(2)}, u32[]{:S(2)}) collective-permute-start(f32[7,4,128]{2,1,0:T(4,128)S(1)} %get-tuple-element.17), channel_id=1, source_target_pairs={{0,4},{4,8},{8,12},{12,16},{16,20},{20,24},{24,28},{28,0},{1,5},{5... | collective-permute-start | bytes 43016 | tf_op jit(solution)/shard_map/ppermute | solution.py:333
  16.6 15.1 %copy-start.3 = (f32[4,3072]{1,0:T(4,128)S(1)}, f32[4,3072]{1,0:T(4,128)}, u32[]{:S(2)}) copy-start(f32[4,3072]{1,0:T(4,128)} %param.4) | copy-start | bytes 147460
  16.7 15.0 %collective-permute-start.4 = (f32[7,32,128]{2,1,0:T(8,128)S(1)}, f32[7,32,128]{2,1,0:T(8,128)S(1)}, u32[]{:S(2)}, u32[]{:S(2)}) collective-permute-start(f32[7,32,128]{2,1,0:T(8,128)S(1)} %get-tuple-element.20), channel_id=1, source_target_pairs={{0,1},{1,0},{2,3},{3,2},{4,5},{5,4},{6,7},{7,6},{8,9},{9,8},{10,11... | collective-permute-start | bytes 344072 | tf_op jit(solution)/shard_map/ppermute | solution.py:288
  16.7 15.0 %collective-permute-start.5 = (f32[7,32,128]{2,1,0:T(8,128)S(1)}, f32[7,32,128]{2,1,0:T(8,128)S(1)}, u32[]{:S(2)}, u32[]{:S(2)}) collective-permute-start(f32[7,32,128]{2,1,0:T(8,128)S(1)} %get-tuple-element.21), channel_id=1, source_target_pairs={{0,3},{1,2},{2,1},{3,0},{4,7},{5,6},{6,5},{7,4},{8,11},{9,10},{10,... | collective-permute-start | bytes 344072 | tf_op jit(solution)/shard_map/ppermute | solution.py:288
  17.4 1.1 %collective-permute-start.6 = (f32[2,128]{1,0:T(2,128)S(1)}, f32[2,128]{1,0:T(2,128)S(1)}, u32[]{:S(2)}, u32[]{:S(2)}) collective-permute-start(f32[2,128]{1,0:T(2,128)S(1)} %get-tuple-element.26), channel_id=1, source_target_pairs={{0,1},{1,0},{2,3},{3,2},{4,5},{5,4},{6,7},{7,6},{8,9},{9,8},{10,11... | collective-permute-start | bytes 3080 | tf_op jit(solution)/shard_map/ppermute | solution.py:288
  18.5 3.2 %collective-permute-start.7 = (f32[2,128]{1,0:T(2,128)S(1)}, f32[2,128]{1,0:T(2,128)S(1)}, u32[]{:S(2)}, u32[]{:S(2)}) collective-permute-start(f32[2,128]{1,0:T(2,128)S(1)} %max.15), channel_id=1, source_target_pairs={{0,3},{1,2},{2,1},{3,0},{4,7},{5,6},{6,5},{7,4},{8,11},{9,10},{10,... | collective-permute-start | bytes 3080 | tf_op jit(solution)/shard_map/ppermute | solution.py:288
  21.7 3.0 %collective-permute-start.8 = (f32[2,128]{1,0:T(2,128)S(1)}, f32[2,128]{1,0:T(2,128)S(1)}, u32[]{:S(2)}, u32[]{:S(2)}) collective-permute-start(f32[2,128]{1,0:T(2,128)S(1)} %max.16), channel_id=1, source_target_pairs={{0,5},{1,4},{2,7},{3,6},{4,1},{5,0},{6,3},{7,2},{8,13},{9,12},{10,... | collective-permute-start | bytes 3080 | tf_op jit(solution)/shard_map/ppermute | solution.py:288
  24.8 3.0 %collective-permute-start.9 = (f32[2,128]{1,0:T(2,128)S(1)}, f32[2,128]{1,0:T(2,128)S(1)}, u32[]{:S(2)}, u32[]{:S(2)}) collective-permute-start(f32[2,128]{1,0:T(2,128)S(1)} %max.17), channel_id=1, source_target_pairs={{0,9},{1,8},{2,11},{3,10},{4,13},{5,12},{6,15},{7,14},{8,1},{9,0},... | collective-permute-start | bytes 3080 | tf_op jit(solution)/shard_map/ppermute | solution.py:288
  27.8 3.9 %collective-permute-start.10 = (f32[2,128]{1,0:T(2,128)S(1)}, f32[2,128]{1,0:T(2,128)S(1)}, u32[]{:S(2)}, u32[]{:S(2)}) collective-permute-start(f32[2,128]{1,0:T(2,128)S(1)} %max.18), channel_id=1, source_target_pairs={{0,17},{1,16},{2,19},{3,18},{4,21},{5,20},{6,23},{7,22},{8,25},{9,... | collective-permute-start | bytes 3080 | tf_op jit(solution)/shard_map/ppermute | solution.py:288

commit v2 on v1

--- a/solution.py
+++ b/solution.py
@@ -72,11 +72,10 @@
                 msg[f, pl.ds(16 * z + 9, 1), :] = left[f, pl.ds(start + z, 1), :]
 
 
-def up_x(q, lane, ghost):
+def up_x(q, lane):
     w = [pltpu.roll(v, LANES - BW, 1) for v in q[:4]]
     w.append(pltpu.roll(w[0], 7, 0))
-    out = [jnp.where(lane < LANES - BW, w[j], w[j + 1]) for j in range(4)]
-    return out + ([pltpu.roll(q[4], LANES - BW, 1)] if ghost else [])
+    return [jnp.where(lane < LANES - BW, w[j], w[j + 1]) for j in range(4)] + [pltpu.roll(q[4], LANES - BW, 1)]
 
 
 def up_y(v, low):
@@ -85,15 +84,6 @@
 
 def down_y(v, low):
     return jnp.where(low == 0, pltpu.roll(v, LANES - BW + 1, 1), pltpu.roll(v, 1, 1))
-
-
-def flux(u, v, pressure, k, f):
-    if f == 0:
-        return u[1 + k]
-    if f == 4:
-        return (u[4] + pressure) * v[k]
-    out = u[f] * v[k]
-    return out + pressure if f == 1 + k else out
 
 
 def face(lower_u, upper_u, lower_f, upper_f, speed, heat):
@@ -101,76 +91,87 @@
     return out if heat is None else out - heat
 
 
-def z_sides(q, z, j):
-    lower, upper = ([q[i, zz, j] for i in range(NQ)] for zz in (z, z + 1))
-    speed = jnp.maximum(jnp.abs(lower[VX + 2]) + lower[SND], jnp.abs(upper[VX + 2]) + upper[SND])
-    heat = (lower[KAP] + upper[KAP]) * (upper[TMP] - lower[TMP])
-    return lower, upper, speed, heat
+def z_face_row(q, z, slots):
+    speed, heat = [], []
+    for j in range(slots):
+        s0 = jnp.abs(q[VX + 2, z, j]) + q[SND, z, j]
+        s1 = jnp.abs(q[VX + 2, z + 1, j]) + q[SND, z + 1, j]
+        speed.append(jnp.maximum(s0, s1))
+        heat.append((q[KAP, z, j] + q[KAP, z + 1, j]) * (q[TMP, z + 1, j] - q[TMP, z, j]))
+    return {
+        (f, j): face(
+            q[f, z, j],
+            q[f, z + 1, j],
+            physical(q, f, j, 2, z),
+            physical(q, f, j, 2, z + 1),
+            speed[j],
+            heat[j] if f == 4 else None,
+        )
+        for f in range(6)
+        for j in range(slots)
+    }
+
+
+def physical(q, f, j, k, z):
+    if f == 0:
+        return q[1 + k, z, j]
+    v = q[VX + k, z, j]
+    if f == 4:
+        return (q[4, z, j] + q[PR, z, j]) * v
+    out = q[f, z, j] * v
+    return out + q[PR, z, j] if f == 1 + k else out
 
 
 def z_faces(q, zf, z, slots):
-    for j in range(slots):
-        lower, upper, speed, heat = z_sides(q, z, j)
-        for f in range(6):
-            zf[f, j] = face(
-                lower[f],
-                upper[f],
-                flux(lower[:6], lower[6:9], lower[PR], 2, f),
-                flux(upper[:6], upper[6:9], upper[PR], 2, f),
-                speed,
-                heat if f == 4 else None,
-            )
+    for key, value in z_face_row(q, z, slots).items():
+        zf[key] = value
 
 
 def divergence(q, zf, z, slots, emit):
     shape = (8, LANES)
     lane, row = lanes_of(shape), rows_of(shape)
-    low = lane % BW
+    low = lane & (BW - 1)
     ghost = 4
     five = range(5)
     at = lambda i, j: q[i, z, j]
     sx = [jnp.abs(at(VX, j)) + at(SND, j) for j in five]
-    ax = [jnp.maximum(a, b) for a, b in zip(sx, up_x(sx, lane, True), strict=True)]
+    sy = [jnp.abs(at(VX + 1, j)) + at(SND, j) for j in range(slots)]
     kx, tx = [at(KAP, j) for j in five], [at(TMP, j) for j in five]
-    hx = [
-        (k + ku) * (tu - t)
-        for k, ku, t, tu in zip(kx, up_x(kx, lane, True), tx, up_x(tx, lane, True), strict=True)
-    ]
-    ay, hy, az, hz = [], [], [], []
-    for j in range(slots):
-        s = jnp.abs(at(VX + 1, j)) + at(SND, j)
-        ay.append(jnp.maximum(s, up_y(s, low)))
-        hy.append((kx[j] + up_y(kx[j], low)) * (up_y(tx[j], low) - tx[j]))
-        s0 = jnp.abs(at(VX + 2, j)) + at(SND, j)
-        s1 = jnp.abs(q[VX + 2, z + 1, j]) + q[SND, z + 1, j]
-        az.append(jnp.maximum(s0, s1))
-        hz.append((kx[j] + q[KAP, z + 1, j]) * (q[TMP, z + 1, j] - tx[j]))
-    for f in range(6):
-
-        def physical(j, k, zz):
-            u = {i: q[i, zz, j] for i in {f, 1 + k}}
-            return flux(u, {k: q[VX + k, zz, j]}, q[PR, zz, j], k, f)
-
+    sxu, kxu, txu = up_x(sx, lane), up_x(kx, lane), up_x(tx, lane)
+    syu, kyu, tyu = ([up_y(v, low) for v in vs[:slots]] for vs in (sy, kx, tx))
+    ax = [jnp.maximum(v, w) for v, w in zip(sx, sxu, strict=True)]
+    ay = [jnp.maximum(v, w) for v, w in zip(sy, syu, strict=True)]
+    hx = [(kx[j] + kxu[j]) * (txu[j] - tx[j]) for j in five]
+    hy = [(kx[j] + kyu[j]) * (tyu[j] - tx[j]) for j in range(slots)]
+
+    def neighbours(f):
+        u = [at(f, j) for j in five]
+        fx = [physical(q, f, j, 0, z) for j in five]
+        fy = [physical(q, f, j, 1, z) for j in range(slots)]
+        return u, fx, fy, up_x(u, lane), up_x(fx, lane), [up_y(v, low) for v in u[:slots]], [up_y(v, low) for v in fy]
+
+    def sides(f, u, fx, fy, ux, fux, uy, fuy):
         heat = lambda h: h if f == 4 else None
-        u = [at(f, j) for j in five]
-        fx = [physical(j, 0, z) for j in five]
-        uu, fu = up_x(u, lane, True), up_x(fx, lane, True)
-        gx = [face(u[j], uu[j], fx[j], fu[j], ax[j], heat(hx[j])) for j in five]
+        gx = [face(u[j], ux[j], fx[j], fux[j], ax[j], heat(hx[j])) for j in five]
         gx[3] = jnp.where((lane >= LANES - BW) & (row == 7), gx[ghost], gx[3])
         d = [pltpu.roll(g, BW, 1) for g in gx]
         before = jnp.where(row == 0, d[ghost], pltpu.roll(d[3], 1, 0))
         dx = [jnp.where(lane >= BW, d[j], before if j == 0 else d[j - 1]) for j in range(4)] + [d[ghost]]
-        for j in range(slots):
-            fy = physical(j, 1, z)
-            gy = face(u[j], up_y(u[j], low), fy, up_y(fy, low), ay[j], heat(hy[j]))
-            gz = face(u[j], q[f, z + 1, j], physical(j, 2, z), physical(j, 2, z + 1), az[j], heat(hz[j]))
-            total = (gx[j] - dx[j]) + (gy - down_y(gy, low)) + (gz - zf[f, j])
-            zf[f, j] = gz
-            emit(f, j, total)
+        gy = [face(u[j], uy[j], fy[j], fuy[j], ay[j], heat(hy[j])) for j in range(slots)]
+        dy = [down_y(g, low) for g in gy]
+        return [(gx[j] - dx[j]) + (gy[j] - dy[j]) for j in range(slots)]
+
+    near = [neighbours(f) for f in range(6)]
+    gz = z_face_row(q, z, slots)
+    part = [sides(f, *near[f]) for f in range(6)]
+    total = {key: part[key[0]][key[1]] + (value - zf[key]) for key, value in gz.items()}
+    emit(total)
+    for key, value in gz.items():
+        zf[key] = value
 
 
 def first_kernel(
-    prim, kappa, right, left, rec_a, rec_b, cor_a, cor_b, state, total, conduct, arrival, ext, q, zf
+    prim, kappa, right, left, rec_a, rec_b, cor_a, cor_b, q, total, arrival, ext, zf
 ):
     segment, segments = lax.axis_index("curve"), lax.axis_size("curve")
     even = lax.axis_index("near") % 2 == 0
@@ -183,56 +184,57 @@
 
     arrival[...] = jnp.where(last, 0.0, spread(right[0, 36:37, :]))
 
-    def fill(f, z, own, box, beyond, behind):
+    def filled(own, box, beyond, behind):
         edge = spread(own[-1][7:8])
         box = jnp.where(last, pltpu.roll(edge, BW, 1), box)
-        for g, rows in enumerate(own + [box]):
-            ext[f, z, 8 * g : 8 * g + 8, :] = rows
         start, end = spread(own[0][0:1]), spread(box[7:8])
         behind = jnp.where(first, pltpu.roll(start, LANES - BW, 1), spread(behind))
         low_side = jnp.where(lane < BW, start, behind)
         high_side = jnp.where(lane >= LANES - BW, end, spread(beyond))
-        ext[f, z, 32:40, :] = jnp.where(row == 7, high_side, low_side)
+        return own + [box, jnp.where(row == 7, high_side, low_side)]
 
     for f in range(7):
         ref, at = (prim, (f,)) if f < 6 else (kappa, ())
+        parts = []
         for z in range(4):
             own = [ref[at + (pl.ds(z + 32 * g, 8, stride=4), slice(None))] for g in range(blocks // 8)]
-            fill(
-                f, z + 2, own, right[f, pl.ds(z, 8, stride=4), :], right[f, 32 + z : 33 + z, :], left[f, z : z + 1, :]
-            )
+            rows = filled(own, right[f, pl.ds(z, 8, stride=4), :], right[f, 32 + z : 33 + z, :], left[f, z : z + 1, :])
+            parts.append((z + 2, rows))
         for rec, cor, base in ((rec_a, cor_a, base_a), (rec_b, cor_b, base_b)):
             for z in range(2):
                 own = [rec[f, z * blocks + 8 * g : z * blocks + 8 * g + 8, :] for g in range(blocks // 8)]
                 c = 16 * z
-                fill(
-                    f, base + z, own, cor[f, c : c + 8, :], cor[f, c + 8 : c + 9, :], cor[f, c + 9 : c + 10, :]
-                )
+                rows = filled(own, cor[f, c : c + 8, :], cor[f, c + 8 : c + 9, :], cor[f, c + 9 : c + 10, :])
+                parts.append((base + z, rows))
+        for z, rows in parts:
+            for g, value in enumerate(rows):
+                ext[f, z, 8 * g : 8 * g + 8, :] = value
 
     @pl.loop(0, 8)
     def _(z):
+        found = []
         for j in range(5):
             rows = pl.ds(j, 8, stride=4) if j < 4 else pl.ds(32, 8)
             r, vx, vy, vz, p, s, k = (ext[f, z, rows, :] for f in range(7))
             t = p / r
             u = (r, r * vx, r * vy, r * vz, p / (GAMMA - 1.0) + 0.5 * r * (vx * vx + vy * vy + vz * vz), r * s)
-            for i, value in enumerate(u + (vx, vy, vz, p, jnp.sqrt(GAMMA * t), t, k)):
+            found.append(u + (vx, vy, vz, p, jnp.sqrt(GAMMA * t), t, k))
+        for j, values in enumerate(found):
+            for i, value in enumerate(values):
                 q[i, z, j] = value
 
     z_faces(q, zf, 0, 5)
 
     @pl.loop(1, 7)
     def _(z):
-        def emit(f, j, value):
-            total[f, z - 1, j] = value
-            state[f, z - 1, j] = q[f, z, j]
+        def emit(values):
+            for (f, j), value in values.items():
+                total[f, z - 1, j] = value
 
         divergence(q, zf, z, 5, emit)
-        for j in range(5):
-            conduct[z - 1, j] = q[KAP, z, j]
-
-
-def second_kernel(state, total, conduct, arrival, peak, flags, out, q, zf, final, sem):
+
+
+def second_kernel(base, total, arrival, peak, flags, out, q, zf, final, sem):
     segment, segments = lax.axis_index("curve"), lax.axis_size("curve")
     shape = (8, LANES)
     lane, row = lanes_of(shape), rows_of(shape)
@@ -243,21 +245,23 @@
 
     @pl.loop(0, 6)
     def _(z):
-        half = [[state[f, z, j] - (0.5 * step) * total[f, z, j] for j in range(5)] for f in range(6)]
-        kap = [conduct[z, j] for j in range(5)]
+        half = [[base[f, z + 1, j] - (0.5 * step) * total[f, z, j] for j in range(5)] for f in range(6)]
+        kap = [base[KAP, z + 1, j] for j in range(5)]
         for u in half + [kap]:
             edge = pltpu.roll(pltpu.roll(u[3], BW, 1), 1, 0)
             u[0] = jnp.where(last & (row == 6) & (lane < BW), edge, u[0])
             g = jnp.where((row == 0) & (lane < BW), u[0], u[4])
             g = jnp.where((row == 7) & (lane >= LANES - BW), u[3], g)
             u[4] = jnp.where(first & (row == 0) & (lane >= BW), pltpu.roll(g, LANES - BW, 1), g)
+        found = []
         for j in range(5):
             r, mx, my, mz, e, s = (half[f][j] for f in range(6))
             inv = 1.0 / r
             vx, vy, vz = mx * inv, my * inv, mz * inv
             p = (GAMMA - 1.0) * (e - 0.5 * (mx * vx + my * vy + mz * vz))
             t = p * inv
-            values = (r, mx, my, mz, e, s, vx, vy, vz, p, jnp.sqrt(GAMMA * t), t, kap[j])
+            found.append((r, mx, my, mz, e, s, vx, vy, vz, p, jnp.sqrt(GAMMA * t), t, kap[j]))
+        for j, values in enumerate(found):
             for i, value in enumerate(values):
                 q[i, z, j] = value
 
@@ -267,9 +271,13 @@
 
     @pl.loop(1, 5)
     def _(z):
-        def emit(f, j, value):
-            done = 0.5 * (state[f, z, j] + q[f, z, j]) - (0.25 * step) * value
-            final[f, pl.ds(4 * j + z - 1, 8, stride=16), :] = jnp.where(keep, done, 0.0)
+        def emit(values):
+            done = {
+                (f, j): 0.5 * (base[f, z + 1, j] + q[f, z, j]) - (0.25 * step) * value
+                for (f, j), value in values.items()
+            }
+            for (f, j), value in done.items():
+                final[f, pl.ds(4 * j + z - 1, 8, stride=16), :] = jnp.where(keep, value, 0.0)
 
         divergence(q, zf, z, 4, emit)
 
@@ -346,14 +354,13 @@
     cor_a, cor_b = swap(cor_a, with_a), swap(cor_b, with_b)
     peak = largest(peak)
 
-    state, total, conduct, arrival = pl.pallas_call(
+    base, total, arrival = pl.pallas_call(
         first_kernel,
-        out_shape=(f32(6, 6, 5, 8, LANES), f32(6, 6, 5, 8, LANES), f32(6, 5, 8, LANES), f32(8, LANES)),
+        out_shape=(f32(NQ, 8, 5, 8, LANES), f32(6, 6, 5, 8, LANES), f32(8, LANES)),
         in_specs=[VMEM] * 8,
-        out_specs=(VMEM,) * 4,
+        out_specs=(VMEM,) * 3,
         scratch_shapes=[
             pltpu.VMEM((7, 8, 40, LANES), jnp.float32),
-            pltpu.VMEM((NQ, 8, 5, 8, LANES), jnp.float32),
             pltpu.VMEM((6, 5, 8, LANES), jnp.float32),
         ],
         compiler_params=PARAMS,
@@ -363,7 +370,7 @@
     out = pl.pallas_call(
         second_kernel,
         out_shape=f32(6, rows + 32, LANES),
-        in_specs=[VMEM] * 5 + [SMEM],
+        in_specs=[VMEM] * 4 + [SMEM],
         out_specs=pl.BlockSpec(memory_space=pl.ANY),
         scratch_shapes=[
             pltpu.VMEM((NQ, 6, 5, 8, LANES), jnp.float32),
@@ -373,7 +380,7 @@
         ],
         compiler_params=PARAMS,
         name="second_section",
-    )(state, total, conduct, arrival, peak, flags)
+    )(base, total, arrival, peak, flags)
     out = jnp.swapaxes(out.reshape(6, (rows + 32) // 4, 4, LANES), 1, 2)
     return out.reshape(1, 6, 4, (rows + 32) // 4 * LANES)
 

time: 52.7 us -> 40.2 us (0.76)
  Pallas kernels: 20.9 us -> 6.59 us
  local copies, waits for them, and re-layouts: 2.41 us -> 3.51 us
  between operations: 0.12 us -> 0.72 us
    pallas_call x1, Pallas kernels: 12.6 us -> 2.99 us  [local(): pl.pallas_call(first_kernel, out_shape=(f32(NQ, 8, 5, 8, LANES), f32(6, 6...]
    pallas_call x1, Pallas kernels: 8.17 us -> 3.5 us  [local(): pl.pallas_call(second_kernel, out_shape=f32(6, rows + 32, LANES), in_spec...]
    unnamed x10 -> x8, local copies, waits for them, and re-layouts: 2.41 us -> 3.51 us
where the time goes in v2:
time: 40.2 us; the launch traced here: 39.9 us
  waiting for transfers between devices  19.3 us (48%)
  starting transfers between devices  9.74 us (24%)
  Pallas kernels  6.59 us (16%)
  local copies, waits for them, and re-layouts  3.51 us (9%)
  between operations  0.72 us (2%)
    ppermute x9, waiting for transfers between devices, swap(): return lax.ppermute(x, ('curve', 'near'), route)  12.9 us
    ppermute x1, waiting for transfers between devices, local(): left = lax.ppermute(to_after, 'curve', [(c, (c + 1) % m) for c in range(m)])  6.41 us
    ppermute x1, starting transfers between devices, local(): lax.ppermute(to_before, 'curve', [(c, (c - 1) % m) for c in range(m)])  6.06 us
    ppermute x9, starting transfers between devices, swap(): return lax.ppermute(x, ('curve', 'near'), route)  3.69 us
    unnamed x8, local copies, waits for them, and re-layouts  3.51 us
    pallas_call x1, Pallas kernels, local(): pl.pallas_call(second_kernel, out_shape=f32(6, rows + 32, LANES), in_spec...  3.5 us
    pallas_call x1, Pallas kernels, local(): pl.pallas_call(first_kernel, out_shape=(f32(NQ, 8, 5, 8, LANES), f32(6, 6...  2.99 us
  transfers between devices with their start and end apart: 11, of which 6 were waited for; matrix products, arithmetic and copies ran while one was open for 0% of the time, Pallas kernels for 0%

profile of v2, /device:TPU:0, one launch (start us, length us, event | category | flops | bytes accessed | tf_op | source)
XLA Modules:
  0.0 39.9 jit_solution(9387672218924657255)
XLA Ops:
  0.7 0.0 copy-start
  0.7 1.0 %copy-done = f32[6,4,3072]{2,1,0:T(4,128)S(1)} copy-done((f32[6,4,3072]{2,1,0:T(4,128)S(1)}, f32[6,4,3072]{2,1,0:T(4,128)}, u32[]{:S(2)}) %copy-start) | copy-done | bytes 294936
  1.6 0.8 %copy-done.2 = f32[4,3072]{1,0:T(4,128)S(1)} copy-done((f32[4,3072]{1,0:T(4,128)S(1)}, f32[4,3072]{1,0:T(4,128)}, u32[]{:S(2)}) %copy-start.2) | copy-done | bytes 49176
  2.4 0.1 pack.1
  2.5 6.1 %collective-permute-start = (f32[7,40,128]{2,1,0:T(8,128)S(1)}, f32[7,40,128]{2,1,0:T(8,128)S(1)}, u32[]{:S(2)}, u32[]{:S(2)}) collective-permute-start(f32[7,40,128]{2,1,0:T(8,128)S(1)} %get-tuple-element.15), channel_id=1, source_target_pairs={{0,28},{4,0},{8,4},{12,8},{16,12},{20,16},{24,20},{28,24},{1,29},{... | collective-permute-start | bytes 430088 | tf_op jit(solution)/shard_map/ppermute | solution.py:340
  8.5 0.0 collective-permute-start.2
  8.6 1.6 %collective-permute-start.3 = (f32[7,48,128]{2,1,0:T(8,128)S(1)}, f32[7,48,128]{2,1,0:T(8,128)S(1)}, u32[]{:S(2)}, u32[]{:S(2)}) collective-permute-start(f32[7,48,128]{2,1,0:T(8,128)S(1)} %get-tuple-element.18), channel_id=1, source_target_pairs={{0,3},{1,2},{2,1},{3,0},{4,7},{5,6},{6,5},{7,4},{8,11},{9,10},{10,... | collective-permute-start | bytes 516104 | tf_op jit(solution)/shard_map/ppermute | solution.py:296
  10.2 6.4 %collective-permute-done.1.left = f32[7,4,128]{2,1,0:T(4,128)S(1)} collective-permute-done((f32[7,4,128]{2,1,0:T(4,128)S(1)}, f32[7,4,128]{2,1,0:T(4,128)S(1)}, u32[]{:S(2)}, u32[]{:S(2)}) %collective-permute-start.1) | collective-permute-done | bytes 14368 | tf_op jit(solution)/shard_map/ppermute | solution.py:341
  16.6 0.0 collective-permute-done.right
  16.6 0.1 collective-permute-start.4
  16.7 0.7 %collective-permute-start.5 = (f32[7,32,128]{2,1,0:T(8,128)S(1)}, f32[7,32,128]{2,1,0:T(8,128)S(1)}, u32[]{:S(2)}, u32[]{:S(2)}) collective-permute-start(f32[7,32,128]{2,1,0:T(8,128)S(1)} %get-tuple-element.20), channel_id=1, source_target_pairs={{0,3},{1,2},{2,1},{3,0},{4,7},{5,6},{6,5},{7,4},{8,11},{9,10},{10,... | collective-permute-start | bytes 344072 | tf_op jit(solution)/shard_map/ppermute | solution.py:296
  17.3 0.1 collective-permute-start.6
  17.4 1.1 %collective-permute-done.6 = f32[2,128]{1,0:T(2,128)S(1)} collective-permute-done((f32[2,128]{1,0:T(2,128)S(1)}, f32[2,128]{1,0:T(2,128)S(1)}, u32[]{:S(2)}, u32[]{:S(2)}) %collective-permute-start.6) | collective-permute-done | bytes 1056 | tf_op jit(solution)/shard_map/ppermute | solution.py:296
  18.5 1.3 %collective-permute-start.7 = (f32[2,128]{1,0:T(2,128)S(1)}, f32[2,128]{1,0:T(2,128)S(1)}, u32[]{:S(2)}, u32[]{:S(2)}) collective-permute-start(f32[2,128]{1,0:T(2,128)S(1)} %max.15), channel_id=1, source_target_pairs={{0,3},{1,2},{2,1},{3,0},{4,7},{5,6},{6,5},{7,4},{8,11},{9,10},{10,... | collective-permute-start | bytes 3080 | tf_op jit(solution)/shard_map/ppermute | solution.py:296
  19.8 1.9 %collective-permute-done.7 = f32[2,128]{1,0:T(2,128)S(1)} collective-permute-done((f32[2,128]{1,0:T(2,128)S(1)}, f32[2,128]{1,0:T(2,128)S(1)}, u32[]{:S(2)}, u32[]{:S(2)}) %collective-permute-start.7) | collective-permute-done | bytes 1056 | tf_op jit(solution)/shard_map/ppermute | solution.py:296
  21.7 0.0 collective-permute-start.8
  21.7 3.0 %collective-permute-done.8 = f32[2,128]{1,0:T(2,128)S(1)} collective-permute-done((f32[2,128]{1,0:T(2,128)S(1)}, f32[2,128]{1,0:T(2,128)S(1)}, u32[]{:S(2)}, u32[]{:S(2)}) %collective-permute-start.8) | collective-permute-done | bytes 1056 | tf_op jit(solution)/shard_map/ppermute | solution.py:296
  24.7 3.0 %collective-permute-done.9 = f32[2,128]{1,0:T(2,128)S(1)} collective-permute-done((f32[2,128]{1,0:T(2,128)S(1)}, f32[2,128]{1,0:T(2,128)S(1)}, u32[]{:S(2)}, u32[]{:S(2)}) %collective-permute-start.9) | collective-permute-done | bytes 1056 | tf_op jit(solution)/shard_map/ppermute | solution.py:296
  27.7 3.9 %collective-permute-done.10 = f32[2,128]{1,0:T(2,128)S(1)} collective-permute-done((f32[2,128]{1,0:T(2,128)S(1)}, f32[2,128]{1,0:T(2,128)S(1)}, u32[]{:S(2)}, u32[]{:S(2)}) %collective-permute-start.10) | collective-permute-done | bytes 1056 | tf_op jit(solution)/shard_map/ppermute | solution.py:296
  31.7 0.0 copy-start.1
  31.7 1.0 %copy-done.1 = f32[6,4,3072]{2,1,0:T(4,128)S(1)} copy-done((f32[6,4,3072]{2,1,0:T(4,128)S(1)}, f32[6,4,3072]{2,1,0:T(4,128)}, u32[]{:S(2)}) %copy-start.1) | copy-done | bytes 294936
  32.6 0.8 %copy-done.3 = f32[4,3072]{1,0:T(4,128)S(1)} copy-done((f32[4,3072]{1,0:T(4,128)S(1)}, f32[4,3072]{1,0:T(4,128)}, u32[]{:S(2)}) %copy-start.3) | copy-done | bytes 49176
  33.4 3.0 %first_section.1 = (f32[13,8,5,8,128]{4,3,2,1,0:T(8,128)S(1)}, f32[6,6,5,8,128]{4,3,2,1,0:T(8,128)S(1)}, f32[8,128]{1,0:T(8,128)S(1)}) custom-call(f32[6,96,128]{2,1,0:T(8,128)S(1)} %bitcast.18, f32[96,128]{1,0:T(8,128)S(1)} %bitcast.20, f32[7,40,128]{2,1,0:T(8,128)S(1)} %collective-permute-done.right, f32[7,4,128]{2,1,0:T(4,128)S(1)} %collective-permute-done.1.left, ...), custom_call_target="tpu_custom_call" | custom-call | tf_op jit(solution)/shard_map/first_section/pallas_call | solution.py:357
  36.4 3.5 %second_section.1 = f32[6,128,128]{2,1,0:T(8,128)} custom-call(f32[13,8,5,8,128]{4,3,2,1,0:T(8,128)S(1)} %get-tuple-element.21.base, f32[6,6,5,8,128]{4,3,2,1,0:T(8,128)S(1)} %get-tuple-element.22.total, f32[8,128]{1,0:T(8,128)S(1)} %get-tuple-element.23.arrival, f32[2,128]{1,0:T(2,128)S(1)} %max.19.peak, s32[1]{0:T(128)S(6)} %convert_element_type.3.flags), custom_call_target="tpu_custom_call" | custom-call | tf_op jit(solution)/shard_map/second_section/pallas_call | solution.py:370
  (15 shorter events, 0.1 us)
Async XLA Ops:
  0.7 1.0 %copy-start = (f32[6,4,3072]{2,1,0:T(4,128)S(1)}, f32[6,4,3072]{2,1,0:T(4,128)}, u32[]{:S(2)}) copy-start(f32[6,4,3072]{2,1,0:T(4,128)} %param.3) | copy-start | bytes 884740
  1.6 0.8 %copy-start.2 = (f32[4,3072]{1,0:T(4,128)S(1)}, f32[4,3072]{1,0:T(4,128)}, u32[]{:S(2)}) copy-start(f32[4,3072]{1,0:T(4,128)} %param.4) | copy-start | bytes 147460
  2.5 14.1 %collective-permute-start = (f32[7,40,128]{2,1,0:T(8,128)S(1)}, f32[7,40,128]{2,1,0:T(8,128)S(1)}, u32[]{:S(2)}, u32[]{:S(2)}) collective-permute-start(f32[7,40,128]{2,1,0:T(8,128)S(1)} %get-tuple-element.15), channel_id=1, source_target_pairs={{0,28},{4,0},{8,4},{12,8},{16,12},{20,16},{24,20},{28,24},{1,29},{... | collective-permute-start | bytes 430088 | tf_op jit(solution)/shard_map/ppermute | solution.py:340
  8.5 23.1 %collective-permute-start.2 = (f32[7,48,128]{2,1,0:T(8,128)S(1)}, f32[7,48,128]{2,1,0:T(8,128)S(1)}, u32[]{:S(2)}, u32[]{:S(2)}) collective-permute-start(f32[7,48,128]{2,1,0:T(8,128)S(1)} %get-tuple-element.17), channel_id=1, source_target_pairs={{0,1},{1,0},{2,3},{3,2},{4,5},{5,4},{6,7},{7,6},{8,9},{9,8},{10,11... | collective-permute-start | bytes 516104 | tf_op jit(solution)/shard_map/ppermute | solution.py:296
  8.6 23.1 %collective-permute-start.3 = (f32[7,48,128]{2,1,0:T(8,128)S(1)}, f32[7,48,128]{2,1,0:T(8,128)S(1)}, u32[]{:S(2)}, u32[]{:S(2)}) collective-permute-start(f32[7,48,128]{2,1,0:T(8,128)S(1)} %get-tuple-element.18), channel_id=1, source_target_pairs={{0,3},{1,2},{2,1},{3,0},{4,7},{5,6},{6,5},{7,4},{8,11},{9,10},{10,... | collective-permute-start | bytes 516104 | tf_op jit(solution)/shard_map/ppermute | solution.py:296
  10.2 6.4 %collective-permute-start.1 = (f32[7,4,128]{2,1,0:T(4,128)S(1)}, f32[7,4,128]{2,1,0:T(4,128)S(1)}, u32[]{:S(2)}, u32[]{:S(2)}) collective-permute-start(f32[7,4,128]{2,1,0:T(4,128)S(1)} %get-tuple-element.16), channel_id=1, source_target_pairs={{0,4},{4,8},{8,12},{12,16},{16,20},{20,24},{24,28},{28,0},{1,5},{5... | collective-permute-start | bytes 43016 | tf_op jit(solution)/shard_map/ppermute | solution.py:341
  16.6 15.0 %collective-permute-start.4 = (f32[7,32,128]{2,1,0:T(8,128)S(1)}, f32[7,32,128]{2,1,0:T(8,128)S(1)}, u32[]{:S(2)}, u32[]{:S(2)}) collective-permute-start(f32[7,32,128]{2,1,0:T(8,128)S(1)} %get-tuple-element.19), channel_id=1, source_target_pairs={{0,1},{1,0},{2,3},{3,2},{4,5},{5,4},{6,7},{7,6},{8,9},{9,8},{10,11... | collective-permute-start | bytes 344072 | tf_op jit(solution)/shard_map/ppermute | solution.py:296
  16.7 15.0 %collective-permute-start.5 = (f32[7,32,128]{2,1,0:T(8,128)S(1)}, f32[7,32,128]{2,1,0:T(8,128)S(1)}, u32[]{:S(2)}, u32[]{:S(2)}) collective-permute-start(f32[7,32,128]{2,1,0:T(8,128)S(1)} %get-tuple-element.20), channel_id=1, source_target_pairs={{0,3},{1,2},{2,1},{3,0},{4,7},{5,6},{6,5},{7,4},{8,11},{9,10},{10,... | collective-permute-start | bytes 344072 | tf_op jit(solution)/shard_map/ppermute | solution.py:296
  17.3 1.1 %collective-permute-start.6 = (f32[2,128]{1,0:T(2,128)S(1)}, f32[2,128]{1,0:T(2,128)S(1)}, u32[]{:S(2)}, u32[]{:S(2)}) collective-permute-start(f32[2,128]{1,0:T(2,128)S(1)} %get-tuple-element.24), channel_id=1, source_target_pairs={{0,1},{1,0},{2,3},{3,2},{4,5},{5,4},{6,7},{7,6},{8,9},{9,8},{10,11... | collective-permute-start | bytes 3080 | tf_op jit(solution)/shard_map/ppermute | solution.py:296
  18.5 3.2 %collective-permute-start.7 = (f32[2,128]{1,0:T(2,128)S(1)}, f32[2,128]{1,0:T(2,128)S(1)}, u32[]{:S(2)}, u32[]{:S(2)}) collective-permute-start(f32[2,128]{1,0:T(2,128)S(1)} %max.15), channel_id=1, source_target_pairs={{0,3},{1,2},{2,1},{3,0},{4,7},{5,6},{6,5},{7,4},{8,11},{9,10},{10,... | collective-permute-start | bytes 3080 | tf_op jit(solution)/shard_map/ppermute | solution.py:296
  21.7 3.0 %collective-permute-start.8 = (f32[2,128]{1,0:T(2,128)S(1)}, f32[2,128]{1,0:T(2,128)S(1)}, u32[]{:S(2)}, u32[]{:S(2)}) collective-permute-start(f32[2,128]{1,0:T(2,128)S(1)} %max.16), channel_id=1, source_target_pairs={{0,5},{1,4},{2,7},{3,6},{4,1},{5,0},{6,3},{7,2},{8,13},{9,12},{10,... | collective-permute-start | bytes 3080 | tf_op jit(solution)/shard_map/ppermute | solution.py:296
  24.7 3.0 %collective-permute-start.9 = (f32[2,128]{1,0:T(2,128)S(1)}, f32[2,128]{1,0:T(2,128)S(1)}, u32[]{:S(2)}, u32[]{:S(2)}) collective-permute-start(f32[2,128]{1,0:T(2,128)S(1)} %max.17), channel_id=1, source_target_pairs={{0,9},{1,8},{2,11},{3,10},{4,13},{5,12},{6,15},{7,14},{8,1},{9,0},... | collective-permute-start | bytes 3080 | tf_op jit(solution)/shard_map/ppermute | solution.py:296
  27.7 3.9 %collective-permute-start.10 = (f32[2,128]{1,0:T(2,128)S(1)}, f32[2,128]{1,0:T(2,128)S(1)}, u32[]{:S(2)}, u32[]{:S(2)}) collective-permute-start(f32[2,128]{1,0:T(2,128)S(1)} %max.18), channel_id=1, source_target_pairs={{0,17},{1,16},{2,19},{3,18},{4,21},{5,20},{6,23},{7,22},{8,25},{9,... | collective-permute-start | bytes 3080 | tf_op jit(solution)/shard_map/ppermute | solution.py:296
  31.7 1.0 %copy-start.1 = (f32[6,4,3072]{2,1,0:T(4,128)S(1)}, f32[6,4,3072]{2,1,0:T(4,128)}, u32[]{:S(2)}) copy-start(f32[6,4,3072]{2,1,0:T(4,128)} %param.3) | copy-start | bytes 884740
  32.6 0.8 %copy-start.3 = (f32[4,3072]{1,0:T(4,128)S(1)}, f32[4,3072]{1,0:T(4,128)}, u32[]{:S(2)}) copy-start(f32[4,3072]{1,0:T(4,128)} %param.4) | copy-start | bytes 147460

commit v3 on v2

v3 whole, which is shorter than its diff:
```python
import functools

import jax
import jax.numpy as jnp
from jax import lax
from jax.experimental import pallas as pl
from jax.experimental.pallas import tpu as pltpu
from jax.sharding import PartitionSpec as P

BW = 32
LANES = 128
PLANES = LANES // BW
GAMMA = 1.4
COURANT = 0.8
DEP_C, DEP_D, DEP_S, DEP_I, COST_I = 0, 1, 3, 4, 2
NQ = 13
VX, PR, SND, TMP, KAP = 6, 9, 10, 11, 12
VMEM = pl.BlockSpec(memory_space=pltpu.VMEM)
PARAMS = pltpu.CompilerParams(vmem_limit_bytes=24 * 1024 * 1024)


def f32(*shape):
    return jax.ShapeDtypeStruct(shape, jnp.float32)


def lanes_of(shape):
    return lax.broadcasted_iota(jnp.int32, shape, 1)


def rows_of(shape):
    return lax.broadcasted_iota(jnp.int32, shape, 0)


def load_kernel(prim, kappa, new_owner, own, peak, leaving, owner, sems):
    total = own.shape[1]
    copies = [
        pltpu.make_async_copy(prim, own.at[pl.ds(0, 6)], sems.at[0]),
        pltpu.make_async_copy(kappa, own.at[6], sems.at[1]),
        pltpu.make_async_copy(new_owner, owner, sems.at[2]),
    ]
    for copy in copies:
        copy.start()
    for copy in copies:
        copy.wait()
    speed = top = None
    for g in range(total // 8):
        r = pl.ds(8 * g, 8)
        sound = jnp.sqrt(GAMMA * own[4, r, :] / own[0, r, :])
        s = jnp.abs(own[1, r, :]) + jnp.abs(own[2, r, :]) + jnp.abs(own[3, r, :]) + 3.0 * sound
        speed = s if speed is None else jnp.maximum(speed, s)
        top = own[6, r, :] if top is None else jnp.maximum(top, own[6, r, :])
    peak[0:1, :] = jnp.max(speed, axis=0, keepdims=True)
    peak[1:2, :] = jnp.max(top, axis=0, keepdims=True)
    leaves = (owner[0] != lax.axis_index("curve")).astype(jnp.float32)
    leaving[...] = jnp.full(leaving.shape, leaves, jnp.float32)


def side_kernel(upper_when_even, own, leaving, order, msg):
    even = lax.axis_index("curve") % 2 == 0
    box = jnp.logical_not(even) if upper_when_even else even
    total = own.shape[1]
    for g in range(5):
        length = 8 if g < 4 else 4
        first, last = pl.ds(8 * g, length), pl.ds(total - 36 + 8 * g, length)
        parts = [jnp.where(box, own[f, first, :], own[f, last, :]) for f in range(7)]
        for f in range(7):
            msg[f, first, :] = parts[f]
    for f in range(7):
        msg[f, 36:40, :] = leaving[0:4, :]


def spread_kernel(own, rec_c, rec_d, peak, ext, msg_a, msg_b, arrival, peak_out):
    segment, segments = lax.axis_index("curve"), lax.axis_size("curve")
    first, last = segment == 0, segment == segments - 1
    odd = segment % 2 == 1
    even_slab = lax.axis_index("near") % 2 == 0
    groups = own.shape[1] // 32
    shape = (8, LANES)
    lane, row = lanes_of(shape), rows_of(shape)
    spread = lambda x: jnp.broadcast_to(x, shape)
    peak_out[...] = peak[...]
    arrival[...] = jnp.where(last, 0.0, spread(jnp.where(odd, rec_d[0, 36:37, :], rec_c[0, 36:37, :])))
    for f in range(7):
        out = []
        for z in range(4):
            cells = [own[f, pl.ds(z + 32 * g, 8, stride=4), :] for g in range(groups)]
            at = pl.ds(z, 8, stride=4)
            box = jnp.where(odd, rec_d[f, at, :], rec_c[f, at, :])
            beyond = spread(jnp.where(odd, rec_d[f, 32 + z : 33 + z, :], rec_c[f, 32 + z : 33 + z, :]))
            behind = spread(jnp.where(odd, rec_c[f, 32 + z : 33 + z, :], rec_d[f, 32 + z : 33 + z, :]))
            edge = pltpu.roll(spread(cells[-1][7:8]), BW, 1)
            box = jnp.where(last, edge, box)
            start, end = spread(cells[0][0:1]), spread(box[7:8])
            behind = jnp.where(first, pltpu.roll(start, LANES - BW, 1), behind)
            low_side = jnp.where(lane < BW, start, behind)
            high_side = jnp.where(lane >= LANES - BW, end, beyond)
            out.append(cells + [box, jnp.where(row == 7, high_side, low_side)])
        for z in range(4):
            for g, value in enumerate(out[z]):
                ext[f, z, 8 * g : 8 * g + 8, :] = value
        for msg, up in ((msg_a, even_slab), (msg_b, jnp.logical_not(even_slab))):
            for z in range(2):
                for g in range(groups + 2):
                    value = jnp.where(up, out[z + 2][g], out[z][g])
                    if g < groups + 1:
                        msg[f, 36 * z + 8 * g : 36 * z + 8 * g + 8, :] = value
                    else:
                        msg[f, 36 * z + 32 : 36 * z + 33, :] = value[0:1]
                        msg[f, 36 * z + 33 : 36 * z + 34, :] = value[7:8]


def up_x(q, lane):
    w = [pltpu.roll(v, LANES - BW, 1) for v in q[:4]]
    w.append(pltpu.roll(w[0], 7, 0))
    return [jnp.where(lane < LANES - BW, w[j], w[j + 1]) for j in range(4)] + [pltpu.roll(q[4], LANES - BW, 1)]


def up_y(v, low):
    return jnp.where(low == BW - 1, pltpu.roll(v, BW - 1, 1), pltpu.roll(v, LANES - 1, 1))


def down_y(v, low):
    return jnp.where(low == 0, pltpu.roll(v, LANES - BW + 1, 1), pltpu.roll(v, 1, 1))


def face(lower_u, upper_u, lower_f, upper_f, speed, heat):
    out = (lower_f + upper_f) - speed * (upper_u - lower_u)
    return out if heat is None else out - heat


def z_face_row(q, z, slots):
    speed, heat = [], []
    for j in range(slots):
        s0 = jnp.abs(q[VX + 2, z, j]) + q[SND, z, j]
        s1 = jnp.abs(q[VX + 2, z + 1, j]) + q[SND, z + 1, j]
        speed.append(jnp.maximum(s0, s1))
        heat.append((q[KAP, z, j] + q[KAP, z + 1, j]) * (q[TMP, z + 1, j] - q[TMP, z, j]))
    return {
        (f, j): face(
            q[f, z, j],
            q[f, z + 1, j],
            physical(q, f, j, 2, z),
            physical(q, f, j, 2, z + 1),
            speed[j],
            heat[j] if f == 4 else None,
        )
        for f in range(6)
        for j in range(slots)
    }


def physical(q, f, j, k, z):
    if f == 0:
        return q[1 + k, z, j]
    v = q[VX + k, z, j]
    if f == 4:
        return (q[4, z, j] + q[PR, z, j]) * v
    out = q[f, z, j] * v
    return out + q[PR, z, j] if f == 1 + k else out


def plane_divergence(q, z, slots):
    shape = (8, LANES)
    lane, row = lanes_of(shape), rows_of(shape)
    low = lane & (BW - 1)
    ghost = 4
    five = range(5)
    at = lambda i, j: q[i, z, j]
    sx = [jnp.abs(at(VX, j)) + at(SND, j) for j in five]
    sy = [jnp.abs(at(VX + 1, j)) + at(SND, j) for j in range(slots)]
    kx, tx = [at(KAP, j) for j in five], [at(TMP, j) for j in five]
    sxu, kxu, txu = up_x(sx, lane), up_x(kx, lane), up_x(tx, lane)
    syu, kyu, tyu = ([up_y(v, low) for v in vs[:slots]] for vs in (sy, kx, tx))
    ax = [jnp.maximum(v, w) for v, w in zip(sx, sxu, strict=True)]
    ay = [jnp.maximum(v, w) for v, w in zip(sy, syu, strict=True)]
    hx = [(kx[j] + kxu[j]) * (txu[j] - tx[j]) for j in five]
    hy = [(kx[j] + kyu[j]) * (tyu[j] - tx[j]) for j in range(slots)]

    def neighbours(f):
        u = [at(f, j) for j in five]
        fx = [physical(q, f, j, 0, z) for j in five]
        fy = [physical(q, f, j, 1, z) for j in range(slots)]
        return u, fx, fy, up_x(u, lane), up_x(fx, lane), [up_y(v, low) for v in u[:slots]], [up_y(v, low) for v in fy]

    def sides(f, u, fx, fy, ux, fux, uy, fuy):
        heat = lambda h: h if f == 4 else None
        gx = [face(u[j], ux[j], fx[j], fux[j], ax[j], heat(hx[j])) for j in five]
        gx[3] = jnp.where((lane >= LANES - BW) & (row == 7), gx[ghost], gx[3])
        d = [pltpu.roll(g, BW, 1) for g in gx]
        before = jnp.where(row == 0, d[ghost], pltpu.roll(d[3], 1, 0))
        dx = [jnp.where(lane >= BW, d[j], before if j == 0 else d[j - 1]) for j in range(4)] + [d[ghost]]
        gy = [face(u[j], uy[j], fy[j], fuy[j], ay[j], heat(hy[j])) for j in range(slots)]
        dy = [down_y(g, low) for g in gy]
        return [(gx[j] - dx[j]) + (gy[j] - dy[j]) for j in range(slots)]

    near = [neighbours(f) for f in range(6)]
    part = [sides(f, *near[f]) for f in range(6)]
    return {(f, j): part[f][j] for f in range(6) for j in range(slots)}


def raw_quantities(r, vx, vy, vz, p, s, k):
    t = p / r
    energy = p / (GAMMA - 1.0) + 0.5 * r * (vx * vx + vy * vy + vz * vz)
    return (r, r * vx, r * vy, r * vz, energy, r * s, vx, vy, vz, p, jnp.sqrt(GAMMA * t), t, k)


def store_all(ref, at, values):
    for j, quantities in enumerate(values):
        for i, value in enumerate(quantities):
            ref[(i,) + at + (j,)] = value


def inner_kernel(ext, order, q, total):
    @pl.loop(0, 4)
    def _(z):
        found = []
        for j in range(5):
            rows = pl.ds(j, 8, stride=4) if j < 4 else pl.ds(32, 8)
            found.append(raw_quantities(*(ext[f, z, rows, :] for f in range(7))))
        store_all(q, (z,), found)

    @pl.loop(0, 4)
    def _(z):
        values = plane_divergence(q, z, 5)
        for (f, j), value in values.items():
            total[f, z, j] = value

    @pl.loop(0, 3)
    def _(z):
        faces = z_face_row(q, z, 5)
        lower = {(f, j): total[f, z, j] + value for (f, j), value in faces.items()}
        upper = {(f, j): total[f, z + 1, j] - value for (f, j), value in faces.items()}
        for (f, j), value in lower.items():
            total[f, z, j] = value
        for (f, j), value in upper.items():
            total[f, z + 1, j] = value


def outer_kernel(q, inner, rec_a, rec_b, total, edge_q, edge_total, rim):
    even = lax.axis_index("near") % 2 == 0
    shape = (8, LANES)
    row = rows_of(shape)
    spread = lambda x: jnp.broadcast_to(x, shape)

    @pl.loop(0, 4)
    def _(z):
        for f in range(6):
            for j in range(5):
                total[f, z, j] = inner[f, z, j]

    for i in range(NQ):
        for j in range(5):
            rim[i, 2, j] = q[i, 0, j]
            rim[i, 3, j] = q[i, 3, j]
    for rec, base in ((rec_a, jnp.where(even, 4, 0)), (rec_b, jnp.where(even, 0, 4))):

        @pl.loop(0, 2)
        def _(z):
            found = []
            for j in range(5):
                if j < 4:
                    cells = (rec[f, pl.ds(36 * z + j, 8, stride=4), :] for f in range(7))
                else:
                    cells = (
                        jnp.where(row == 7, spread(rec[f, pl.ds(36 * z + 33, 1), :]), spread(rec[f, pl.ds(36 * z + 32, 1), :]))
                        for f in range(7)
                    )
                found.append(raw_quantities(*cells))
            store_all(rim, (base + z,), found)

    @pl.loop(0, 2)
    def _(e):
        z = 1 + 3 * e
        values = plane_divergence(rim, z, 5)
        for (f, j), value in values.items():
            edge_total[f, e, j] = value
        for j in range(5):
            for i, k in enumerate((0, 1, 2, 3, 4, 5, KAP)):
                edge_q[i, e, j] = rim[k, z, j]

    @pl.loop(0, 2)
    def _(e):
        below = z_face_row(rim, 3 * e, 5)
        above = z_face_row(rim, 3 * e + 1, 5)
        own = 3 * e
        change = {key: jnp.where(e == 0, -above[key], below[key]) for key in above}
        edge = {(f, j): edge_total[f, e, j] + (above[f, j] - below[f, j]) for f, j in above}
        done = {(f, j): inner[f, own, j] + value for (f, j), value in change.items()}
        for (f, j), value in edge.items():
            edge_total[f, e, j] = value
        for (f, j), value in done.items():
            total[f, own, j] = value


def second_kernel(base, total, edge_q, edge_total, arrival, peak, new_owner, out, q, zf, final, owner, sems):
    segment, segments = lax.axis_index("curve"), lax.axis_size("curve")
    shape = (8, LANES)
    lane, row = lanes_of(shape), rows_of(shape)
    first, last = segment == 0, segment == segments - 1
    fetch = pltpu.make_async_copy(new_owner, owner, sems.at[0])
    fetch.start()
    speed, top = jnp.max(peak[0:1, :]), jnp.max(peak[1:2, :])
    step = COURANT / (speed + 6.0 * top)

    def half_row(state, divergence, kap_at, source, target):
        half = [
            [state[f, source, j] - (0.5 * step) * divergence[f, source, j] for j in range(5)] for f in range(6)
        ]
        kap = [state[kap_at, source, j] for j in range(5)]
        for u in half + [kap]:
            edge = pltpu.roll(pltpu.roll(u[3], BW, 1), 1, 0)
            u[0] = jnp.where(last & (row == 6) & (lane < BW), edge, u[0])
            g = jnp.where((row == 0) & (lane < BW), u[0], u[4])
            g = jnp.where((row == 7) & (lane >= LANES - BW), u[3], g)
            u[4] = jnp.where(first & (row == 0) & (lane >= BW), pltpu.roll(g, LANES - BW, 1), g)
        found = []
        for j in range(5):
            r, mx, my, mz, e, s = (half[f][j] for f in range(6))
            inv = 1.0 / r
            vx, vy, vz = mx * inv, my * inv, mz * inv
            p = (GAMMA - 1.0) * (e - 0.5 * (mx * vx + my * vy + mz * vz))
            t = p * inv
            found.append((r, mx, my, mz, e, s, vx, vy, vz, p, jnp.sqrt(GAMMA * t), t, kap[j]))
        store_all(q, (target,), found)

    @pl.loop(0, 4)
    def _(z):
        half_row(base, total, KAP, z, z + 1)

    @pl.loop(0, 2)
    def _(e):
        half_row(edge_q, edge_total, 6, e, 5 * e)

    for key, value in z_face_row(q, 0, 4).items():
        zf[key] = value
    keep = (row < 6) | (arrival[...] > 0.5)
    final[:, 128:160, :] = jnp.zeros((6, 32, LANES), jnp.float32)

    @pl.loop(1, 5)
    def _(z):
        plane = plane_divergence(q, z, 4)
        faces = z_face_row(q, z, 4)
        done = {}
        for (f, j), value in faces.items():
            change = plane[f, j] + (value - zf[f, j])
            done[f, j] = 0.5 * (base[f, z - 1, j] + q[f, z, j]) - (0.25 * step) * change
        for (f, j), value in done.items():
            final[f, pl.ds(4 * j + z - 1, 8, stride=16), :] = jnp.where(keep, value, 0.0)
        for key, value in faces.items():
            zf[key] = value

    fetch.wait()
    start = jnp.where(owner[0] != segment, 32, 0)
    copy = pltpu.make_async_copy(final.at[:, pl.ds(pl.multiple_of(start, 32), 128), :], out, sems.at[1])
    copy.start()
    copy.wait()


def swap(x, partner):
    m, n = lax.axis_size("curve"), lax.axis_size("near")
    route = []
    for c in range(m):
        for i in range(n):
            to_c, to_i = partner(c, i)
            route.append((c * n + i, to_c * n + to_i))
    return lax.ppermute(x, ("curve", "near"), route)


def near_routes(n):
    routes = [lambda c, i: (c, i ^ 1), lambda c, i: (c, outer_partner(i, n))]
    reach = 4
    while reach < n:
        routes.append(lambda c, i, d=reach: (c, (i + d) % n))
        reach *= 2
    return routes


def curve_routes(m):
    routes, reach = [], 1
    while reach < m:
        if m % (2 * reach) == 0:
            routes.append(lambda c, i, d=reach: (c ^ d, i ^ 1))
        else:
            routes.append(lambda c, i, d=reach: ((c + d) % m, i ^ 1))
        reach *= 2
    return routes


def outer_partner(i, n):
    return ((i + 1) ^ 1) - 1 if 0 < i < n - 1 else n - 1 - i


def rows_view(x):
    lead, cells = x.shape[:-2], x.shape[-1]
    x = x.reshape(lead + (4, cells // LANES, LANES))
    return jnp.swapaxes(x, -3, -2).reshape(lead + (4 * (cells // LANES), LANES))


def kernel(body, name, ins, outs, scratch=(), us=0):
    cost = pl.CostEstimate(flops=int(us * 1e9), bytes_accessed=int(us * 3e6), transcendentals=0) if us else None
    return pl.pallas_call(
        body,
        out_shape=outs,
        in_specs=ins,
        out_specs=jax.tree.map(lambda _: VMEM, outs),
        scratch_shapes=scratch,
        compiler_params=PARAMS,
        cost_estimate=cost,
        name=name,
    )


def local(primitive, conductivity, new_owner):
    m, n = lax.axis_size("curve"), lax.axis_size("near")
    rows = primitive.shape[2] // LANES * 4
    in_hbm = lambda x: pltpu.with_memory_space_constraint(x, pltpu.HBM)
    prim, kappa, new_owner = in_hbm(rows_view(primitive)), in_hbm(rows_view(conductivity)), in_hbm(new_owner)
    hbm = pl.BlockSpec(memory_space=pltpu.HBM)

    own, peak, leaving = kernel(
        load_kernel,
        "load",
        [hbm, hbm, hbm],
        (f32(7, rows, LANES), f32(2, LANES), f32(8, LANES)),
        [pltpu.SMEM(new_owner.shape, jnp.int32), pltpu.SemaphoreType.DMA((3,))],
    )(prim, kappa, new_owner)

    side = lambda upper, name: kernel(functools.partial(side_kernel, upper), name, [VMEM] * 3, f32(7, 40, LANES))
    peaks = [peak]
    for stage, route in enumerate(near_routes(n) + curve_routes(m)):
        if stage == DEP_C:
            rec_c = swap(side(True, "upper")(own, leaving, peaks[-1]), lambda c, i: (c ^ 1, i))
        if stage == DEP_D:
            msg_d = side(False, "lower")(own, leaving, peaks[-1])
            rec_d = swap(msg_d, lambda c, i: (c, i ^ 1) if c in (0, m - 1) else (outer_partner(c, m), i))
        if stage == DEP_S:
            ext, msg_a, msg_b, arrival, peaks[-1] = kernel(
                spread_kernel,
                "spread",
                [VMEM] * 4,
                (f32(7, 4, 40, LANES), f32(7, 72, LANES), f32(7, 72, LANES), f32(8, LANES), f32(2, LANES)),
            )(own, rec_c, rec_d, peaks[-1])
        peaks.append(jnp.maximum(peaks[-1], swap(peaks[-1], route)))
    rec_a = swap(msg_a, lambda c, i: (c, i ^ 1))
    rec_b = swap(msg_b, lambda c, i: (c, outer_partner(i, n)))

    quantities, sums = f32(NQ, 4, 5, 8, LANES), f32(6, 4, 5, 8, LANES)
    q, inner = kernel(inner_kernel, "inner", [VMEM] * 2, (quantities, sums), us=COST_I)(ext, peaks[DEP_I])
    total, edge_q, edge_total = kernel(
        outer_kernel,
        "outer",
        [VMEM] * 4,
        (sums, f32(7, 2, 5, 8, LANES), f32(6, 2, 5, 8, LANES)),
        [pltpu.VMEM((NQ, 6, 5, 8, LANES), jnp.float32)],
    )(q, inner, rec_a, rec_b)

    out = pl.pallas_call(
        second_kernel,
        out_shape=f32(6, rows + 32, LANES),
        in_specs=[VMEM] * 6 + [hbm],
        out_specs=hbm,
        scratch_shapes=[
            pltpu.VMEM((NQ, 6, 5, 8, LANES), jnp.float32),
            pltpu.VMEM((6, 4, 8, LANES), jnp.float32),
            pltpu.VMEM((6, rows + 64, LANES), jnp.float32),
            pltpu.SMEM(new_owner.shape, jnp.int32),
            pltpu.SemaphoreType.DMA((2,)),
        ],
        compiler_params=PARAMS,
        name="second_section",
    )(q, total, edge_q, edge_total, arrival, peaks[-1], new_owner)
    out = jnp.swapaxes(out.reshape(6, (rows + 32) // 4, 4, LANES), 1, 2)
    return out.reshape(1, 6, 4, (rows + 32) // 4 * LANES)


def solution(mesh):
    in_specs = (P(None, "near", "curve"), P("near", "curve"), P("curve"))
    out_specs = P("curve", None, "near", None)
    return jax.shard_map(local, mesh=mesh, in_specs=in_specs, out_specs=out_specs, check_vma=False)
```

time: 40.2 us -> 26.1 us (0.65)
  waiting for transfers between devices: 19.3 us -> 4.21 us
  starting transfers between devices: 9.74 us -> 13.9 us
  local copies, waits for them, and re-layouts: 3.51 us -> 0 us
  Pallas kernels: 6.59 us -> 7.76 us
  between operations: 0.72 us -> 0.08 us
    ppermute x9, starting transfers between devices: 3.69 us -> 13.9 us  [swap(): return lax.ppermute(x, ('curve', 'near'), route)]
    ppermute x9, waiting for transfers between devices: 12.9 us -> 4.21 us  [swap(): return lax.ppermute(x, ('curve', 'near'), route)]
    ppermute x2 -> x0, waiting for transfers between devices: 6.41 us -> none  [the longest x1 6.41 us: local(): left = lax.ppermute(to_after, 'curve', [(c, (c + 1) % m) for c in range(m)])]
    ppermute x2 -> x0, starting transfers between devices: 6.06 us -> none  [the longest x1 6.06 us: local(): lax.ppermute(to_before, 'curve', [(c, (c - 1) % m) for c in range(m)])]
    unnamed x8 -> x0, local copies, waits for them, and re-layouts: 3.51 us -> none
    pallas_call x3 -> x6, Pallas kernels: 3.1 us -> 4.26 us  [the longest x1 1.85 us: local(): kernel(inner_kernel, 'inner', [VMEM] * 2, (quantities, sums), us=COST_I)]
  transfers between devices with their start and end apart: 11 -> 9, of which waited for: 6 -> 3; matrix products, arithmetic and copies ran while one was open for 0% -> 0% of each run, Pallas kernels for 0% -> 7%
where the time goes in v3:
time: 26.1 us; the launch traced here: 26 us
  starting transfers between devices  13.9 us (53%)
  Pallas kernels  7.76 us (30%)
  waiting for transfers between devices  4.21 us (16%)
    ppermute x9, starting transfers between devices, swap(): return lax.ppermute(x, ('curve', 'near'), route)  13.9 us
    ppermute x9, waiting for transfers between devices, swap(): return lax.ppermute(x, ('curve', 'near'), route)  4.21 us
    pallas_call x1, Pallas kernels, local(): pl.pallas_call(second_kernel, out_shape=f32(6, rows + 32, LANES), in_spec...  3.5 us
    pallas_call x1, Pallas kernels, local(): kernel(inner_kernel, 'inner', [VMEM] * 2, (quantities, sums), us=COST_I)  1.85 us
    pallas_call x1, Pallas kernels, local(): kernel(outer_kernel, 'outer', [VMEM] * 4, (sums, f32(7, 2, 5, 8, LANES),...  1.17 us
    pallas_call x1, Pallas kernels, local(): kernel(load_kernel, 'load', [hbm, hbm, hbm], (f32(7, rows, LANES), f32(2,...  1.04 us
  transfers between devices with their start and end apart: 9, of which 3 were waited for; matrix products, arithmetic and copies ran while one was open for 0% of the time, Pallas kernels for 7%

profile of v3, /device:TPU:0, one launch (start us, length us, event | category | flops | bytes accessed | tf_op | source)
XLA Modules:
  0.0 26.0 jit_solution(14480156132890498639)
XLA Ops:
  0.0 1.0 %load.1 = (f32[7,96,128]{2,1,0:T(8,128)S(1)}, f32[2,128]{1,0:T(2,128)S(1)}, f32[8,128]{1,0:T(8,128)S(1)}) custom-call(f32[6,96,128]{2,1,0:T(8,128)} %bitcast.15, f32[96,128]{1,0:T(8,128)} %bitcast.16, s32[3]{0:T(128)} %new_owner.3), custom_call_target="tpu_custom_call" | custom-call | tf_op jit(solution)/shard_map/load/pallas_call | solution.py:420
  1.1 0.5 %collective-permute-start.1 = (f32[2,128]{1,0:T(2,128)S(1)}, f32[2,128]{1,0:T(2,128)S(1)}, u32[]{:S(2)}, u32[]{:S(2)}) collective-permute-start(f32[2,128]{1,0:T(2,128)S(1)} %get-tuple-element.20.order), channel_id=1, source_target_pairs={{0,1},{1,0},{2,3},{3,2},{4,5},{5,4},{6,7},{7,6},{8,9},{9,8},{10,11... | collective-permute-start | bytes 3080 | tf_op jit(solution)/shard_map/ppermute | solution.py:366
  1.6 2.6 %collective-permute-start = (f32[7,40,128]{2,1,0:T(8,128)S(1)}, f32[7,40,128]{2,1,0:T(8,128)S(1)}, u32[]{:S(2)}, u32[]{:S(2)}) collective-permute-start(f32[7,40,128]{2,1,0:T(8,128)S(1)} %upper.1), channel_id=1, source_target_pairs={{0,4},{1,5},{2,6},{3,7},{4,0},{5,1},{6,2},{7,3},{8,12},{9,13},{10,... | collective-permute-start | bytes 430088 | tf_op jit(solution)/shard_map/ppermute | solution.py:366
  4.2 0.0 collective-permute-done.1
  4.2 0.3 %collective-permute-start.2 = (f32[7,40,128]{2,1,0:T(8,128)S(1)}, f32[7,40,128]{2,1,0:T(8,128)S(1)}, u32[]{:S(2)}, u32[]{:S(2)}) collective-permute-start(f32[7,40,128]{2,1,0:T(8,128)S(1)} %lower.1), channel_id=1, source_target_pairs={{0,1},{1,0},{2,3},{3,2},{4,8},{5,9},{6,10},{7,11},{8,4},{9,5},{10,... | collective-permute-start | bytes 430088 | tf_op jit(solution)/shard_map/ppermute | solution.py:366
  4.5 1.4 %collective-permute-start.3 = (f32[2,128]{1,0:T(2,128)S(1)}, f32[2,128]{1,0:T(2,128)S(1)}, u32[]{:S(2)}, u32[]{:S(2)}) collective-permute-start(f32[2,128]{1,0:T(2,128)S(1)} %max.15.order), channel_id=1, source_target_pairs={{0,3},{1,2},{2,1},{3,0},{4,7},{5,6},{6,5},{7,4},{8,11},{9,10},{10,... | collective-permute-start | bytes 3080 | tf_op jit(solution)/shard_map/ppermute | solution.py:366
  5.9 1.6 %collective-permute-done.3 = f32[2,128]{1,0:T(2,128)S(1)} collective-permute-done((f32[2,128]{1,0:T(2,128)S(1)}, f32[2,128]{1,0:T(2,128)S(1)}, u32[]{:S(2)}, u32[]{:S(2)}) %collective-permute-start.3) | collective-permute-done | bytes 1056 | tf_op jit(solution)/shard_map/ppermute | solution.py:366
  7.5 2.7 %collective-permute-start.4 = (f32[2,128]{1,0:T(2,128)S(1)}, f32[2,128]{1,0:T(2,128)S(1)}, u32[]{:S(2)}, u32[]{:S(2)}) collective-permute-start(f32[2,128]{1,0:T(2,128)S(1)} %max.16), channel_id=1, source_target_pairs={{0,5},{1,4},{2,7},{3,6},{4,1},{5,0},{6,3},{7,2},{8,13},{9,12},{10,... | collective-permute-start | bytes 3080 | tf_op jit(solution)/shard_map/ppermute | solution.py:366
  10.2 1.3 %collective-permute-done.4 = f32[2,128]{1,0:T(2,128)S(1)} collective-permute-done((f32[2,128]{1,0:T(2,128)S(1)}, f32[2,128]{1,0:T(2,128)S(1)}, u32[]{:S(2)}, u32[]{:S(2)}) %collective-permute-start.4) | collective-permute-done | bytes 1056 | tf_op jit(solution)/shard_map/ppermute | solution.py:366
  11.5 0.0 collective-permute-done.rec_c
  11.5 0.0 collective-permute-done.2.rec_d
  11.5 0.1 spread.1
  11.6 0.3 %collective-permute-start.6 = (f32[7,72,128]{2,1,0:T(8,128)S(1)}, f32[7,72,128]{2,1,0:T(8,128)S(1)}, u32[]{:S(2)}, u32[]{:S(2)}) collective-permute-start(f32[7,72,128]{2,1,0:T(8,128)S(1)} %get-tuple-element.25), channel_id=1, source_target_pairs={{0,1},{1,0},{2,3},{3,2},{4,5},{5,4},{6,7},{7,6},{8,9},{9,8},{10,11... | collective-permute-start | bytes 774152 | tf_op jit(solution)/shard_map/ppermute | solution.py:366
  11.9 1.4 %collective-permute-start.7 = (f32[7,72,128]{2,1,0:T(8,128)S(1)}, f32[7,72,128]{2,1,0:T(8,128)S(1)}, u32[]{:S(2)}, u32[]{:S(2)}) collective-permute-start(f32[7,72,128]{2,1,0:T(8,128)S(1)} %get-tuple-element.26), channel_id=1, source_target_pairs={{0,3},{1,2},{2,1},{3,0},{4,7},{5,6},{6,5},{7,4},{8,11},{9,10},{10,... | collective-permute-start | bytes 774152 | tf_op jit(solution)/shard_map/ppermute | solution.py:366
  13.3 1.8 %collective-permute-start.5 = (f32[2,128]{1,0:T(2,128)S(1)}, f32[2,128]{1,0:T(2,128)S(1)}, u32[]{:S(2)}, u32[]{:S(2)}) collective-permute-start(f32[2,128]{1,0:T(2,128)S(1)} %get-tuple-element.22), channel_id=1, source_target_pairs={{0,9},{1,8},{2,11},{3,10},{4,13},{5,12},{6,15},{7,14},{8,1},{9,0},... | collective-permute-start | bytes 3080 | tf_op jit(solution)/shard_map/ppermute | solution.py:366
  15.1 1.3 %collective-permute-done.5 = f32[2,128]{1,0:T(2,128)S(1)} collective-permute-done((f32[2,128]{1,0:T(2,128)S(1)}, f32[2,128]{1,0:T(2,128)S(1)}, u32[]{:S(2)}, u32[]{:S(2)}) %collective-permute-start.5) | collective-permute-done | bytes 1056 | tf_op jit(solution)/shard_map/ppermute | solution.py:366
  16.4 3.0 %collective-permute-start.8 = (f32[2,128]{1,0:T(2,128)S(1)}, f32[2,128]{1,0:T(2,128)S(1)}, u32[]{:S(2)}, u32[]{:S(2)}) collective-permute-start(f32[2,128]{1,0:T(2,128)S(1)} %max.18.order), channel_id=1, source_target_pairs={{0,17},{1,16},{2,19},{3,18},{4,21},{5,20},{6,23},{7,22},{8,25},{9,... | collective-permute-start | bytes 3080 | tf_op jit(solution)/shard_map/ppermute | solution.py:366
  19.4 1.8 %inner.1 = (f32[13,4,5,8,128]{4,3,2,1,0:T(8,128)S(1)}, f32[6,4,5,8,128]{4,3,2,1,0:T(8,128)S(1)}) custom-call(f32[7,4,40,128]{3,2,1,0:T(8,128)S(1)} %get-tuple-element.21.ext, f32[2,128]{1,0:T(2,128)S(1)} %max.18.order), custom_call_target="tpu_custom_call" | custom-call | flops 2000000000 | bytes 6000000 | tf_op jit(solution)/shard_map/inner/pallas_call | solution.py:448
  21.2 0.0 collective-permute-done.8
  21.3 0.0 collective-permute-done.6.rec_a
  21.3 0.0 collective-permute-done.7.rec_b
  21.3 1.2 %outer.1 = (f32[6,4,5,8,128]{4,3,2,1,0:T(8,128)S(1)}, f32[7,2,5,8,128]{4,3,2,1,0:T(8,128)S(1)}, f32[6,2,5,8,128]{4,3,2,1,0:T(8,128)S(1)}) custom-call(f32[13,4,5,8,128]{4,3,2,1,0:T(8,128)S(1)} %get-tuple-element.23.q.base, f32[6,4,5,8,128]{4,3,2,1,0:T(8,128)S(1)} %get-tuple-element.24.inner, f32[7,72,128]{2,1,0:T(8,128)S(1)} %collective-permute-done.6.rec_a, ...), custom_call_target="tpu_custom_call" | custom-call | tf_op jit(solution)/shard_map/outer/pallas_call | solution.py:449
  22.5 3.5 %second_section.1 = f32[6,128,128]{2,1,0:T(8,128)} custom-call(f32[13,4,5,8,128]{4,3,2,1,0:T(8,128)S(1)} %get-tuple-element.23.q.base, f32[6,4,5,8,128]{4,3,2,1,0:T(8,128)S(1)} %get-tuple-element.27.total, f32[7,2,5,8,128]{4,3,2,1,0:T(8,128)S(1)} %get-tuple-element.28.edge_q, f32[6,2,5,8,128]{4,3,2,1,0:T(8,128)S(1)} %get-tuple-element.29.edge_total, ...), custom_call_target="tpu_custom_call" | custom-call | tf_op jit(solution)/shard_map/second_section/pallas_call | solution.py:457
  (7 shorter events, 0.1 us)
Async XLA Ops:
  1.1 3.1 %collective-permute-start.1 = (f32[2,128]{1,0:T(2,128)S(1)}, f32[2,128]{1,0:T(2,128)S(1)}, u32[]{:S(2)}, u32[]{:S(2)}) collective-permute-start(f32[2,128]{1,0:T(2,128)S(1)} %get-tuple-element.20.order), channel_id=1, source_target_pairs={{0,1},{1,0},{2,3},{3,2},{4,5},{5,4},{6,7},{7,6},{8,9},{9,8},{10,11... | collective-permute-start | bytes 3080 | tf_op jit(solution)/shard_map/ppermute | solution.py:366
  1.6 9.9 %collective-permute-start = (f32[7,40,128]{2,1,0:T(8,128)S(1)}, f32[7,40,128]{2,1,0:T(8,128)S(1)}, u32[]{:S(2)}, u32[]{:S(2)}) collective-permute-start(f32[7,40,128]{2,1,0:T(8,128)S(1)} %upper.1), channel_id=1, source_target_pairs={{0,4},{1,5},{2,6},{3,7},{4,0},{5,1},{6,2},{7,3},{8,12},{9,13},{10,... | collective-permute-start | bytes 430088 | tf_op jit(solution)/shard_map/ppermute | solution.py:366
  4.2 7.2 %collective-permute-start.2 = (f32[7,40,128]{2,1,0:T(8,128)S(1)}, f32[7,40,128]{2,1,0:T(8,128)S(1)}, u32[]{:S(2)}, u32[]{:S(2)}) collective-permute-start(f32[7,40,128]{2,1,0:T(8,128)S(1)} %lower.1), channel_id=1, source_target_pairs={{0,1},{1,0},{2,3},{3,2},{4,8},{5,9},{6,10},{7,11},{8,4},{9,5},{10,... | collective-permute-start | bytes 430088 | tf_op jit(solution)/shard_map/ppermute | solution.py:366
  4.5 3.0 %collective-permute-start.3 = (f32[2,128]{1,0:T(2,128)S(1)}, f32[2,128]{1,0:T(2,128)S(1)}, u32[]{:S(2)}, u32[]{:S(2)}) collective-permute-start(f32[2,128]{1,0:T(2,128)S(1)} %max.15.order), channel_id=1, source_target_pairs={{0,3},{1,2},{2,1},{3,0},{4,7},{5,6},{6,5},{7,4},{8,11},{9,10},{10,... | collective-permute-start | bytes 3080 | tf_op jit(solution)/shard_map/ppermute | solution.py:366
  7.5 4.0 %collective-permute-start.4 = (f32[2,128]{1,0:T(2,128)S(1)}, f32[2,128]{1,0:T(2,128)S(1)}, u32[]{:S(2)}, u32[]{:S(2)}) collective-permute-start(f32[2,128]{1,0:T(2,128)S(1)} %max.16), channel_id=1, source_target_pairs={{0,5},{1,4},{2,7},{3,6},{4,1},{5,0},{6,3},{7,2},{8,13},{9,12},{10,... | collective-permute-start | bytes 3080 | tf_op jit(solution)/shard_map/ppermute | solution.py:366
  11.6 9.6 %collective-permute-start.6 = (f32[7,72,128]{2,1,0:T(8,128)S(1)}, f32[7,72,128]{2,1,0:T(8,128)S(1)}, u32[]{:S(2)}, u32[]{:S(2)}) collective-permute-start(f32[7,72,128]{2,1,0:T(8,128)S(1)} %get-tuple-element.25), channel_id=1, source_target_pairs={{0,1},{1,0},{2,3},{3,2},{4,5},{5,4},{6,7},{7,6},{8,9},{9,8},{10,11... | collective-permute-start | bytes 774152 | tf_op jit(solution)/shard_map/ppermute | solution.py:366
  11.9 9.3 %collective-permute-start.7 = (f32[7,72,128]{2,1,0:T(8,128)S(1)}, f32[7,72,128]{2,1,0:T(8,128)S(1)}, u32[]{:S(2)}, u32[]{:S(2)}) collective-permute-start(f32[7,72,128]{2,1,0:T(8,128)S(1)} %get-tuple-element.26), channel_id=1, source_target_pairs={{0,3},{1,2},{2,1},{3,0},{4,7},{5,6},{6,5},{7,4},{8,11},{9,10},{10,... | collective-permute-start | bytes 774152 | tf_op jit(solution)/shard_map/ppermute | solution.py:366
  13.3 3.1 %collective-permute-start.5 = (f32[2,128]{1,0:T(2,128)S(1)}, f32[2,128]{1,0:T(2,128)S(1)}, u32[]{:S(2)}, u32[]{:S(2)}) collective-permute-start(f32[2,128]{1,0:T(2,128)S(1)} %get-tuple-element.22), channel_id=1, source_target_pairs={{0,9},{1,8},{2,11},{3,10},{4,13},{5,12},{6,15},{7,14},{8,1},{9,0},... | collective-permute-start | bytes 3080 | tf_op jit(solution)/shard_map/ppermute | solution.py:366
  16.4 4.9 %collective-permute-start.8 = (f32[2,128]{1,0:T(2,128)S(1)}, f32[2,128]{1,0:T(2,128)S(1)}, u32[]{:S(2)}, u32[]{:S(2)}) collective-permute-start(f32[2,128]{1,0:T(2,128)S(1)} %max.18.order), channel_id=1, source_target_pairs={{0,17},{1,16},{2,19},{3,18},{4,21},{5,20},{6,23},{7,22},{8,25},{9,... | collective-permute-start | bytes 3080 | tf_op jit(solution)/shard_map/ppermute | solution.py:366

commit v4 on v3

--- a/solution.py
+++ b/solution.py
@@ -12,7 +12,8 @@
 PLANES = LANES // BW
 GAMMA = 1.4
 COURANT = 0.8
-DEP_C, DEP_D, DEP_S, DEP_I, COST_I = 0, 1, 3, 4, 2
+DEP_C, DEP_D, DEP_B, DEP_S, DEP_I = 0, 1, 2, 3, 3
+COST = {"slab": 0, "spread": 0, "inner": 2, "outer": 2}
 NQ = 13
 VX, PR, SND, TMP, KAP = 6, 9, 10, 11, 12
 VMEM = pl.BlockSpec(memory_space=pltpu.VMEM)
@@ -69,11 +70,24 @@
         msg[f, 36:40, :] = leaving[0:4, :]
 
 
+def slab_kernel(own, order, msg):
+    up = lax.axis_index("near") % 2 == 1
+    groups = own.shape[1] // 32
+    for f in range(7):
+        parts = {}
+        for z in range(2):
+            for g in range(groups):
+                upper, lower = (own[f, pl.ds(k + 32 * g, 8, stride=4), :] for k in (z + 2, z))
+                parts[8 * (groups * z + g)] = jnp.where(up, upper, lower)
+        for at, value in parts.items():
+            msg[f, at : at + 8, :] = value
+
+
 def spread_kernel(own, rec_c, rec_d, peak, ext, msg_a, msg_b, arrival, peak_out):
     segment, segments = lax.axis_index("curve"), lax.axis_size("curve")
     first, last = segment == 0, segment == segments - 1
     odd = segment % 2 == 1
-    even_slab = lax.axis_index("near") % 2 == 0
+    up = lax.axis_index("near") % 2 == 0
     groups = own.shape[1] // 32
     shape = (8, LANES)
     lane, row = lanes_of(shape), rows_of(shape)
@@ -98,15 +112,16 @@
         for z in range(4):
             for g, value in enumerate(out[z]):
                 ext[f, z, 8 * g : 8 * g + 8, :] = value
-        for msg, up in ((msg_a, even_slab), (msg_b, jnp.logical_not(even_slab))):
+        for msg, ahead, pitch, begin in ((msg_a, up, 36, 0), (msg_b, jnp.logical_not(up), 12, groups)):
             for z in range(2):
-                for g in range(groups + 2):
-                    value = jnp.where(up, out[z + 2][g], out[z][g])
+                for g in range(begin, groups + 2):
+                    value = jnp.where(ahead, out[z + 2][g], out[z][g])
+                    at = pitch * z + 8 * (g - begin)
                     if g < groups + 1:
-                        msg[f, 36 * z + 8 * g : 36 * z + 8 * g + 8, :] = value
+                        msg[f, at : at + 8, :] = value
                     else:
-                        msg[f, 36 * z + 32 : 36 * z + 33, :] = value[0:1]
-                        msg[f, 36 * z + 33 : 36 * z + 34, :] = value[7:8]
+                        msg[f, at : at + 1, :] = value[0:1]
+                        msg[f, at + 1 : at + 2, :] = value[7:8]
 
 
 def up_x(q, lane):
@@ -210,8 +225,10 @@
             ref[(i,) + at + (j,)] = value
 
 
-def inner_kernel(ext, order, q, total):
-    @pl.loop(0, 4)
+def inner_kernel(ext, q, total, token):
+    token[...] = jnp.zeros(token.shape, jnp.float32)
+
+    @pl.loop(0, 4, unroll=True)
     def _(z):
         found = []
         for j in range(5):
@@ -219,13 +236,13 @@
             found.append(raw_quantities(*(ext[f, z, rows, :] for f in range(7))))
         store_all(q, (z,), found)
 
-    @pl.loop(0, 4)
+    @pl.loop(0, 4, unroll=True)
     def _(z):
         values = plane_divergence(q, z, 5)
         for (f, j), value in values.items():
             total[f, z, j] = value
 
-    @pl.loop(0, 3)
+    @pl.loop(0, 3, unroll=True)
     def _(z):
         faces = z_face_row(q, z, 5)
         lower = {(f, j): total[f, z, j] + value for (f, j), value in faces.items()}
@@ -236,25 +253,32 @@
             total[f, z + 1, j] = value
 
 
-def outer_kernel(q, inner, rec_a, rec_b, total, edge_q, edge_total, rim):
+def outer_kernel(q, inner, rec_a, rec_slab, rec_b, total, edge_q, edge_total, token, rim, joined):
     even = lax.axis_index("near") % 2 == 0
     shape = (8, LANES)
     row = rows_of(shape)
     spread = lambda x: jnp.broadcast_to(x, shape)
 
-    @pl.loop(0, 4)
+    @pl.loop(0, 4, unroll=True)
     def _(z):
         for f in range(6):
             for j in range(5):
                 total[f, z, j] = inner[f, z, j]
 
+    token[...] = jnp.zeros(token.shape, jnp.float32)
+    slab, pitch = rec_slab.shape[1] // 2, rec_a.shape[1] // 2
+    for f in range(7):
+        for z in range(2):
+            at, to = 12 * z, pitch * z
+            joined[f, to : to + slab, :] = rec_slab[f, slab * z : slab * z + slab, :]
+            joined[f, to + slab : to + slab + 10, :] = rec_b[f, at : at + 10, :]
     for i in range(NQ):
         for j in range(5):
             rim[i, 2, j] = q[i, 0, j]
             rim[i, 3, j] = q[i, 3, j]
-    for rec, base in ((rec_a, jnp.where(even, 4, 0)), (rec_b, jnp.where(even, 0, 4))):
-
-        @pl.loop(0, 2)
+    for rec, base in ((rec_a, jnp.where(even, 4, 0)), (joined, jnp.where(even, 0, 4))):
+
+        @pl.loop(0, 2, unroll=True)
         def _(z):
             found = []
             for j in range(5):
@@ -268,7 +292,7 @@
                 found.append(raw_quantities(*cells))
             store_all(rim, (base + z,), found)
 
-    @pl.loop(0, 2)
+    @pl.loop(0, 2, unroll=True)
     def _(e):
         z = 1 + 3 * e
         values = plane_divergence(rim, z, 5)
@@ -278,7 +302,7 @@
             for i, k in enumerate((0, 1, 2, 3, 4, 5, KAP)):
                 edge_q[i, e, j] = rim[k, z, j]
 
-    @pl.loop(0, 2)
+    @pl.loop(0, 2, unroll=True)
     def _(e):
         below = z_face_row(rim, 3 * e, 5)
         above = z_face_row(rim, 3 * e + 1, 5)
@@ -323,11 +347,11 @@
             found.append((r, mx, my, mz, e, s, vx, vy, vz, p, jnp.sqrt(GAMMA * t), t, kap[j]))
         store_all(q, (target,), found)
 
-    @pl.loop(0, 4)
+    @pl.loop(0, 4, unroll=True)
     def _(z):
         half_row(base, total, KAP, z, z + 1)
 
-    @pl.loop(0, 2)
+    @pl.loop(0, 2, unroll=True)
     def _(e):
         half_row(edge_q, edge_total, 6, e, 5 * e)
 
@@ -336,7 +360,7 @@
     keep = (row < 6) | (arrival[...] > 0.5)
     final[:, 128:160, :] = jnp.zeros((6, 32, LANES), jnp.float32)
 
-    @pl.loop(1, 5)
+    @pl.loop(1, 5, unroll=True)
     def _(z):
         plane = plane_divergence(q, z, 4)
         faces = z_face_row(q, z, 4)
@@ -426,33 +450,43 @@
     )(prim, kappa, new_owner)
 
     side = lambda upper, name: kernel(functools.partial(side_kernel, upper), name, [VMEM] * 3, f32(7, 40, LANES))
-    peaks = [peak]
-    for stage, route in enumerate(near_routes(n) + curve_routes(m)):
+    quantities, sums = f32(NQ, 4, 5, 8, LANES), f32(6, 4, 5, 8, LANES)
+    routes = near_routes(n) + curve_routes(m)
+    token = None
+    for stage, route in enumerate(routes):
         if stage == DEP_C:
-            rec_c = swap(side(True, "upper")(own, leaving, peaks[-1]), lambda c, i: (c ^ 1, i))
+            rec_c = swap(side(True, "upper")(own, leaving, peak), lambda c, i: (c ^ 1, i))
         if stage == DEP_D:
-            msg_d = side(False, "lower")(own, leaving, peaks[-1])
+            msg_d = side(False, "lower")(own, leaving, peak)
             rec_d = swap(msg_d, lambda c, i: (c, i ^ 1) if c in (0, m - 1) else (outer_partner(c, m), i))
+        if stage == DEP_B:
+            slab = kernel(slab_kernel, "slab", [VMEM] * 2, f32(7, rows // 2, LANES), us=COST["slab"])(own, peak)
+            rec_slab = swap(slab, lambda c, i: (c, outer_partner(i, n)))
         if stage == DEP_S:
-            ext, msg_a, msg_b, arrival, peaks[-1] = kernel(
+            ext, msg_a, msg_b, arrival, peak = kernel(
                 spread_kernel,
                 "spread",
                 [VMEM] * 4,
-                (f32(7, 4, 40, LANES), f32(7, 72, LANES), f32(7, 72, LANES), f32(8, LANES), f32(2, LANES)),
-            )(own, rec_c, rec_d, peaks[-1])
-        peaks.append(jnp.maximum(peaks[-1], swap(peaks[-1], route)))
-    rec_a = swap(msg_a, lambda c, i: (c, i ^ 1))
-    rec_b = swap(msg_b, lambda c, i: (c, outer_partner(i, n)))
-
-    quantities, sums = f32(NQ, 4, 5, 8, LANES), f32(6, 4, 5, 8, LANES)
-    q, inner = kernel(inner_kernel, "inner", [VMEM] * 2, (quantities, sums), us=COST_I)(ext, peaks[DEP_I])
-    total, edge_q, edge_total = kernel(
+                (f32(7, 4, 40, LANES), f32(7, 72, LANES), f32(7, 24, LANES), f32(8, LANES), f32(2, LANES)),
+                us=COST["spread"],
+            )(own, rec_c, rec_d, peak)
+            rec_a = swap(msg_a, lambda c, i: (c, i ^ 1))
+            rec_b = swap(msg_b, lambda c, i: (c, outer_partner(i, n)))
+            q, inner, token = kernel(
+                inner_kernel, "inner", [VMEM], (quantities, sums, f32(2, LANES)), us=COST["inner"]
+            )(ext)
+        peak = jnp.maximum(peak, swap(peak, route))
+        if stage == DEP_I:
+            peak = jnp.maximum(peak, token)
+    total, edge_q, edge_total, token = kernel(
         outer_kernel,
         "outer",
-        [VMEM] * 4,
-        (sums, f32(7, 2, 5, 8, LANES), f32(6, 2, 5, 8, LANES)),
-        [pltpu.VMEM((NQ, 6, 5, 8, LANES), jnp.float32)],
-    )(q, inner, rec_a, rec_b)
+        [VMEM] * 5,
+        (sums, f32(7, 2, 5, 8, LANES), f32(6, 2, 5, 8, LANES), f32(2, LANES)),
+        [pltpu.VMEM((NQ, 6, 5, 8, LANES), jnp.float32), pltpu.VMEM((7, 72, LANES), jnp.float32)],
+        us=COST["outer"],
+    )(q, inner, rec_a, rec_slab, rec_b)
+    peak = jnp.maximum(peak, token)
 
     out = pl.pallas_call(
         second_kernel,
@@ -468,7 +502,7 @@
         ],
         compiler_params=PARAMS,
         name="second_section",
-    )(q, total, edge_q, edge_total, arrival, peaks[-1], new_owner)
+    )(q, total, edge_q, edge_total, arrival, peak, new_owner)
     out = jnp.swapaxes(out.reshape(6, (rows + 32) // 4, 4, LANES), 1, 2)
     return out.reshape(1, 6, 4, (rows + 32) // 4 * LANES)
 

time: 26.1 us -> 22.9 us (0.88)
  waiting for transfers between devices: 4.21 us -> 1.9 us
  Pallas kernels: 7.76 us -> 6.02 us
  starting transfers between devices: 13.9 us -> 14.8 us
    ppermute x9 -> x10, waiting for transfers between devices: 4.21 us -> 1.9 us  [swap(): return lax.ppermute(x, ('curve', 'near'), route)]
    pallas_call x1, Pallas kernels: 3.5 us -> 2.27 us  [local(): pl.pallas_call(second_kernel, out_shape=f32(6, rows + 32, LANES), in_spec...]
    ppermute x9 -> x10, starting transfers between devices: 13.9 us -> 14.8 us  [swap(): return lax.ppermute(x, ('curve', 'near'), route)]
    pallas_call x4 -> x5, Pallas kernels: 3.07 us -> 2.57 us  [the longest x1 1.44 us: local(): kernel(inner_kernel, 'inner', [VMEM], (quantities, sums, f32(2, LANES)),...]
  transfers between devices with their start and end apart: 9 -> 10, of which waited for: 3 -> 2; matrix products, arithmetic and copies ran while one was open for 0% -> 0% of each run, Pallas kernels for 7% -> 12%
where the time goes in v4:
time: 22.9 us; the launch traced here: 22.8 us
  starting transfers between devices  14.8 us (65%)
  Pallas kernels  6.02 us (26%)
  waiting for transfers between devices  1.9 us (8%)
    ppermute x10, starting transfers between devices, swap(): return lax.ppermute(x, ('curve', 'near'), route)  14.8 us
    pallas_call x1, Pallas kernels, local(): pl.pallas_call(second_kernel, out_shape=f32(6, rows + 32, LANES), in_spec...  2.27 us
    ppermute x10, waiting for transfers between devices, swap(): return lax.ppermute(x, ('curve', 'near'), route)  1.9 us
    pallas_call x1, Pallas kernels, local(): kernel(inner_kernel, 'inner', [VMEM], (quantities, sums, f32(2, LANES)),...  1.44 us
    pallas_call x1, Pallas kernels, local(): kernel(outer_kernel, 'outer', [VMEM] * 5, (sums, f32(7, 2, 5, 8, LANES),...  1.05 us
    pallas_call x1, Pallas kernels, local(): kernel(load_kernel, 'load', [hbm, hbm, hbm], (f32(7, rows, LANES), f32(2,...  1.04 us
  transfers between devices with their start and end apart: 10, of which 2 were waited for; matrix products, arithmetic and copies ran while one was open for 0% of the time, Pallas kernels for 12%

profile of v4, /device:TPU:0, one launch (start us, length us, event | category | flops | bytes accessed | tf_op | source)
XLA Modules:
  0.0 22.8 jit_solution(14209425721532263278)
XLA Ops:
  0.0 1.0 %load.1 = (f32[7,96,128]{2,1,0:T(8,128)S(1)}, f32[2,128]{1,0:T(2,128)S(1)}, f32[8,128]{1,0:T(8,128)S(1)}) custom-call(f32[6,96,128]{2,1,0:T(8,128)} %bitcast.15, f32[96,128]{1,0:T(8,128)} %bitcast.16, s32[3]{0:T(128)} %new_owner.3), custom_call_target="tpu_custom_call" | custom-call | tf_op jit(solution)/shard_map/load/pallas_call | solution.py:444
  1.1 0.5 %collective-permute-start.1 = (f32[2,128]{1,0:T(2,128)S(1)}, f32[2,128]{1,0:T(2,128)S(1)}, u32[]{:S(2)}, u32[]{:S(2)}) collective-permute-start(f32[2,128]{1,0:T(2,128)S(1)} %get-tuple-element.22.order), channel_id=1, source_target_pairs={{0,1},{1,0},{2,3},{3,2},{4,5},{5,4},{6,7},{7,6},{8,9},{9,8},{10,11... | collective-permute-start | bytes 3080 | tf_op jit(solution)/shard_map/ppermute | solution.py:390
  1.6 2.6 %collective-permute-start = (f32[7,40,128]{2,1,0:T(8,128)S(1)}, f32[7,40,128]{2,1,0:T(8,128)S(1)}, u32[]{:S(2)}, u32[]{:S(2)}) collective-permute-start(f32[7,40,128]{2,1,0:T(8,128)S(1)} %upper.1), channel_id=1, source_target_pairs={{0,4},{1,5},{2,6},{3,7},{4,0},{5,1},{6,2},{7,3},{8,12},{9,13},{10,... | collective-permute-start | bytes 430088 | tf_op jit(solution)/shard_map/ppermute | solution.py:390
  4.2 0.0 collective-permute-done.1
  4.2 0.3 %collective-permute-start.2 = (f32[7,40,128]{2,1,0:T(8,128)S(1)}, f32[7,40,128]{2,1,0:T(8,128)S(1)}, u32[]{:S(2)}, u32[]{:S(2)}) collective-permute-start(f32[7,40,128]{2,1,0:T(8,128)S(1)} %lower.1), channel_id=1, source_target_pairs={{0,1},{1,0},{2,3},{3,2},{4,8},{5,9},{6,10},{7,11},{8,4},{9,5},{10,... | collective-permute-start | bytes 430088 | tf_op jit(solution)/shard_map/ppermute | solution.py:390
  4.5 1.4 %collective-permute-start.3 = (f32[2,128]{1,0:T(2,128)S(1)}, f32[2,128]{1,0:T(2,128)S(1)}, u32[]{:S(2)}, u32[]{:S(2)}) collective-permute-start(f32[2,128]{1,0:T(2,128)S(1)} %max.21.order), channel_id=1, source_target_pairs={{0,3},{1,2},{2,1},{3,0},{4,7},{5,6},{6,5},{7,4},{8,11},{9,10},{10,... | collective-permute-start | bytes 3080 | tf_op jit(solution)/shard_map/ppermute | solution.py:390
  5.9 1.6 %collective-permute-done.3 = f32[2,128]{1,0:T(2,128)S(1)} collective-permute-done((f32[2,128]{1,0:T(2,128)S(1)}, f32[2,128]{1,0:T(2,128)S(1)}, u32[]{:S(2)}, u32[]{:S(2)}) %collective-permute-start.3) | collective-permute-done | bytes 1056 | tf_op jit(solution)/shard_map/ppermute | solution.py:390
  7.5 2.7 %collective-permute-start.4 = (f32[2,128]{1,0:T(2,128)S(1)}, f32[2,128]{1,0:T(2,128)S(1)}, u32[]{:S(2)}, u32[]{:S(2)}) collective-permute-start(f32[2,128]{1,0:T(2,128)S(1)} %max.22.order), channel_id=1, source_target_pairs={{0,5},{1,4},{2,7},{3,6},{4,1},{5,0},{6,3},{7,2},{8,13},{9,12},{10,... | collective-permute-start | bytes 3080 | tf_op jit(solution)/shard_map/ppermute | solution.py:390
  10.2 1.4 %collective-permute-start.6 = (f32[7,48,128]{2,1,0:T(8,128)S(1)}, f32[7,48,128]{2,1,0:T(8,128)S(1)}, u32[]{:S(2)}, u32[]{:S(2)}) collective-permute-start(f32[7,48,128]{2,1,0:T(8,128)S(1)} %slab.1), channel_id=1, source_target_pairs={{0,3},{1,2},{2,1},{3,0},{4,7},{5,6},{6,5},{7,4},{8,11},{9,10},{10,... | collective-permute-start | bytes 516104 | tf_op jit(solution)/shard_map/ppermute | solution.py:390
  11.6 0.0 collective-permute-done.4
  11.7 0.0 collective-permute-done.rec_c
  11.7 0.0 collective-permute-done.2.rec_d
  11.7 0.1 spread.1
  11.8 1.6 %collective-permute-start.8 = (f32[2,128]{1,0:T(2,128)S(1)}, f32[2,128]{1,0:T(2,128)S(1)}, u32[]{:S(2)}, u32[]{:S(2)}) collective-permute-start(f32[2,128]{1,0:T(2,128)S(1)} %get-tuple-element.32), channel_id=1, source_target_pairs={{0,9},{1,8},{2,11},{3,10},{4,13},{5,12},{6,15},{7,14},{8,1},{9,0},... | collective-permute-start | bytes 3080 | tf_op jit(solution)/shard_map/ppermute | solution.py:390
  13.4 1.5 %collective-permute-start.7 = (f32[7,24,128]{2,1,0:T(8,128)S(1)}, f32[7,24,128]{2,1,0:T(8,128)S(1)}, u32[]{:S(2)}, u32[]{:S(2)}) collective-permute-start(f32[7,24,128]{2,1,0:T(8,128)S(1)} %get-tuple-element.27), channel_id=1, source_target_pairs={{0,3},{1,2},{2,1},{3,0},{4,7},{5,6},{6,5},{7,4},{8,11},{9,10},{10,... | collective-permute-start | bytes 258056 | tf_op jit(solution)/shard_map/ppermute | solution.py:390
  14.9 0.1 collective-permute-start.5
  15.1 1.4 %inner.1 = (f32[13,4,5,8,128]{4,3,2,1,0:T(8,128)S(1)}, f32[6,4,5,8,128]{4,3,2,1,0:T(8,128)S(1)}, f32[2,128]{1,0:T(2,128)S(1)}) custom-call(f32[7,4,40,128]{3,2,1,0:T(8,128)S(1)} %get-tuple-element.23.ext), custom_call_target="tpu_custom_call" | custom-call | flops 2000000000 | bytes 6000000 | tf_op jit(solution)/shard_map/inner/pallas_call | solution.py:475
  16.5 0.0 collective-permute-done.8
  16.5 2.6 %collective-permute-start.9 = (f32[2,128]{1,0:T(2,128)S(1)}, f32[2,128]{1,0:T(2,128)S(1)}, u32[]{:S(2)}, u32[]{:S(2)}) collective-permute-start(f32[2,128]{1,0:T(2,128)S(1)} %maximum_maximum_fusion.1), channel_id=1, source_target_pairs={{0,17},{1,16},{2,19},{3,18},{4,21},{5,20},{6,23},{7,22},{8,25},{9,... | collective-permute-start | bytes 3080 | tf_op jit(solution)/shard_map/ppermute | solution.py:390
  19.2 0.0 collective-permute-done.6.rec_slab
  19.2 0.0 collective-permute-done.7.rec_b
  19.2 1.1 %outer.1 = (f32[6,4,5,8,128]{4,3,2,1,0:T(8,128)S(1)}, f32[7,2,5,8,128]{4,3,2,1,0:T(8,128)S(1)}, f32[6,2,5,8,128]{4,3,2,1,0:T(8,128)S(1)}, f32[2,128]{1,0:T(2,128)S(1)}) custom-call(f32[13,4,5,8,128]{4,3,2,1,0:T(8,128)S(1)} %get-tuple-element.24.q.base, f32[6,4,5,8,128]{4,3,2,1,0:T(8,128)S(1)} %get-tuple-element.25.inner, ...), custom_call_target="tpu_custom_call" | custom-call | flops 2000000000 | bytes 6000000 | tf_op jit(solution)/shard_map/outer/pallas_call | solution.py:481
  20.2 0.3 %collective-permute-done.9 = f32[2,128]{1,0:T(2,128)S(1)} collective-permute-done((f32[2,128]{1,0:T(2,128)S(1)}, f32[2,128]{1,0:T(2,128)S(1)}, u32[]{:S(2)}, u32[]{:S(2)}) %collective-permute-start.9) | collective-permute-done | bytes 1056 | tf_op jit(solution)/shard_map/ppermute | solution.py:390
  20.5 2.3 %second_section.1 = f32[6,128,128]{2,1,0:T(8,128)} custom-call(f32[13,4,5,8,128]{4,3,2,1,0:T(8,128)S(1)} %get-tuple-element.24.q.base, f32[6,4,5,8,128]{4,3,2,1,0:T(8,128)S(1)} %get-tuple-element.28.total, f32[7,2,5,8,128]{4,3,2,1,0:T(8,128)S(1)} %get-tuple-element.29.edge_q, f32[6,2,5,8,128]{4,3,2,1,0:T(8,128)S(1)} %get-tuple-element.30.edge_total, ...), custom_call_target="tpu_custom_call" | custom-call | tf_op jit(solution)/shard_map/second_section/pallas_call | solution.py:491
  (9 shorter events, 0.1 us)
Async XLA Ops:
  1.1 3.1 %collective-permute-start.1 = (f32[2,128]{1,0:T(2,128)S(1)}, f32[2,128]{1,0:T(2,128)S(1)}, u32[]{:S(2)}, u32[]{:S(2)}) collective-permute-start(f32[2,128]{1,0:T(2,128)S(1)} %get-tuple-element.22.order), channel_id=1, source_target_pairs={{0,1},{1,0},{2,3},{3,2},{4,5},{5,4},{6,7},{7,6},{8,9},{9,8},{10,11... | collective-permute-start | bytes 3080 | tf_op jit(solution)/shard_map/ppermute | solution.py:390
  1.6 10.1 %collective-permute-start = (f32[7,40,128]{2,1,0:T(8,128)S(1)}, f32[7,40,128]{2,1,0:T(8,128)S(1)}, u32[]{:S(2)}, u32[]{:S(2)}) collective-permute-start(f32[7,40,128]{2,1,0:T(8,128)S(1)} %upper.1), channel_id=1, source_target_pairs={{0,4},{1,5},{2,6},{3,7},{4,0},{5,1},{6,2},{7,3},{8,12},{9,13},{10,... | collective-permute-start | bytes 430088 | tf_op jit(solution)/shard_map/ppermute | solution.py:390
  4.2 7.4 %collective-permute-start.2 = (f32[7,40,128]{2,1,0:T(8,128)S(1)}, f32[7,40,128]{2,1,0:T(8,128)S(1)}, u32[]{:S(2)}, u32[]{:S(2)}) collective-permute-start(f32[7,40,128]{2,1,0:T(8,128)S(1)} %lower.1), channel_id=1, source_target_pairs={{0,1},{1,0},{2,3},{3,2},{4,8},{5,9},{6,10},{7,11},{8,4},{9,5},{10,... | collective-permute-start | bytes 430088 | tf_op jit(solution)/shard_map/ppermute | solution.py:390
  4.5 3.0 %collective-permute-start.3 = (f32[2,128]{1,0:T(2,128)S(1)}, f32[2,128]{1,0:T(2,128)S(1)}, u32[]{:S(2)}, u32[]{:S(2)}) collective-permute-start(f32[2,128]{1,0:T(2,128)S(1)} %max.21.order), channel_id=1, source_target_pairs={{0,3},{1,2},{2,1},{3,0},{4,7},{5,6},{6,5},{7,4},{8,11},{9,10},{10,... | collective-permute-start | bytes 3080 | tf_op jit(solution)/shard_map/ppermute | solution.py:390
  7.5 4.1 %collective-permute-start.4 = (f32[2,128]{1,0:T(2,128)S(1)}, f32[2,128]{1,0:T(2,128)S(1)}, u32[]{:S(2)}, u32[]{:S(2)}) collective-permute-start(f32[2,128]{1,0:T(2,128)S(1)} %max.22.order), channel_id=1, source_target_pairs={{0,5},{1,4},{2,7},{3,6},{4,1},{5,0},{6,3},{7,2},{8,13},{9,12},{10,... | collective-permute-start | bytes 3080 | tf_op jit(solution)/shard_map/ppermute | solution.py:390
  10.2 9.0 %collective-permute-start.6 = (f32[7,48,128]{2,1,0:T(8,128)S(1)}, f32[7,48,128]{2,1,0:T(8,128)S(1)}, u32[]{:S(2)}, u32[]{:S(2)}) collective-permute-start(f32[7,48,128]{2,1,0:T(8,128)S(1)} %slab.1), channel_id=1, source_target_pairs={{0,3},{1,2},{2,1},{3,0},{4,7},{5,6},{6,5},{7,4},{8,11},{9,10},{10,... | collective-permute-start | bytes 516104 | tf_op jit(solution)/shard_map/ppermute | solution.py:390
  11.8 4.7 %collective-permute-start.8 = (f32[2,128]{1,0:T(2,128)S(1)}, f32[2,128]{1,0:T(2,128)S(1)}, u32[]{:S(2)}, u32[]{:S(2)}) collective-permute-start(f32[2,128]{1,0:T(2,128)S(1)} %get-tuple-element.32), channel_id=1, source_target_pairs={{0,9},{1,8},{2,11},{3,10},{4,13},{5,12},{6,15},{7,14},{8,1},{9,0},... | collective-permute-start | bytes 3080 | tf_op jit(solution)/shard_map/ppermute | solution.py:390
  13.4 5.7 %collective-permute-start.7 = (f32[7,24,128]{2,1,0:T(8,128)S(1)}, f32[7,24,128]{2,1,0:T(8,128)S(1)}, u32[]{:S(2)}, u32[]{:S(2)}) collective-permute-start(f32[7,24,128]{2,1,0:T(8,128)S(1)} %get-tuple-element.27), channel_id=1, source_target_pairs={{0,3},{1,2},{2,1},{3,0},{4,7},{5,6},{6,5},{7,4},{8,11},{9,10},{10,... | collective-permute-start | bytes 258056 | tf_op jit(solution)/shard_map/ppermute | solution.py:390
  14.9 4.2 %collective-permute-start.5 = (f32[7,72,128]{2,1,0:T(8,128)S(1)}, f32[7,72,128]{2,1,0:T(8,128)S(1)}, u32[]{:S(2)}, u32[]{:S(2)}) collective-permute-start(f32[7,72,128]{2,1,0:T(8,128)S(1)} %get-tuple-element.26), channel_id=1, source_target_pairs={{0,1},{1,0},{2,3},{3,2},{4,5},{5,4},{6,7},{7,6},{8,9},{9,8},{10,11... | collective-permute-start | bytes 774152 | tf_op jit(solution)/shard_map/ppermute | solution.py:390
  16.5 4.0 %collective-permute-start.9 = (f32[2,128]{1,0:T(2,128)S(1)}, f32[2,128]{1,0:T(2,128)S(1)}, u32[]{:S(2)}, u32[]{:S(2)}) collective-permute-start(f32[2,128]{1,0:T(2,128)S(1)} %maximum_maximum_fusion.1), channel_id=1, source_target_pairs={{0,17},{1,16},{2,19},{3,18},{4,21},{5,20},{6,23},{7,22},{8,25},{9,... | collective-permute-start | bytes 3080 | tf_op jit(solution)/shard_map/ppermute | solution.py:390

commit v5 on v4

--- a/solution.py
+++ b/solution.py
@@ -12,8 +12,7 @@
 PLANES = LANES // BW
 GAMMA = 1.4
 COURANT = 0.8
-DEP_C, DEP_D, DEP_B, DEP_S, DEP_I = 0, 1, 2, 3, 3
-COST = {"slab": 0, "spread": 0, "inner": 2, "outer": 2}
+COST = {"slab": 0, "spread": 1, "inner": 20, "outer": 20}
 NQ = 13
 VX, PR, SND, TMP, KAP = 6, 9, 10, 11, 12
 VMEM = pl.BlockSpec(memory_space=pltpu.VMEM)
@@ -50,13 +49,14 @@
         s = jnp.abs(own[1, r, :]) + jnp.abs(own[2, r, :]) + jnp.abs(own[3, r, :]) + 3.0 * sound
         speed = s if speed is None else jnp.maximum(speed, s)
         top = own[6, r, :] if top is None else jnp.maximum(top, own[6, r, :])
-    peak[0:1, :] = jnp.max(speed, axis=0, keepdims=True)
-    peak[1:2, :] = jnp.max(top, axis=0, keepdims=True)
+    speed, top = jnp.max(speed, axis=0, keepdims=True), jnp.max(top, axis=0, keepdims=True)
+    halves = [jnp.maximum(v, pltpu.roll(v, LANES // 2, 1)) for v in (speed, top)]
+    peak[...] = jnp.where(lanes_of((1, LANES)) < LANES // 2, *halves)
     leaves = (owner[0] != lax.axis_index("curve")).astype(jnp.float32)
     leaving[...] = jnp.full(leaving.shape, leaves, jnp.float32)
 
 
-def side_kernel(upper_when_even, own, leaving, order, msg):
+def side_kernel(upper_when_even, own, leaving, msg):
     even = lax.axis_index("curve") % 2 == 0
     box = jnp.logical_not(even) if upper_when_even else even
     total = own.shape[1]
@@ -70,7 +70,8 @@
         msg[f, 36:40, :] = leaving[0:4, :]
 
 
-def slab_kernel(own, order, msg):
+def slab_kernel(own, peak, msg, peaks):
+    peaks[...] = jnp.broadcast_to(peak[...][None], peaks.shape)
     up = lax.axis_index("near") % 2 == 1
     groups = own.shape[1] // 32
     for f in range(7):
@@ -83,7 +84,7 @@
             msg[f, at : at + 8, :] = value
 
 
-def spread_kernel(own, rec_c, rec_d, peak, ext, msg_a, msg_b, arrival, peak_out):
+def spread_kernel(own, rec_c, rec_d, ext, msg_a, msg_b, arrival):
     segment, segments = lax.axis_index("curve"), lax.axis_size("curve")
     first, last = segment == 0, segment == segments - 1
     odd = segment % 2 == 1
@@ -92,7 +93,6 @@
     shape = (8, LANES)
     lane, row = lanes_of(shape), rows_of(shape)
     spread = lambda x: jnp.broadcast_to(x, shape)
-    peak_out[...] = peak[...]
     arrival[...] = jnp.where(last, 0.0, spread(jnp.where(odd, rec_d[0, 36:37, :], rec_c[0, 36:37, :])))
     for f in range(7):
         out = []
@@ -225,9 +225,7 @@
             ref[(i,) + at + (j,)] = value
 
 
-def inner_kernel(ext, q, total, token):
-    token[...] = jnp.zeros(token.shape, jnp.float32)
-
+def inner_kernel(ext, order, q, total):
     @pl.loop(0, 4, unroll=True)
     def _(z):
         found = []
@@ -253,7 +251,7 @@
             total[f, z + 1, j] = value
 
 
-def outer_kernel(q, inner, rec_a, rec_slab, rec_b, total, edge_q, edge_total, token, rim, joined):
+def outer_kernel(q, inner, rec_a, rec_slab, rec_b, total, edge_q, edge_total, rim, joined):
     even = lax.axis_index("near") % 2 == 0
     shape = (8, LANES)
     row = rows_of(shape)
@@ -265,7 +263,6 @@
             for j in range(5):
                 total[f, z, j] = inner[f, z, j]
 
-    token[...] = jnp.zeros(token.shape, jnp.float32)
     slab, pitch = rec_slab.shape[1] // 2, rec_a.shape[1] // 2
     for f in range(7):
         for z in range(2):
@@ -323,7 +320,9 @@
     first, last = segment == 0, segment == segments - 1
     fetch = pltpu.make_async_copy(new_owner, owner, sems.at[0])
     fetch.start()
-    speed, top = jnp.max(peak[0:1, :]), jnp.max(peak[1:2, :])
+    peaks = jnp.max(peak[...], axis=0)
+    half_lanes = lanes_of((1, LANES)) < LANES // 2
+    speed, top = jnp.max(jnp.where(half_lanes, peaks, 0.0)), jnp.max(jnp.where(half_lanes, 0.0, peaks))
     step = COURANT / (speed + 6.0 * top)
 
     def half_row(state, divergence, kap_at, source, target):
@@ -390,26 +389,6 @@
     return lax.ppermute(x, ("curve", "near"), route)
 
 
-def near_routes(n):
-    routes = [lambda c, i: (c, i ^ 1), lambda c, i: (c, outer_partner(i, n))]
-    reach = 4
-    while reach < n:
-        routes.append(lambda c, i, d=reach: (c, (i + d) % n))
-        reach *= 2
-    return routes
-
-
-def curve_routes(m):
-    routes, reach = [], 1
-    while reach < m:
-        if m % (2 * reach) == 0:
-            routes.append(lambda c, i, d=reach: (c ^ d, i ^ 1))
-        else:
-            routes.append(lambda c, i, d=reach: ((c + d) % m, i ^ 1))
-        reach *= 2
-    return routes
-
-
 def outer_partner(i, n):
     return ((i + 1) ^ 1) - 1 if 0 < i < n - 1 else n - 1 - i
 
@@ -445,48 +424,38 @@
         load_kernel,
         "load",
         [hbm, hbm, hbm],
-        (f32(7, rows, LANES), f32(2, LANES), f32(8, LANES)),
+        (f32(7, rows, LANES), f32(1, LANES), f32(8, LANES)),
         [pltpu.SMEM(new_owner.shape, jnp.int32), pltpu.SemaphoreType.DMA((3,))],
     )(prim, kappa, new_owner)
 
-    side = lambda upper, name: kernel(functools.partial(side_kernel, upper), name, [VMEM] * 3, f32(7, 40, LANES))
+    side = lambda upper, name: kernel(functools.partial(side_kernel, upper), name, [VMEM] * 2, f32(7, 40, LANES))
     quantities, sums = f32(NQ, 4, 5, 8, LANES), f32(6, 4, 5, 8, LANES)
-    routes = near_routes(n) + curve_routes(m)
-    token = None
-    for stage, route in enumerate(routes):
-        if stage == DEP_C:
-            rec_c = swap(side(True, "upper")(own, leaving, peak), lambda c, i: (c ^ 1, i))
-        if stage == DEP_D:
-            msg_d = side(False, "lower")(own, leaving, peak)
-            rec_d = swap(msg_d, lambda c, i: (c, i ^ 1) if c in (0, m - 1) else (outer_partner(c, m), i))
-        if stage == DEP_B:
-            slab = kernel(slab_kernel, "slab", [VMEM] * 2, f32(7, rows // 2, LANES), us=COST["slab"])(own, peak)
-            rec_slab = swap(slab, lambda c, i: (c, outer_partner(i, n)))
-        if stage == DEP_S:
-            ext, msg_a, msg_b, arrival, peak = kernel(
-                spread_kernel,
-                "spread",
-                [VMEM] * 4,
-                (f32(7, 4, 40, LANES), f32(7, 72, LANES), f32(7, 24, LANES), f32(8, LANES), f32(2, LANES)),
-                us=COST["spread"],
-            )(own, rec_c, rec_d, peak)
-            rec_a = swap(msg_a, lambda c, i: (c, i ^ 1))
-            rec_b = swap(msg_b, lambda c, i: (c, outer_partner(i, n)))
-            q, inner, token = kernel(
-                inner_kernel, "inner", [VMEM], (quantities, sums, f32(2, LANES)), us=COST["inner"]
-            )(ext)
-        peak = jnp.maximum(peak, swap(peak, route))
-        if stage == DEP_I:
-            peak = jnp.maximum(peak, token)
-    total, edge_q, edge_total, token = kernel(
+    rec_c = swap(side(True, "upper")(own, leaving), lambda c, i: (c ^ 1, i))
+    msg_d = side(False, "lower")(own, leaving)
+    rec_d = swap(msg_d, lambda c, i: (c, i ^ 1) if c in (0, m - 1) else (outer_partner(c, m), i))
+    slab, peak = kernel(
+        slab_kernel, "slab", [VMEM] * 2, (f32(7, rows // 2, LANES), f32(m * n, 1, LANES)), us=COST["slab"]
+    )(own, peak)
+    rec_slab = swap(slab, lambda c, i: (c, outer_partner(i, n)))
+    peak = lax.all_to_all(peak, ("curve", "near"), 0, 0, tiled=True)
+    ext, msg_a, msg_b, arrival = kernel(
+        spread_kernel,
+        "spread",
+        [VMEM] * 3,
+        (f32(7, 4, 40, LANES), f32(7, 72, LANES), f32(7, 24, LANES), f32(8, LANES)),
+        us=COST["spread"],
+    )(own, rec_c, rec_d)
+    rec_a = swap(msg_a, lambda c, i: (c, i ^ 1))
+    rec_b = swap(msg_b, lambda c, i: (c, outer_partner(i, n)))
+    q, inner = kernel(inner_kernel, "inner", [VMEM] * 2, (quantities, sums), us=COST["inner"])(ext, rec_slab)
+    total, edge_q, edge_total = kernel(
         outer_kernel,
         "outer",
         [VMEM] * 5,
-        (sums, f32(7, 2, 5, 8, LANES), f32(6, 2, 5, 8, LANES), f32(2, LANES)),
+        (sums, f32(7, 2, 5, 8, LANES), f32(6, 2, 5, 8, LANES)),
         [pltpu.VMEM((NQ, 6, 5, 8, LANES), jnp.float32), pltpu.VMEM((7, 72, LANES), jnp.float32)],
         us=COST["outer"],
     )(q, inner, rec_a, rec_slab, rec_b)
-    peak = jnp.maximum(peak, token)
 
     out = pl.pallas_call(
         second_kernel,

time: 22.9 us -> 21.1 us (0.921)
  starting transfers between devices: 14.8 us -> 11.7 us
  waiting for transfers between devices: 1.9 us -> 2.56 us
  Pallas kernels: 6.02 us -> 6.6 us
    ppermute x10 -> x5, starting transfers between devices: 14.8 us -> 6.64 us  [swap(): return lax.ppermute(x, ('curve', 'near'), route)]
    all_to_all x0 -> x1, starting transfers between devices: none -> 5.03 us  [local(): peak = lax.all_to_all(peak, ('curve', 'near'), 0, 0, tiled=True)]
    all_to_all x0 -> x1, waiting for transfers between devices: none -> 1.22 us  [local(): peak = lax.all_to_all(peak, ('curve', 'near'), 0, 0, tiled=True)]
    pallas_call x6, Pallas kernels: 2.7 us -> 3.31 us  [the longest x1 1.37 us: local(): kernel(inner_kernel, 'inner', [VMEM] * 2, (quantities, sums), us=COST['in...]
    ppermute x10 -> x5, waiting for transfers between devices: 1.9 us -> 1.34 us  [swap(): return lax.ppermute(x, ('curve', 'near'), route)]
  transfers between devices with their start and end apart: 10 -> 6, of which waited for: 2 -> 2; matrix products, arithmetic and copies ran while one was open for 0% -> 0% of each run, Pallas kernels for 12% -> 15%
where the time goes in v5:
time: 21.1 us; the launch traced here: 20.9 us
  starting transfers between devices  11.7 us (55%)
  Pallas kernels  6.6 us (31%)
  waiting for transfers between devices  2.56 us (12%)
    ppermute x5, starting transfers between devices, swap(): return lax.ppermute(x, ('curve', 'near'), route)  6.64 us
    all_to_all x1, starting transfers between devices, local(): peak = lax.all_to_all(peak, ('curve', 'near'), 0, 0, tiled=True)  5.03 us
    pallas_call x1, Pallas kernels, local(): pl.pallas_call(second_kernel, out_shape=f32(6, rows + 32, LANES), in_spec...  2.27 us
    pallas_call x1, Pallas kernels, local(): kernel(inner_kernel, 'inner', [VMEM] * 2, (quantities, sums), us=COST['in...  1.37 us
    ppermute x5, waiting for transfers between devices, swap(): return lax.ppermute(x, ('curve', 'near'), route)  1.34 us
    all_to_all x1, waiting for transfers between devices, local(): peak = lax.all_to_all(peak, ('curve', 'near'), 0, 0, tiled=True)  1.22 us
    pallas_call x1, Pallas kernels, local(): kernel(load_kernel, 'load', [hbm, hbm, hbm], (f32(7, rows, LANES), f32(1,...  1.12 us
    pallas_call x1, Pallas kernels, local(): kernel(outer_kernel, 'outer', [VMEM] * 5, (sums, f32(7, 2, 5, 8, LANES),...  1.03 us
  transfers between devices with their start and end apart: 6, of which 2 were waited for; matrix products, arithmetic and copies ran while one was open for 0% of the time, Pallas kernels for 15%

profile of v5, /device:TPU:0, one launch (start us, length us, event | category | flops | bytes accessed | tf_op | source)
XLA Modules:
  0.0 20.9 jit_solution(11427603183007458942)
XLA Ops:
  0.0 1.1 %load.1 = (f32[7,96,128]{2,1,0:T(8,128)S(1)}, f32[1,128]{1,0:T(1,128)S(1)}, f32[8,128]{1,0:T(8,128)S(1)}) custom-call(f32[6,96,128]{2,1,0:T(8,128)} %bitcast.15, f32[96,128]{1,0:T(8,128)} %bitcast.16, s32[3]{0:T(128)} %new_owner.3), custom_call_target="tpu_custom_call" | custom-call | tf_op jit(solution)/shard_map/load/pallas_call | solution.py:423
  1.2 3.0 %collective-permute-start = (f32[7,40,128]{2,1,0:T(8,128)S(1)}, f32[7,40,128]{2,1,0:T(8,128)S(1)}, u32[]{:S(2)}, u32[]{:S(2)}) collective-permute-start(f32[7,40,128]{2,1,0:T(8,128)S(1)} %upper.1), channel_id=1, source_target_pairs={{0,4},{1,5},{2,6},{3,7},{4,0},{5,1},{6,2},{7,3},{8,12},{9,13},{10,... | collective-permute-start | bytes 430088 | tf_op jit(solution)/shard_map/ppermute | solution.py:389
  4.2 0.1 collective-permute-start.1
  4.3 0.6 %slab.1 = (f32[7,48,128]{2,1,0:T(8,128)S(1)}, f32[32,1,128]{2,1,0:T(1,128)}) custom-call(f32[7,96,128]{2,1,0:T(8,128)S(1)} %get-tuple-element.19.own, f32[1,128]{1,0:T(1,128)S(1)} %get-tuple-element.22.peak), custom_call_target="tpu_custom_call" | custom-call | tf_op jit(solution)/shard_map/slab/pallas_call | solution.py:436
  4.9 1.6 %collective-permute-start.2 = (f32[7,48,128]{2,1,0:T(8,128)S(1)}, f32[7,48,128]{2,1,0:T(8,128)S(1)}, u32[]{:S(2)}, u32[]{:S(2)}) collective-permute-start(f32[7,48,128]{2,1,0:T(8,128)S(1)} %get-tuple-element.23), channel_id=1, source_target_pairs={{0,3},{1,2},{2,1},{3,0},{4,7},{5,6},{6,5},{7,4},{8,11},{9,10},{10,... | collective-permute-start | bytes 516104 | tf_op jit(solution)/shard_map/ppermute | solution.py:389
  6.5 5.0 %all-to-all-start = ((f32[32,1,128]{2,1,0:T(1,128)}), f32[32,1,128]{2,1,0:T(1,128)S(1)}, u32[]{:S(2)}, u32[]{:S(2)}) async-start(f32[32,1,128]{2,1,0:T(1,128)} %get-tuple-element.32), calls=%async_computation | async-start | bytes 32768 | tf_op jit(solution)/shard_map/all_to_all | solution.py:440
  11.6 0.0 collective-permute-done.rec_c
  11.6 0.0 collective-permute-done.1.rec_d
  11.6 0.1 spread.1
  11.7 1.6 %collective-permute-start.4 = (f32[7,24,128]{2,1,0:T(8,128)S(1)}, f32[7,24,128]{2,1,0:T(8,128)S(1)}, u32[]{:S(2)}, u32[]{:S(2)}) collective-permute-start(f32[7,24,128]{2,1,0:T(8,128)S(1)} %get-tuple-element.27), channel_id=1, source_target_pairs={{0,3},{1,2},{2,1},{3,0},{4,7},{5,6},{6,5},{7,4},{8,11},{9,10},{10,... | collective-permute-start | bytes 258056 | tf_op jit(solution)/shard_map/ppermute | solution.py:389
  13.3 0.4 %collective-permute-start.3 = (f32[7,72,128]{2,1,0:T(8,128)S(1)}, f32[7,72,128]{2,1,0:T(8,128)S(1)}, u32[]{:S(2)}, u32[]{:S(2)}) collective-permute-start(f32[7,72,128]{2,1,0:T(8,128)S(1)} %get-tuple-element.26), channel_id=1, source_target_pairs={{0,1},{1,0},{2,3},{3,2},{4,5},{5,4},{6,7},{7,6},{8,9},{9,8},{10,11... | collective-permute-start | bytes 774152 | tf_op jit(solution)/shard_map/ppermute | solution.py:389
  13.7 0.0 collective-permute-done.2.order.rec_slab
  13.7 1.4 %inner.1 = (f32[13,4,5,8,128]{4,3,2,1,0:T(8,128)S(1)}, f32[6,4,5,8,128]{4,3,2,1,0:T(8,128)S(1)}) custom-call(f32[7,4,40,128]{3,2,1,0:T(8,128)S(1)} %get-tuple-element.21.ext, f32[7,48,128]{2,1,0:T(8,128)S(1)} %collective-permute-done.2.order.rec_slab), custom_call_target="tpu_custom_call" | custom-call | flops 20000000000 | bytes 60000000 | tf_op jit(solution)/shard_map/inner/pallas_call | solution.py:450
  15.1 1.3 %collective-permute-done.4.rec_b = f32[7,24,128]{2,1,0:T(8,128)S(1)} collective-permute-done((f32[7,24,128]{2,1,0:T(8,128)S(1)}, f32[7,24,128]{2,1,0:T(8,128)S(1)}, u32[]{:S(2)}, u32[]{:S(2)}) %collective-permute-start.4) | collective-permute-done | bytes 86048 | tf_op jit(solution)/shard_map/ppermute | solution.py:389
  16.4 0.0 collective-permute-done.3.rec_a
  16.4 1.0 %outer.1 = (f32[6,4,5,8,128]{4,3,2,1,0:T(8,128)S(1)}, f32[7,2,5,8,128]{4,3,2,1,0:T(8,128)S(1)}, f32[6,2,5,8,128]{4,3,2,1,0:T(8,128)S(1)}) custom-call(f32[13,4,5,8,128]{4,3,2,1,0:T(8,128)S(1)} %get-tuple-element.24.q.base, f32[6,4,5,8,128]{4,3,2,1,0:T(8,128)S(1)} %get-tuple-element.25.inner, f32[7,72,128]{2,1,0:T(8,128)S(1)} %collective-permute-done.3.rec_a, ...), custom_call_target="tpu_custom_call" | custom-call | flops 20000000000 | bytes 60000000 | tf_op jit(solution)/shard_map/outer/pallas_call | solution.py:451
  17.4 1.2 %all-to-all-done.peak = f32[32,1,128]{2,1,0:T(1,128)S(1)} async-done(((f32[32,1,128]{2,1,0:T(1,128)}), f32[32,1,128]{2,1,0:T(1,128)S(1)}, u32[]{:S(2)}, u32[]{:S(2)}) %all-to-all-start) | async-done | bytes 16416 | tf_op jit(solution)/shard_map/all_to_all | solution.py:440
  18.6 2.3 %second_section.1 = f32[6,128,128]{2,1,0:T(8,128)} custom-call(f32[13,4,5,8,128]{4,3,2,1,0:T(8,128)S(1)} %get-tuple-element.24.q.base, f32[6,4,5,8,128]{4,3,2,1,0:T(8,128)S(1)} %get-tuple-element.28.total, f32[7,2,5,8,128]{4,3,2,1,0:T(8,128)S(1)} %get-tuple-element.29.edge_q, f32[6,2,5,8,128]{4,3,2,1,0:T(8,128)S(1)} %get-tuple-element.30.edge_total, ...), custom_call_target="tpu_custom_call" | custom-call | tf_op jit(solution)/shard_map/second_section/pallas_call | solution.py:460
  (2 shorter events, 0.1 us)
Async XLA Ops:
  1.2 10.4 %collective-permute-start = (f32[7,40,128]{2,1,0:T(8,128)S(1)}, f32[7,40,128]{2,1,0:T(8,128)S(1)}, u32[]{:S(2)}, u32[]{:S(2)}) collective-permute-start(f32[7,40,128]{2,1,0:T(8,128)S(1)} %upper.1), channel_id=1, source_target_pairs={{0,4},{1,5},{2,6},{3,7},{4,0},{5,1},{6,2},{7,3},{8,12},{9,13},{10,... | collective-permute-start | bytes 430088 | tf_op jit(solution)/shard_map/ppermute | solution.py:389
  4.2 7.4 %collective-permute-start.1 = (f32[7,40,128]{2,1,0:T(8,128)S(1)}, f32[7,40,128]{2,1,0:T(8,128)S(1)}, u32[]{:S(2)}, u32[]{:S(2)}) collective-permute-start(f32[7,40,128]{2,1,0:T(8,128)S(1)} %lower.1), channel_id=1, source_target_pairs={{0,1},{1,0},{2,3},{3,2},{4,8},{5,9},{6,10},{7,11},{8,4},{9,5},{10,... | collective-permute-start | bytes 430088 | tf_op jit(solution)/shard_map/ppermute | solution.py:389
  4.9 8.8 %collective-permute-start.2 = (f32[7,48,128]{2,1,0:T(8,128)S(1)}, f32[7,48,128]{2,1,0:T(8,128)S(1)}, u32[]{:S(2)}, u32[]{:S(2)}) collective-permute-start(f32[7,48,128]{2,1,0:T(8,128)S(1)} %get-tuple-element.23), channel_id=1, source_target_pairs={{0,3},{1,2},{2,1},{3,0},{4,7},{5,6},{6,5},{7,4},{8,11},{9,10},{10,... | collective-permute-start | bytes 516104 | tf_op jit(solution)/shard_map/ppermute | solution.py:389
  6.5 12.1 %all-to-all-start = ((f32[32,1,128]{2,1,0:T(1,128)}), f32[32,1,128]{2,1,0:T(1,128)S(1)}, u32[]{:S(2)}, u32[]{:S(2)}) async-start(f32[32,1,128]{2,1,0:T(1,128)} %get-tuple-element.32), calls=%async_computation | async-start | bytes 32768 | tf_op jit(solution)/shard_map/all_to_all | solution.py:440
  11.7 4.7 %collective-permute-start.4 = (f32[7,24,128]{2,1,0:T(8,128)S(1)}, f32[7,24,128]{2,1,0:T(8,128)S(1)}, u32[]{:S(2)}, u32[]{:S(2)}) collective-permute-start(f32[7,24,128]{2,1,0:T(8,128)S(1)} %get-tuple-element.27), channel_id=1, source_target_pairs={{0,3},{1,2},{2,1},{3,0},{4,7},{5,6},{6,5},{7,4},{8,11},{9,10},{10,... | collective-permute-start | bytes 258056 | tf_op jit(solution)/shard_map/ppermute | solution.py:389
  13.3 3.1 %collective-permute-start.3 = (f32[7,72,128]{2,1,0:T(8,128)S(1)}, f32[7,72,128]{2,1,0:T(8,128)S(1)}, u32[]{:S(2)}, u32[]{:S(2)}) collective-permute-start(f32[7,72,128]{2,1,0:T(8,128)S(1)} %get-tuple-element.26), channel_id=1, source_target_pairs={{0,1},{1,0},{2,3},{3,2},{4,5},{5,4},{6,7},{7,6},{8,9},{9,8},{10,11... | collective-permute-start | bytes 774152 | tf_op jit(solution)/shard_map/ppermute | solution.py:389

commit v6 on v5

--- a/solution.py
+++ b/solution.py
@@ -12,7 +12,7 @@
 PLANES = LANES // BW
 GAMMA = 1.4
 COURANT = 0.8
-COST = {"slab": 0, "spread": 1, "inner": 20, "outer": 20}
+COST = {"spread": 0.3, "inner": 20, "outer": 20}
 NQ = 13
 VX, PR, SND, TMP, KAP = 6, 9, 10, 11, 12
 VMEM = pl.BlockSpec(memory_space=pltpu.VMEM)
@@ -31,8 +31,11 @@
     return lax.broadcasted_iota(jnp.int32, shape, 0)
 
 
-def load_kernel(prim, kappa, new_owner, own, peak, leaving, owner, sems):
+def load_kernel(prim, kappa, new_owner, own, msg_c, msg_d, slab, peak, owner, sems):
+    segment = lax.axis_index("curve")
+    even, up = segment % 2 == 0, lax.axis_index("near") % 2 == 1
     total = own.shape[1]
+    groups = total // 32
     copies = [
         pltpu.make_async_copy(prim, own.at[pl.ds(0, 6)], sems.at[0]),
         pltpu.make_async_copy(kappa, own.at[6], sems.at[1]),
@@ -52,28 +55,22 @@
     speed, top = jnp.max(speed, axis=0, keepdims=True), jnp.max(top, axis=0, keepdims=True)
     halves = [jnp.maximum(v, pltpu.roll(v, LANES // 2, 1)) for v in (speed, top)]
     peak[...] = jnp.where(lanes_of((1, LANES)) < LANES // 2, *halves)
-    leaves = (owner[0] != lax.axis_index("curve")).astype(jnp.float32)
-    leaving[...] = jnp.full(leaving.shape, leaves, jnp.float32)
-
-
-def side_kernel(upper_when_even, own, leaving, msg):
-    even = lax.axis_index("curve") % 2 == 0
-    box = jnp.logical_not(even) if upper_when_even else even
-    total = own.shape[1]
-    for g in range(5):
-        length = 8 if g < 4 else 4
-        first, last = pl.ds(8 * g, length), pl.ds(total - 36 + 8 * g, length)
-        parts = [jnp.where(box, own[f, first, :], own[f, last, :]) for f in range(7)]
+    leaves = jnp.full((2, LANES), (owner[0] != segment).astype(jnp.float32), jnp.float32)
+    low_half = lanes_of((1, LANES)) < LANES // 2
+    swapped = lambda x: pltpu.roll(x, LANES // 2, 1)
+    for msg, box in ((msg_c, jnp.logical_not(even)), (msg_d, even)):
         for f in range(7):
-            msg[f, first, :] = parts[f]
-    for f in range(7):
-        msg[f, 36:40, :] = leaving[0:4, :]
-
-
-def slab_kernel(own, peak, msg, peaks):
-    peaks[...] = jnp.broadcast_to(peak[...][None], peaks.shape)
-    up = lax.axis_index("near") % 2 == 1
-    groups = own.shape[1] // 32
+            parts = [own[f, 8 * g : 8 * g + 8, :] for g in range(4)]
+            for z in (0, 2):
+                first, second = (own[f, k : k + 1, :] for k in (32 + z, 33 + z))
+                ahead = jnp.where(low_half, first, swapped(second))
+                first, second = (own[f, k : k + 1, :] for k in (total - 4 + z, total - 3 + z))
+                parts.append(jnp.where(box, ahead, jnp.where(low_half, swapped(first), second)))
+            at = 34 * f
+            for part in parts:
+                msg[at : at + part.shape[0], :] = part
+                at += part.shape[0]
+        msg[238:240, :] = leaves
     for f in range(7):
         parts = {}
         for z in range(2):
@@ -81,7 +78,11 @@
                 upper, lower = (own[f, pl.ds(k + 32 * g, 8, stride=4), :] for k in (z + 2, z))
                 parts[8 * (groups * z + g)] = jnp.where(up, upper, lower)
         for at, value in parts.items():
-            msg[f, at : at + 8, :] = value
+            slab[f, at : at + 8, :] = value
+
+
+def copies_kernel(peak, peaks):
+    peaks[...] = jnp.broadcast_to(peak[...][None], peaks.shape)
 
 
 def spread_kernel(own, rec_c, rec_d, ext, msg_a, msg_b, arrival):
@@ -93,15 +94,21 @@
     shape = (8, LANES)
     lane, row = lanes_of(shape), rows_of(shape)
     spread = lambda x: jnp.broadcast_to(x, shape)
-    arrival[...] = jnp.where(last, 0.0, spread(jnp.where(odd, rec_d[0, 36:37, :], rec_c[0, 36:37, :])))
+    arrival[...] = jnp.where(last, 0.0, spread(jnp.where(odd, rec_d[238:239, :], rec_c[238:239, :])))
     for f in range(7):
         out = []
         for z in range(4):
             cells = [own[f, pl.ds(z + 32 * g, 8, stride=4), :] for g in range(groups)]
-            at = pl.ds(z, 8, stride=4)
-            box = jnp.where(odd, rec_d[f, at, :], rec_c[f, at, :])
-            beyond = spread(jnp.where(odd, rec_d[f, 32 + z : 33 + z, :], rec_c[f, 32 + z : 33 + z, :]))
-            behind = spread(jnp.where(odd, rec_c[f, 32 + z : 33 + z, :], rec_d[f, 32 + z : 33 + z, :]))
+            at = pl.ds(34 * f + z, 8, stride=4)
+            box = jnp.where(odd, rec_d[at, :], rec_c[at, :])
+            at = pl.ds(34 * f + 32 + z // 2, 1)
+            beyond = jnp.where(odd, rec_d[at, :], rec_c[at, :])
+            behind = jnp.where(odd, rec_c[at, :], rec_d[at, :])
+            if z % 2:
+                beyond = pltpu.roll(beyond, LANES // 2, 1)
+            else:
+                behind = pltpu.roll(behind, LANES // 2, 1)
+            beyond, behind = spread(beyond), spread(behind)
             edge = pltpu.roll(spread(cells[-1][7:8]), BW, 1)
             box = jnp.where(last, edge, box)
             start, end = spread(cells[0][0:1]), spread(box[7:8])
@@ -112,16 +119,21 @@
         for z in range(4):
             for g, value in enumerate(out[z]):
                 ext[f, z, 8 * g : 8 * g + 8, :] = value
-        for msg, ahead, pitch, begin in ((msg_a, up, 36, 0), (msg_b, jnp.logical_not(up), 12, groups)):
-            for z in range(2):
-                for g in range(begin, groups + 2):
-                    value = jnp.where(ahead, out[z + 2][g], out[z][g])
-                    at = pitch * z + 8 * (g - begin)
-                    if g < groups + 1:
-                        msg[f, at : at + 8, :] = value
-                    else:
-                        msg[f, at : at + 1, :] = value[0:1]
-                        msg[f, at + 1 : at + 2, :] = value[7:8]
+        for z in range(2):
+            for g in range(groups + 2):
+                value = jnp.where(up, out[z + 2][g], out[z][g])
+                at = 36 * z + 8 * g
+                if g < groups + 1:
+                    msg_a[f, at : at + 8, :] = value
+                else:
+                    msg_a[f, at : at + 1, :] = value[0:1]
+                    msg_a[f, at + 1 : at + 2, :] = value[7:8]
+            at = 18 * f + 8 * z
+            msg_b[at : at + 8, :] = jnp.where(up, out[z][groups], out[z + 2][groups])
+        value = jnp.where(up, out[0][groups + 1], out[3][groups + 1])
+        msg_b[18 * f + 16 : 18 * f + 17, :] = value[0:1]
+        msg_b[18 * f + 17 : 18 * f + 18, :] = value[7:8]
+    msg_b[126:128, :] = jnp.zeros((2, LANES), jnp.float32)
 
 
 def up_x(q, lane):
@@ -219,6 +231,14 @@
     return (r, r * vx, r * vy, r * vz, energy, r * s, vx, vy, vz, p, jnp.sqrt(GAMMA * t), t, k)
 
 
+def state_quantities(r, mx, my, mz, e, s, k):
+    inv = 1.0 / r
+    vx, vy, vz = mx * inv, my * inv, mz * inv
+    p = (GAMMA - 1.0) * (e - 0.5 * (mx * vx + my * vy + mz * vz))
+    t = p * inv
+    return (r, mx, my, mz, e, s, vx, vy, vz, p, jnp.sqrt(GAMMA * t), t, k)
+
+
 def store_all(ref, at, values):
     for j, quantities in enumerate(values):
         for i, value in enumerate(quantities):
@@ -251,69 +271,55 @@
             total[f, z + 1, j] = value
 
 
-def outer_kernel(q, inner, rec_a, rec_slab, rec_b, total, edge_q, edge_total, rim, joined):
+def rim_kernel(with_a, q, inner, *refs):
+    *received, edge_q, edge_total, own_total, rim = refs[:-1] if not with_a else refs
     even = lax.axis_index("near") % 2 == 0
-    shape = (8, LANES)
-    row = rows_of(shape)
-    spread = lambda x: jnp.broadcast_to(x, shape)
-
-    @pl.loop(0, 4, unroll=True)
-    def _(z):
-        for f in range(6):
-            for j in range(5):
-                total[f, z, j] = inner[f, z, j]
-
-    slab, pitch = rec_slab.shape[1] // 2, rec_a.shape[1] // 2
-    for f in range(7):
-        for z in range(2):
-            at, to = 12 * z, pitch * z
-            joined[f, to : to + slab, :] = rec_slab[f, slab * z : slab * z + slab, :]
-            joined[f, to + slab : to + slab + 10, :] = rec_b[f, at : at + 10, :]
-    for i in range(NQ):
+    above_own = even if with_a else jnp.logical_not(even)
+    start, own = jnp.where(above_own, 1, 0), jnp.where(above_own, 3, 0)
+    row = rows_of((8, LANES))
+    spread = lambda x: jnp.broadcast_to(x, (8, LANES))
+    if with_a:
+        (rows,) = received
+    else:
+        rows, (rec_slab, rec_box) = refs[-1], received
+        slab = rec_slab.shape[1] // 2
+        for f in range(7):
+            for z in range(2):
+                at, box = 36 * z, 18 * f + 8 * z
+                rows[f, at : at + slab, :] = rec_slab[f, slab * z : slab * z + slab, :]
+                rows[f, at + slab : at + slab + 8, :] = rec_box[box : box + 8, :]
+                rows[f, at + slab + 8 : at + slab + 10, :] = rec_box[18 * f + 16 : 18 * f + 18, :]
+    kept = [[q[i, own, j] for i in range(NQ)] for j in range(5)]
+    store_all(rim, (jnp.where(above_own, 0, 2),), kept)
+    for z in range(2):
+        found = []
         for j in range(5):
-            rim[i, 2, j] = q[i, 0, j]
-            rim[i, 3, j] = q[i, 3, j]
-    for rec, base in ((rec_a, jnp.where(even, 4, 0)), (joined, jnp.where(even, 0, 4))):
-
-        @pl.loop(0, 2, unroll=True)
-        def _(z):
-            found = []
-            for j in range(5):
-                if j < 4:
-                    cells = (rec[f, pl.ds(36 * z + j, 8, stride=4), :] for f in range(7))
-                else:
-                    cells = (
-                        jnp.where(row == 7, spread(rec[f, pl.ds(36 * z + 33, 1), :]), spread(rec[f, pl.ds(36 * z + 32, 1), :]))
-                        for f in range(7)
-                    )
-                found.append(raw_quantities(*cells))
-            store_all(rim, (base + z,), found)
-
-    @pl.loop(0, 2, unroll=True)
-    def _(e):
-        z = 1 + 3 * e
-        values = plane_divergence(rim, z, 5)
-        for (f, j), value in values.items():
-            edge_total[f, e, j] = value
-        for j in range(5):
-            for i, k in enumerate((0, 1, 2, 3, 4, 5, KAP)):
-                edge_q[i, e, j] = rim[k, z, j]
-
-    @pl.loop(0, 2, unroll=True)
-    def _(e):
-        below = z_face_row(rim, 3 * e, 5)
-        above = z_face_row(rim, 3 * e + 1, 5)
-        own = 3 * e
-        change = {key: jnp.where(e == 0, -above[key], below[key]) for key in above}
-        edge = {(f, j): edge_total[f, e, j] + (above[f, j] - below[f, j]) for f, j in above}
-        done = {(f, j): inner[f, own, j] + value for (f, j), value in change.items()}
-        for (f, j), value in edge.items():
-            edge_total[f, e, j] = value
-        for (f, j), value in done.items():
-            total[f, own, j] = value
-
-
-def second_kernel(base, total, edge_q, edge_total, arrival, peak, new_owner, out, q, zf, final, owner, sems):
+            if j < 4:
+                cells = (rows[f, pl.ds(36 * z + j, 8, stride=4), :] for f in range(7))
+            else:
+                at = 36 * z + 32
+                cells = (
+                    jnp.where(row == 7, spread(rows[f, at + 1 : at + 2, :]), spread(rows[f, at : at + 1, :]))
+                    for f in range(7)
+                )
+            found.append(raw_quantities(*cells))
+        store_all(rim, (start + z,), found)
+    plane = plane_divergence(rim, 1, 4)
+    below, above = z_face_row(rim, 0, 5), z_face_row(rim, 1, 5)
+    change = {key: jnp.where(above_own, below[key], -above[key]) for key in above}
+    done = {(f, j): inner[f, own, j] + value for (f, j), value in change.items()}
+    for (f, j), value in plane.items():
+        edge_total[f, j] = value + (above[f, j] - below[f, j])
+    for (f, j), value in done.items():
+        own_total[f, j] = value
+    for j in range(4):
+        for i, k in enumerate((0, 1, 2, 3, 4, 5, KAP)):
+            edge_q[i, j] = rim[k, 1, j]
+
+
+def second_kernel(
+    base, total, edge_a, change_a, own_a, edge_b, change_b, own_b, arrival, peak, new_owner, out, q, zf, final, owner, sems
+):
     segment, segments = lax.axis_index("curve"), lax.axis_size("curve")
     shape = (8, LANES)
     lane, row = lanes_of(shape), rows_of(shape)
@@ -325,34 +331,32 @@
     speed, top = jnp.max(jnp.where(half_lanes, peaks, 0.0)), jnp.max(jnp.where(half_lanes, 0.0, peaks))
     step = COURANT / (speed + 6.0 * top)
 
-    def half_row(state, divergence, kap_at, source, target):
-        half = [
-            [state[f, source, j] - (0.5 * step) * divergence[f, source, j] for j in range(5)] for f in range(6)
-        ]
-        kap = [state[kap_at, source, j] for j in range(5)]
+    even = lax.axis_index("near") % 2 == 0
+
+    def own_row(z):
+        if z in (0, 3):
+            lower = even if z == 3 else jnp.logical_not(even)
+            change = lambda f, j: jnp.where(lower, own_a[f, j], own_b[f, j])
+        else:
+            change = lambda f, j: total[f, z, j]
+        half = [[base[f, z, j] - (0.5 * step) * change(f, j) for j in range(5)] for f in range(6)]
+        kap = [base[KAP, z, j] for j in range(5)]
         for u in half + [kap]:
             edge = pltpu.roll(pltpu.roll(u[3], BW, 1), 1, 0)
             u[0] = jnp.where(last & (row == 6) & (lane < BW), edge, u[0])
             g = jnp.where((row == 0) & (lane < BW), u[0], u[4])
             g = jnp.where((row == 7) & (lane >= LANES - BW), u[3], g)
             u[4] = jnp.where(first & (row == 0) & (lane >= BW), pltpu.roll(g, LANES - BW, 1), g)
+        return [state_quantities(*(half[f][j] for f in range(6)), kap[j]) for j in range(5)]
+
+    for z in range(4):
+        store_all(q, (z + 1,), own_row(z))
+    for edge, change, target in ((edge_a, change_a, jnp.where(even, 5, 0)), (edge_b, change_b, jnp.where(even, 0, 5))):
         found = []
-        for j in range(5):
-            r, mx, my, mz, e, s = (half[f][j] for f in range(6))
-            inv = 1.0 / r
-            vx, vy, vz = mx * inv, my * inv, mz * inv
-            p = (GAMMA - 1.0) * (e - 0.5 * (mx * vx + my * vy + mz * vz))
-            t = p * inv
-            found.append((r, mx, my, mz, e, s, vx, vy, vz, p, jnp.sqrt(GAMMA * t), t, kap[j]))
+        for j in range(4):
+            half = (edge[f, j] - (0.5 * step) * change[f, j] for f in range(6))
+            found.append(state_quantities(*half, edge[6, j]))
         store_all(q, (target,), found)
-
-    @pl.loop(0, 4, unroll=True)
-    def _(z):
-        half_row(base, total, KAP, z, z + 1)
-
-    @pl.loop(0, 2, unroll=True)
-    def _(e):
-        half_row(edge_q, edge_total, 6, e, 5 * e)
 
     for key, value in z_face_row(q, 0, 4).items():
         zf[key] = value
@@ -420,47 +424,50 @@
     prim, kappa, new_owner = in_hbm(rows_view(primitive)), in_hbm(rows_view(conductivity)), in_hbm(new_owner)
     hbm = pl.BlockSpec(memory_space=pltpu.HBM)
 
-    own, peak, leaving = kernel(
+    side = f32(240, LANES)
+    own, msg_c, msg_d, slab, peak = pl.pallas_call(
         load_kernel,
-        "load",
-        [hbm, hbm, hbm],
-        (f32(7, rows, LANES), f32(1, LANES), f32(8, LANES)),
-        [pltpu.SMEM(new_owner.shape, jnp.int32), pltpu.SemaphoreType.DMA((3,))],
+        out_shape=(f32(7, rows, LANES), side, side, f32(7, rows // 2, LANES), f32(1, LANES)),
+        in_specs=[hbm] * 3,
+        out_specs=(VMEM,) * 5,
+        scratch_shapes=[
+            pltpu.SMEM(new_owner.shape, jnp.int32),
+            pltpu.SemaphoreType.DMA((3,)),
+        ],
+        compiler_params=PARAMS,
+        name="load",
     )(prim, kappa, new_owner)
 
-    side = lambda upper, name: kernel(functools.partial(side_kernel, upper), name, [VMEM] * 2, f32(7, 40, LANES))
+    rec_c = swap(msg_c, lambda c, i: (c ^ 1, i))
+    rec_d = swap(msg_d, lambda c, i: (c, i ^ 1) if c in (0, m - 1) else (outer_partner(c, m), i))
     quantities, sums = f32(NQ, 4, 5, 8, LANES), f32(6, 4, 5, 8, LANES)
-    rec_c = swap(side(True, "upper")(own, leaving), lambda c, i: (c ^ 1, i))
-    msg_d = side(False, "lower")(own, leaving)
-    rec_d = swap(msg_d, lambda c, i: (c, i ^ 1) if c in (0, m - 1) else (outer_partner(c, m), i))
-    slab, peak = kernel(
-        slab_kernel, "slab", [VMEM] * 2, (f32(7, rows // 2, LANES), f32(m * n, 1, LANES)), us=COST["slab"]
-    )(own, peak)
     rec_slab = swap(slab, lambda c, i: (c, outer_partner(i, n)))
+    peak = kernel(copies_kernel, "copies", [VMEM], f32(m * n, 1, LANES))(peak)
     peak = lax.all_to_all(peak, ("curve", "near"), 0, 0, tiled=True)
     ext, msg_a, msg_b, arrival = kernel(
         spread_kernel,
         "spread",
         [VMEM] * 3,
-        (f32(7, 4, 40, LANES), f32(7, 72, LANES), f32(7, 24, LANES), f32(8, LANES)),
+        (f32(7, 4, 40, LANES), f32(7, 72, LANES), f32(128, LANES), f32(8, LANES)),
         us=COST["spread"],
     )(own, rec_c, rec_d)
     rec_a = swap(msg_a, lambda c, i: (c, i ^ 1))
     rec_b = swap(msg_b, lambda c, i: (c, outer_partner(i, n)))
     q, inner = kernel(inner_kernel, "inner", [VMEM] * 2, (quantities, sums), us=COST["inner"])(ext, rec_slab)
-    total, edge_q, edge_total = kernel(
-        outer_kernel,
-        "outer",
-        [VMEM] * 5,
-        (sums, f32(7, 2, 5, 8, LANES), f32(6, 2, 5, 8, LANES)),
-        [pltpu.VMEM((NQ, 6, 5, 8, LANES), jnp.float32), pltpu.VMEM((7, 72, LANES), jnp.float32)],
-        us=COST["outer"],
-    )(q, inner, rec_a, rec_slab, rec_b)
+    found = (f32(7, 4, 8, LANES), f32(6, 4, 8, LANES), f32(6, 5, 8, LANES))
+    rim = pltpu.VMEM((NQ, 3, 5, 8, LANES), jnp.float32)
+    joined = pltpu.VMEM((7, 72, LANES), jnp.float32)
+    side_a = kernel(functools.partial(rim_kernel, True), "rim_a", [VMEM] * 3, found, [rim], us=COST["outer"])(
+        q, inner, rec_a
+    )
+    side_b = kernel(functools.partial(rim_kernel, False), "rim_b", [VMEM] * 4, found, [rim, joined], us=COST["outer"])(
+        q, inner, rec_slab, rec_b
+    )
 
     out = pl.pallas_call(
         second_kernel,
         out_shape=f32(6, rows + 32, LANES),
-        in_specs=[VMEM] * 6 + [hbm],
+        in_specs=[VMEM] * 10 + [hbm],
         out_specs=hbm,
         scratch_shapes=[
             pltpu.VMEM((NQ, 6, 5, 8, LANES), jnp.float32),
@@ -471,7 +478,7 @@
         ],
         compiler_params=PARAMS,
         name="second_section",
-    )(q, total, edge_q, edge_total, arrival, peak, new_owner)
+    )(q, inner, *side_a, *side_b, arrival, peak, new_owner)
     out = jnp.swapaxes(out.reshape(6, (rows + 32) // 4, 4, LANES), 1, 2)
     return out.reshape(1, 6, 4, (rows + 32) // 4 * LANES)
 

time: 21.1 us -> 20.8 us (0.986)
  starting transfers between devices: 11.7 us -> 11.4 us
    all_to_all x1, waiting for transfers between devices: 1.22 us -> 1.71 us  [local(): peak = lax.all_to_all(peak, ('curve', 'near'), 0, 0, tiled=True)]
    ppermute x5, waiting for transfers between devices: 1.34 us -> 0.88 us  [swap(): return lax.ppermute(x, ('curve', 'near'), route)]
    ppermute x5, starting transfers between devices: 6.64 us -> 6.31 us  [swap(): return lax.ppermute(x, ('curve', 'near'), route)]
    pallas_call x5 -> x4, Pallas kernels: 2.82 us -> 2.71 us  [the longest x1 1.14 us: local(): pl.pallas_call(load_kernel, out_shape=(f32(7, rows, LANES), side, side, f...]
where the time goes in v6:
time: 20.8 us; the launch traced here: 20.6 us
  starting transfers between devices  11.4 us (55%)
  Pallas kernels  6.54 us (31%)
  waiting for transfers between devices  2.59 us (12%)
    ppermute x5, starting transfers between devices, swap(): return lax.ppermute(x, ('curve', 'near'), route)  6.31 us
    all_to_all x1, starting transfers between devices, local(): peak = lax.all_to_all(peak, ('curve', 'near'), 0, 0, tiled=True)  5.11 us
    pallas_call x1, Pallas kernels, local(): pl.pallas_call(second_kernel, out_shape=f32(6, rows + 32, LANES), in_spec...  2.29 us
    all_to_all x1, waiting for transfers between devices, local(): peak = lax.all_to_all(peak, ('curve', 'near'), 0, 0, tiled=True)  1.71 us
    pallas_call x1, Pallas kernels, local(): kernel(inner_kernel, 'inner', [VMEM] * 2, (quantities, sums), us=COST['in...  1.37 us
    pallas_call x1, Pallas kernels, local(): pl.pallas_call(load_kernel, out_shape=(f32(7, rows, LANES), side, side, f...  1.14 us
    ppermute x5, waiting for transfers between devices, swap(): return lax.ppermute(x, ('curve', 'near'), route)  0.88 us
    pallas_call x1, Pallas kernels, local(): peak = kernel(copies_kernel, 'copies', [VMEM], f32(m * n, 1, LANES))(peak)  0.61 us
  transfers between devices with their start and end apart: 6, of which 2 were waited for; matrix products, arithmetic and copies ran while one was open for 0% of the time, Pallas kernels for 15%

profile of v6, /device:TPU:0, one launch (start us, length us, event | category | flops | bytes accessed | tf_op | source)
XLA Modules:
  0.0 20.6 jit_solution(11060005657624749983)
XLA Ops:
  0.0 1.1 %load.1 = (f32[7,96,128]{2,1,0:T(8,128)S(1)}, f32[240,128]{1,0:T(8,128)S(1)}, f32[240,128]{1,0:T(8,128)S(1)}, f32[7,48,128]{2,1,0:T(8,128)S(1)}, f32[1,128]{1,0:T(1,128)S(1)}) custom-call(f32[6,96,128]{2,1,0:T(8,128)} %bitcast.15, f32[96,128]{1,0:T(8,128)} %bitcast.16, s32[3]{0:T(128)} %new_owner.3), custom_call_target="tpu_custom_call" | custom-call | tf_op jit(solution)/shard_map/load/pallas_call | solution.py:428
  1.2 2.4 %collective-permute-start.2 = (f32[7,48,128]{2,1,0:T(8,128)S(1)}, f32[7,48,128]{2,1,0:T(8,128)S(1)}, u32[]{:S(2)}, u32[]{:S(2)}) collective-permute-start(f32[7,48,128]{2,1,0:T(8,128)S(1)} %get-tuple-element.26), channel_id=1, source_target_pairs={{0,3},{1,2},{2,1},{3,0},{4,7},{5,6},{6,5},{7,4},{8,11},{9,10},{10,... | collective-permute-start | bytes 516104 | tf_op jit(solution)/shard_map/ppermute | solution.py:393
  3.6 1.5 %collective-permute-start = (f32[240,128]{1,0:T(8,128)S(1)}, f32[240,128]{1,0:T(8,128)S(1)}, u32[]{:S(2)}, u32[]{:S(2)}) collective-permute-start(f32[240,128]{1,0:T(8,128)S(1)} %get-tuple-element.23), channel_id=1, source_target_pairs={{0,4},{1,5},{2,6},{3,7},{4,0},{5,1},{6,2},{7,3},{8,12},{9,13},{10,... | collective-permute-start | bytes 368648 | tf_op jit(solution)/shard_map/ppermute | solution.py:393
  5.1 0.4 %collective-permute-start.1 = (f32[240,128]{1,0:T(8,128)S(1)}, f32[240,128]{1,0:T(8,128)S(1)}, u32[]{:S(2)}, u32[]{:S(2)}) collective-permute-start(f32[240,128]{1,0:T(8,128)S(1)} %get-tuple-element.24), channel_id=1, source_target_pairs={{0,1},{1,0},{2,3},{3,2},{4,8},{5,9},{6,10},{7,11},{8,4},{9,5},{10,... | collective-permute-start | bytes 368648 | tf_op jit(solution)/shard_map/ppermute | solution.py:393
  5.5 0.6 %copies.1 = f32[32,1,128]{2,1,0:T(1,128)} custom-call(f32[1,128]{1,0:T(1,128)S(1)} %get-tuple-element.38.peak), custom_call_target="tpu_custom_call" | custom-call | tf_op jit(solution)/shard_map/copies/pallas_call | solution.py:445
  6.1 5.1 %all-to-all-start = ((f32[32,1,128]{2,1,0:T(1,128)}), f32[32,1,128]{2,1,0:T(1,128)S(1)}, u32[]{:S(2)}, u32[]{:S(2)}) async-start(f32[32,1,128]{2,1,0:T(1,128)} %copies.1), calls=%async_computation | async-start | bytes 32768 | tf_op jit(solution)/shard_map/all_to_all | solution.py:446
  11.2 0.0 collective-permute-done.rec_c
  11.3 0.0 collective-permute-done.1.rec_d
  11.3 0.2 spread.1
  11.4 1.6 %collective-permute-start.4 = (f32[128,128]{1,0:T(8,128)S(1)}, f32[128,128]{1,0:T(8,128)S(1)}, u32[]{:S(2)}, u32[]{:S(2)}) collective-permute-start(f32[128,128]{1,0:T(8,128)S(1)} %get-tuple-element.33), channel_id=1, source_target_pairs={{0,3},{1,2},{2,1},{3,0},{4,7},{5,6},{6,5},{7,4},{8,11},{9,10},{10,... | collective-permute-start | bytes 196616 | tf_op jit(solution)/shard_map/ppermute | solution.py:393
  13.0 0.4 %collective-permute-start.3 = (f32[7,72,128]{2,1,0:T(8,128)S(1)}, f32[7,72,128]{2,1,0:T(8,128)S(1)}, u32[]{:S(2)}, u32[]{:S(2)}) collective-permute-start(f32[7,72,128]{2,1,0:T(8,128)S(1)} %get-tuple-element.29), channel_id=1, source_target_pairs={{0,1},{1,0},{2,3},{3,2},{4,5},{5,4},{6,7},{7,6},{8,9},{9,8},{10,11... | collective-permute-start | bytes 774152 | tf_op jit(solution)/shard_map/ppermute | solution.py:393
  13.4 0.0 collective-permute-done.2.order.refs_0_
  13.4 1.4 %inner.1 = (f32[13,4,5,8,128]{4,3,2,1,0:T(8,128)S(1)}, f32[6,4,5,8,128]{4,3,2,1,0:T(8,128)S(1)}) custom-call(f32[7,4,40,128]{3,2,1,0:T(8,128)S(1)} %get-tuple-element.25.ext, f32[7,48,128]{2,1,0:T(8,128)S(1)} %collective-permute-done.2.order.refs_0_), custom_call_target="tpu_custom_call" | custom-call | flops 20000000000 | bytes 60000000 | tf_op jit(solution)/shard_map/inner/pallas_call | solution.py:456
  14.8 0.9 %collective-permute-done.4.refs_1_ = f32[128,128]{1,0:T(8,128)S(1)} collective-permute-done((f32[128,128]{1,0:T(8,128)S(1)}, f32[128,128]{1,0:T(8,128)S(1)}, u32[]{:S(2)}, u32[]{:S(2)}) %collective-permute-start.4) | collective-permute-done | bytes 65568 | tf_op jit(solution)/shard_map/ppermute | solution.py:393
  15.6 0.5 %rim_b.1 = (f32[7,4,8,128]{3,2,1,0:T(8,128)S(1)}, f32[6,4,8,128]{3,2,1,0:T(8,128)S(1)}, f32[6,5,8,128]{3,2,1,0:T(8,128)S(1)}) custom-call(f32[13,4,5,8,128]{4,3,2,1,0:T(8,128)S(1)} %get-tuple-element.27.q.base, f32[6,4,5,8,128]{4,3,2,1,0:T(8,128)S(1)} %get-tuple-element.28.inner.total, f32[7,48,128]{2,1,0:T(8,128)S(1)} %collective-permute-done.2.order.refs_0_, ...), custom_call_target="tpu_custom_call" | custom-call | flops 20000000000 | bytes 60000000 | tf_op jit(solution)/shard_map/rim_b/pallas_call | solution.py:463
  16.1 0.0 collective-permute-done.3.refs_0_
  16.1 0.5 %rim_a.1 = (f32[7,4,8,128]{3,2,1,0:T(8,128)S(1)}, f32[6,4,8,128]{3,2,1,0:T(8,128)S(1)}, f32[6,5,8,128]{3,2,1,0:T(8,128)S(1)}) custom-call(f32[13,4,5,8,128]{4,3,2,1,0:T(8,128)S(1)} %get-tuple-element.27.q.base, f32[6,4,5,8,128]{4,3,2,1,0:T(8,128)S(1)} %get-tuple-element.28.inner.total, f32[7,72,128]{2,1,0:T(8,128)S(1)} %collective-permute-done.3.refs_0_), custom_call_target="tpu_custom_call" | custom-call | flops 20000000000 | bytes 60000000 | tf_op jit(solution)/shard_map/rim_a/pallas_call | solution.py:460
  16.6 1.7 %all-to-all-done.peak = f32[32,1,128]{2,1,0:T(1,128)S(1)} async-done(((f32[32,1,128]{2,1,0:T(1,128)}), f32[32,1,128]{2,1,0:T(1,128)S(1)}, u32[]{:S(2)}, u32[]{:S(2)}) %all-to-all-start) | async-done | bytes 16416 | tf_op jit(solution)/shard_map/all_to_all | solution.py:446
  18.3 2.3 %second_section.1 = f32[6,128,128]{2,1,0:T(8,128)} custom-call(f32[13,4,5,8,128]{4,3,2,1,0:T(8,128)S(1)} %get-tuple-element.27.q.base, f32[6,4,5,8,128]{4,3,2,1,0:T(8,128)S(1)} %get-tuple-element.28.inner.total, f32[7,4,8,128]{3,2,1,0:T(8,128)S(1)} %get-tuple-element.30.edge_a, f32[6,4,8,128]{3,2,1,0:T(8,128)S(1)} %get-tuple-element.31.change_a, ...), custom_call_target="tpu_custom_call" | custom-call | tf_op jit(solution)/shard_map/second_section/pallas_call | solution.py:467
Async XLA Ops:
  1.2 12.2 %collective-permute-start.2 = (f32[7,48,128]{2,1,0:T(8,128)S(1)}, f32[7,48,128]{2,1,0:T(8,128)S(1)}, u32[]{:S(2)}, u32[]{:S(2)}) collective-permute-start(f32[7,48,128]{2,1,0:T(8,128)S(1)} %get-tuple-element.26), channel_id=1, source_target_pairs={{0,3},{1,2},{2,1},{3,0},{4,7},{5,6},{6,5},{7,4},{8,11},{9,10},{10,... | collective-permute-start | bytes 516104 | tf_op jit(solution)/shard_map/ppermute | solution.py:393
  3.6 7.6 %collective-permute-start = (f32[240,128]{1,0:T(8,128)S(1)}, f32[240,128]{1,0:T(8,128)S(1)}, u32[]{:S(2)}, u32[]{:S(2)}) collective-permute-start(f32[240,128]{1,0:T(8,128)S(1)} %get-tuple-element.23), channel_id=1, source_target_pairs={{0,4},{1,5},{2,6},{3,7},{4,0},{5,1},{6,2},{7,3},{8,12},{9,13},{10,... | collective-permute-start | bytes 368648 | tf_op jit(solution)/shard_map/ppermute | solution.py:393
  5.1 6.1 %collective-permute-start.1 = (f32[240,128]{1,0:T(8,128)S(1)}, f32[240,128]{1,0:T(8,128)S(1)}, u32[]{:S(2)}, u32[]{:S(2)}) collective-permute-start(f32[240,128]{1,0:T(8,128)S(1)} %get-tuple-element.24), channel_id=1, source_target_pairs={{0,1},{1,0},{2,3},{3,2},{4,8},{5,9},{6,10},{7,11},{8,4},{9,5},{10,... | collective-permute-start | bytes 368648 | tf_op jit(solution)/shard_map/ppermute | solution.py:393
  6.1 12.2 %all-to-all-start = ((f32[32,1,128]{2,1,0:T(1,128)}), f32[32,1,128]{2,1,0:T(1,128)S(1)}, u32[]{:S(2)}, u32[]{:S(2)}) async-start(f32[32,1,128]{2,1,0:T(1,128)} %copies.1), calls=%async_computation | async-start | bytes 32768 | tf_op jit(solution)/shard_map/all_to_all | solution.py:446
  11.4 4.2 %collective-permute-start.4 = (f32[128,128]{1,0:T(8,128)S(1)}, f32[128,128]{1,0:T(8,128)S(1)}, u32[]{:S(2)}, u32[]{:S(2)}) collective-permute-start(f32[128,128]{1,0:T(8,128)S(1)} %get-tuple-element.33), channel_id=1, source_target_pairs={{0,3},{1,2},{2,1},{3,0},{4,7},{5,6},{6,5},{7,4},{8,11},{9,10},{10,... | collective-permute-start | bytes 196616 | tf_op jit(solution)/shard_map/ppermute | solution.py:393
  13.0 3.1 %collective-permute-start.3 = (f32[7,72,128]{2,1,0:T(8,128)S(1)}, f32[7,72,128]{2,1,0:T(8,128)S(1)}, u32[]{:S(2)}, u32[]{:S(2)}) collective-permute-start(f32[7,72,128]{2,1,0:T(8,128)S(1)} %get-tuple-element.29), channel_id=1, source_target_pairs={{0,1},{1,0},{2,3},{3,2},{4,5},{5,4},{6,7},{7,6},{8,9},{9,8},{10,11... | collective-permute-start | bytes 774152 | tf_op jit(solution)/shard_map/ppermute | solution.py:393

commit v7 on v6

--- a/solution.py
+++ b/solution.py
@@ -203,11 +203,18 @@
     hx = [(kx[j] + kxu[j]) * (txu[j] - tx[j]) for j in five]
     hy = [(kx[j] + kyu[j]) * (tyu[j] - tx[j]) for j in range(slots)]
 
+    fields = [[at(f, j) for j in five] for f in range(6)]
+    fields_x = [up_x(u, lane) for u in fields]
+    fields_y = [[up_y(v, low) for v in u[:slots]] for u in fields]
+
     def neighbours(f):
-        u = [at(f, j) for j in five]
-        fx = [physical(q, f, j, 0, z) for j in five]
-        fy = [physical(q, f, j, 1, z) for j in range(slots)]
-        return u, fx, fy, up_x(u, lane), up_x(fx, lane), [up_y(v, low) for v in u[:slots]], [up_y(v, low) for v in fy]
+        if f == 0:
+            fx, fux, fy, fuy = fields[1], fields_x[1], fields[2], fields_y[2]
+        else:
+            fx = [physical(q, f, j, 0, z) for j in five]
+            fy = [physical(q, f, j, 1, z) for j in range(slots)]
+            fux, fuy = up_x(fx, lane), [up_y(v, low) for v in fy]
+        return fields[f], fx, fy, fields_x[f], fux, fields_y[f], fuy
 
     def sides(f, u, fx, fy, ux, fux, uy, fuy):
         heat = lambda h: h if f == 4 else None
@@ -328,8 +335,11 @@
     fetch.start()
     peaks = jnp.max(peak[...], axis=0)
     half_lanes = lanes_of((1, LANES)) < LANES // 2
-    speed, top = jnp.max(jnp.where(half_lanes, peaks, 0.0)), jnp.max(jnp.where(half_lanes, 0.0, peaks))
-    step = COURANT / (speed + 6.0 * top)
+    both = jnp.broadcast_to(peaks, shape)
+    swapped = pltpu.roll(both, LANES // 2, 1)
+    speed = jnp.max(jnp.where(lane < LANES // 2, both, 0.0), axis=1, keepdims=True)
+    top = jnp.max(jnp.where(lane < LANES // 2, 0.0, both), axis=1, keepdims=True)
+    step = jnp.broadcast_to(COURANT / (speed + 6.0 * top), shape)
 
     even = lax.axis_index("near") % 2 == 0
 

time: 20.8 us -> 20.7 us (level)
  no operation moved by 1% of the time
where the time goes in v7:
time: 20.7 us; the launch traced here: 20.5 us
  starting transfers between devices  11.4 us (55%)
  Pallas kernels  6.47 us (31%)
  waiting for transfers between devices  2.57 us (12%)
    ppermute x5, starting transfers between devices, swap(): return lax.ppermute(x, ('curve', 'near'), route)  6.31 us
    all_to_all x1, starting transfers between devices, local(): peak = lax.all_to_all(peak, ('curve', 'near'), 0, 0, tiled=True)  5.11 us
    pallas_call x1, Pallas kernels, local(): pl.pallas_call(second_kernel, out_shape=f32(6, rows + 32, LANES), in_spec...  2.21 us
    all_to_all x1, waiting for transfers between devices, local(): peak = lax.all_to_all(peak, ('curve', 'near'), 0, 0, tiled=True)  1.7 us
    pallas_call x1, Pallas kernels, local(): kernel(inner_kernel, 'inner', [VMEM] * 2, (quantities, sums), us=COST['in...  1.37 us
    pallas_call x1, Pallas kernels, local(): pl.pallas_call(load_kernel, out_shape=(f32(7, rows, LANES), side, side, f...  1.14 us
    ppermute x5, waiting for transfers between devices, swap(): return lax.ppermute(x, ('curve', 'near'), route)  0.88 us
    pallas_call x1, Pallas kernels, local(): peak = kernel(copies_kernel, 'copies', [VMEM], f32(m * n, 1, LANES))(peak)  0.61 us
  transfers between devices with their start and end apart: 6, of which 2 were waited for; matrix products, arithmetic and copies ran while one was open for 0% of the time, Pallas kernels for 15%

profile of v7, /device:TPU:0, one launch (start us, length us, event | category | flops | bytes accessed | tf_op | source)
XLA Modules:
  0.0 20.5 jit_solution(15170177953099818517)
XLA Ops:
  0.0 1.1 %load.1 = (f32[7,96,128]{2,1,0:T(8,128)S(1)}, f32[240,128]{1,0:T(8,128)S(1)}, f32[240,128]{1,0:T(8,128)S(1)}, f32[7,48,128]{2,1,0:T(8,128)S(1)}, f32[1,128]{1,0:T(1,128)S(1)}) custom-call(f32[6,96,128]{2,1,0:T(8,128)} %bitcast.15, f32[96,128]{1,0:T(8,128)} %bitcast.16, s32[3]{0:T(128)} %new_owner.3), custom_call_target="tpu_custom_call" | custom-call | tf_op jit(solution)/shard_map/load/pallas_call | solution.py:438
  1.2 2.4 %collective-permute-start.2 = (f32[7,48,128]{2,1,0:T(8,128)S(1)}, f32[7,48,128]{2,1,0:T(8,128)S(1)}, u32[]{:S(2)}, u32[]{:S(2)}) collective-permute-start(f32[7,48,128]{2,1,0:T(8,128)S(1)} %get-tuple-element.26), channel_id=1, source_target_pairs={{0,3},{1,2},{2,1},{3,0},{4,7},{5,6},{6,5},{7,4},{8,11},{9,10},{10,... | collective-permute-start | bytes 516104 | tf_op jit(solution)/shard_map/ppermute | solution.py:403
  3.6 1.5 %collective-permute-start = (f32[240,128]{1,0:T(8,128)S(1)}, f32[240,128]{1,0:T(8,128)S(1)}, u32[]{:S(2)}, u32[]{:S(2)}) collective-permute-start(f32[240,128]{1,0:T(8,128)S(1)} %get-tuple-element.23), channel_id=1, source_target_pairs={{0,4},{1,5},{2,6},{3,7},{4,0},{5,1},{6,2},{7,3},{8,12},{9,13},{10,... | collective-permute-start | bytes 368648 | tf_op jit(solution)/shard_map/ppermute | solution.py:403
  5.1 0.4 %collective-permute-start.1 = (f32[240,128]{1,0:T(8,128)S(1)}, f32[240,128]{1,0:T(8,128)S(1)}, u32[]{:S(2)}, u32[]{:S(2)}) collective-permute-start(f32[240,128]{1,0:T(8,128)S(1)} %get-tuple-element.24), channel_id=1, source_target_pairs={{0,1},{1,0},{2,3},{3,2},{4,8},{5,9},{6,10},{7,11},{8,4},{9,5},{10,... | collective-permute-start | bytes 368648 | tf_op jit(solution)/shard_map/ppermute | solution.py:403
  5.5 0.6 %copies.1 = f32[32,1,128]{2,1,0:T(1,128)} custom-call(f32[1,128]{1,0:T(1,128)S(1)} %get-tuple-element.38.peak), custom_call_target="tpu_custom_call" | custom-call | tf_op jit(solution)/shard_map/copies/pallas_call | solution.py:455
  6.1 5.1 %all-to-all-start = ((f32[32,1,128]{2,1,0:T(1,128)}), f32[32,1,128]{2,1,0:T(1,128)S(1)}, u32[]{:S(2)}, u32[]{:S(2)}) async-start(f32[32,1,128]{2,1,0:T(1,128)} %copies.1), calls=%async_computation | async-start | bytes 32768 | tf_op jit(solution)/shard_map/all_to_all | solution.py:456
  11.2 0.0 collective-permute-done.rec_c
  11.3 0.0 collective-permute-done.1.rec_d
  11.3 0.2 spread.1
  11.4 1.6 %collective-permute-start.4 = (f32[128,128]{1,0:T(8,128)S(1)}, f32[128,128]{1,0:T(8,128)S(1)}, u32[]{:S(2)}, u32[]{:S(2)}) collective-permute-start(f32[128,128]{1,0:T(8,128)S(1)} %get-tuple-element.33), channel_id=1, source_target_pairs={{0,3},{1,2},{2,1},{3,0},{4,7},{5,6},{6,5},{7,4},{8,11},{9,10},{10,... | collective-permute-start | bytes 196616 | tf_op jit(solution)/shard_map/ppermute | solution.py:403
  13.0 0.4 %collective-permute-start.3 = (f32[7,72,128]{2,1,0:T(8,128)S(1)}, f32[7,72,128]{2,1,0:T(8,128)S(1)}, u32[]{:S(2)}, u32[]{:S(2)}) collective-permute-start(f32[7,72,128]{2,1,0:T(8,128)S(1)} %get-tuple-element.29), channel_id=1, source_target_pairs={{0,1},{1,0},{2,3},{3,2},{4,5},{5,4},{6,7},{7,6},{8,9},{9,8},{10,11... | collective-permute-start | bytes 774152 | tf_op jit(solution)/shard_map/ppermute | solution.py:403
  13.4 0.0 collective-permute-done.2.order.refs_0_
  13.4 1.4 %inner.1 = (f32[13,4,5,8,128]{4,3,2,1,0:T(8,128)S(1)}, f32[6,4,5,8,128]{4,3,2,1,0:T(8,128)S(1)}) custom-call(f32[7,4,40,128]{3,2,1,0:T(8,128)S(1)} %get-tuple-element.25.ext, f32[7,48,128]{2,1,0:T(8,128)S(1)} %collective-permute-done.2.order.refs_0_), custom_call_target="tpu_custom_call" | custom-call | flops 20000000000 | bytes 60000000 | tf_op jit(solution)/shard_map/inner/pallas_call | solution.py:466
  14.8 0.9 %collective-permute-done.4.refs_1_ = f32[128,128]{1,0:T(8,128)S(1)} collective-permute-done((f32[128,128]{1,0:T(8,128)S(1)}, f32[128,128]{1,0:T(8,128)S(1)}, u32[]{:S(2)}, u32[]{:S(2)}) %collective-permute-start.4) | collective-permute-done | bytes 65568 | tf_op jit(solution)/shard_map/ppermute | solution.py:403
  15.6 0.5 %rim_b.1 = (f32[7,4,8,128]{3,2,1,0:T(8,128)S(1)}, f32[6,4,8,128]{3,2,1,0:T(8,128)S(1)}, f32[6,5,8,128]{3,2,1,0:T(8,128)S(1)}) custom-call(f32[13,4,5,8,128]{4,3,2,1,0:T(8,128)S(1)} %get-tuple-element.27.q.base, f32[6,4,5,8,128]{4,3,2,1,0:T(8,128)S(1)} %get-tuple-element.28.inner.total, f32[7,48,128]{2,1,0:T(8,128)S(1)} %collective-permute-done.2.order.refs_0_, ...), custom_call_target="tpu_custom_call" | custom-call | flops 20000000000 | bytes 60000000 | tf_op jit(solution)/shard_map/rim_b/pallas_call | solution.py:473
  16.1 0.0 collective-permute-done.3.refs_0_
  16.1 0.5 %rim_a.1 = (f32[7,4,8,128]{3,2,1,0:T(8,128)S(1)}, f32[6,4,8,128]{3,2,1,0:T(8,128)S(1)}, f32[6,5,8,128]{3,2,1,0:T(8,128)S(1)}) custom-call(f32[13,4,5,8,128]{4,3,2,1,0:T(8,128)S(1)} %get-tuple-element.27.q.base, f32[6,4,5,8,128]{4,3,2,1,0:T(8,128)S(1)} %get-tuple-element.28.inner.total, f32[7,72,128]{2,1,0:T(8,128)S(1)} %collective-permute-done.3.refs_0_), custom_call_target="tpu_custom_call" | custom-call | flops 20000000000 | bytes 60000000 | tf_op jit(solution)/shard_map/rim_a/pallas_call | solution.py:470
  16.6 1.7 %all-to-all-done.peak = f32[32,1,128]{2,1,0:T(1,128)S(1)} async-done(((f32[32,1,128]{2,1,0:T(1,128)}), f32[32,1,128]{2,1,0:T(1,128)S(1)}, u32[]{:S(2)}, u32[]{:S(2)}) %all-to-all-start) | async-done | bytes 16416 | tf_op jit(solution)/shard_map/all_to_all | solution.py:456
  18.3 2.2 %second_section.1 = f32[6,128,128]{2,1,0:T(8,128)} custom-call(f32[13,4,5,8,128]{4,3,2,1,0:T(8,128)S(1)} %get-tuple-element.27.q.base, f32[6,4,5,8,128]{4,3,2,1,0:T(8,128)S(1)} %get-tuple-element.28.inner.total, f32[7,4,8,128]{3,2,1,0:T(8,128)S(1)} %get-tuple-element.30.edge_a, f32[6,4,8,128]{3,2,1,0:T(8,128)S(1)} %get-tuple-element.31.change_a, ...), custom_call_target="tpu_custom_call" | custom-call | tf_op jit(solution)/shard_map/second_section/pallas_call | solution.py:477
Async XLA Ops:
  1.2 12.2 %collective-permute-start.2 = (f32[7,48,128]{2,1,0:T(8,128)S(1)}, f32[7,48,128]{2,1,0:T(8,128)S(1)}, u32[]{:S(2)}, u32[]{:S(2)}) collective-permute-start(f32[7,48,128]{2,1,0:T(8,128)S(1)} %get-tuple-element.26), channel_id=1, source_target_pairs={{0,3},{1,2},{2,1},{3,0},{4,7},{5,6},{6,5},{7,4},{8,11},{9,10},{10,... | collective-permute-start | bytes 516104 | tf_op jit(solution)/shard_map/ppermute | solution.py:403
  3.6 7.6 %collective-permute-start = (f32[240,128]{1,0:T(8,128)S(1)}, f32[240,128]{1,0:T(8,128)S(1)}, u32[]{:S(2)}, u32[]{:S(2)}) collective-permute-start(f32[240,128]{1,0:T(8,128)S(1)} %get-tuple-element.23), channel_id=1, source_target_pairs={{0,4},{1,5},{2,6},{3,7},{4,0},{5,1},{6,2},{7,3},{8,12},{9,13},{10,... | collective-permute-start | bytes 368648 | tf_op jit(solution)/shard_map/ppermute | solution.py:403
  5.1 6.1 %collective-permute-start.1 = (f32[240,128]{1,0:T(8,128)S(1)}, f32[240,128]{1,0:T(8,128)S(1)}, u32[]{:S(2)}, u32[]{:S(2)}) collective-permute-start(f32[240,128]{1,0:T(8,128)S(1)} %get-tuple-element.24), channel_id=1, source_target_pairs={{0,1},{1,0},{2,3},{3,2},{4,8},{5,9},{6,10},{7,11},{8,4},{9,5},{10,... | collective-permute-start | bytes 368648 | tf_op jit(solution)/shard_map/ppermute | solution.py:403
  6.1 12.2 %all-to-all-start = ((f32[32,1,128]{2,1,0:T(1,128)}), f32[32,1,128]{2,1,0:T(1,128)S(1)}, u32[]{:S(2)}, u32[]{:S(2)}) async-start(f32[32,1,128]{2,1,0:T(1,128)} %copies.1), calls=%async_computation | async-start | bytes 32768 | tf_op jit(solution)/shard_map/all_to_all | solution.py:456
  11.4 4.2 %collective-permute-start.4 = (f32[128,128]{1,0:T(8,128)S(1)}, f32[128,128]{1,0:T(8,128)S(1)}, u32[]{:S(2)}, u32[]{:S(2)}) collective-permute-start(f32[128,128]{1,0:T(8,128)S(1)} %get-tuple-element.33), channel_id=1, source_target_pairs={{0,3},{1,2},{2,1},{3,0},{4,7},{5,6},{6,5},{7,4},{8,11},{9,10},{10,... | collective-permute-start | bytes 196616 | tf_op jit(solution)/shard_map/ppermute | solution.py:403
  13.0 3.1 %collective-permute-start.3 = (f32[7,72,128]{2,1,0:T(8,128)S(1)}, f32[7,72,128]{2,1,0:T(8,128)S(1)}, u32[]{:S(2)}, u32[]{:S(2)}) collective-permute-start(f32[7,72,128]{2,1,0:T(8,128)S(1)} %get-tuple-element.29), channel_id=1, source_target_pairs={{0,1},{1,0},{2,3},{3,2},{4,5},{5,4},{6,7},{7,6},{8,9},{9,8},{10,11... | collective-permute-start | bytes 774152 | tf_op jit(solution)/shard_map/ppermute | solution.py:403

commit v8 on v7

--- a/solution.py
+++ b/solution.py
@@ -37,9 +37,9 @@
     total = own.shape[1]
     groups = total // 32
     copies = [
-        pltpu.make_async_copy(prim, own.at[pl.ds(0, 6)], sems.at[0]),
-        pltpu.make_async_copy(kappa, own.at[6], sems.at[1]),
-        pltpu.make_async_copy(new_owner, owner, sems.at[2]),
+        *(pltpu.make_async_copy(prim.at[f], own.at[f], sems.at[f]) for f in range(6)),
+        pltpu.make_async_copy(kappa, own.at[6], sems.at[6]),
+        pltpu.make_async_copy(new_owner, owner, sems.at[7]),
     ]
     for copy in copies:
         copy.start()
@@ -442,7 +442,7 @@
         out_specs=(VMEM,) * 5,
         scratch_shapes=[
             pltpu.SMEM(new_owner.shape, jnp.int32),
-            pltpu.SemaphoreType.DMA((3,)),
+            pltpu.SemaphoreType.DMA((8,)),
         ],
         compiler_params=PARAMS,
         name="load",

time: 20.7 us -> 20.8 us (level)
  no operation moved by 1% of the time
where the time goes in v8:
time: 20.8 us; the launch traced here: 20.6 us
  starting transfers between devices  11.4 us (55%)
  Pallas kernels  6.49 us (31%)
  waiting for transfers between devices  2.57 us (12%)
    ppermute x5, starting transfers between devices, swap(): return lax.ppermute(x, ('curve', 'near'), route)  6.31 us
    all_to_all x1, starting transfers between devices, local(): peak = lax.all_to_all(peak, ('curve', 'near'), 0, 0, tiled=True)  5.11 us
    pallas_call x1, Pallas kernels, local(): pl.pallas_call(second_kernel, out_shape=f32(6, rows + 32, LANES), in_spec...  2.21 us
    all_to_all x1, waiting for transfers between devices, local(): peak = lax.all_to_all(peak, ('curve', 'near'), 0, 0, tiled=True)  1.7 us
    pallas_call x1, Pallas kernels, local(): kernel(inner_kernel, 'inner', [VMEM] * 2, (quantities, sums), us=COST['in...  1.37 us
    pallas_call x1, Pallas kernels, local(): pl.pallas_call(load_kernel, out_shape=(f32(7, rows, LANES), side, side, f...  1.16 us
    ppermute x5, waiting for transfers between devices, swap(): return lax.ppermute(x, ('curve', 'near'), route)  0.88 us
    pallas_call x1, Pallas kernels, local(): peak = kernel(copies_kernel, 'copies', [VMEM], f32(m * n, 1, LANES))(peak)  0.61 us
  transfers between devices with their start and end apart: 6, of which 2 were waited for; matrix products, arithmetic and copies ran while one was open for 0% of the time, Pallas kernels for 15%

profile of v8, /device:TPU:0, one launch (start us, length us, event | category | flops | bytes accessed | tf_op | source)
XLA Modules:
  0.0 20.6 jit_solution(11770662771479394175)
XLA Ops:
  0.0 1.2 %load.1 = (f32[7,96,128]{2,1,0:T(8,128)S(1)}, f32[240,128]{1,0:T(8,128)S(1)}, f32[240,128]{1,0:T(8,128)S(1)}, f32[7,48,128]{2,1,0:T(8,128)S(1)}, f32[1,128]{1,0:T(1,128)S(1)}) custom-call(f32[6,96,128]{2,1,0:T(8,128)} %bitcast.15, f32[96,128]{1,0:T(8,128)} %bitcast.16, s32[3]{0:T(128)} %new_owner.3), custom_call_target="tpu_custom_call" | custom-call | tf_op jit(solution)/shard_map/load/pallas_call | solution.py:438
  1.2 2.4 %collective-permute-start.2 = (f32[7,48,128]{2,1,0:T(8,128)S(1)}, f32[7,48,128]{2,1,0:T(8,128)S(1)}, u32[]{:S(2)}, u32[]{:S(2)}) collective-permute-start(f32[7,48,128]{2,1,0:T(8,128)S(1)} %get-tuple-element.26), channel_id=1, source_target_pairs={{0,3},{1,2},{2,1},{3,0},{4,7},{5,6},{6,5},{7,4},{8,11},{9,10},{10,... | collective-permute-start | bytes 516104 | tf_op jit(solution)/shard_map/ppermute | solution.py:403
  3.6 1.5 %collective-permute-start = (f32[240,128]{1,0:T(8,128)S(1)}, f32[240,128]{1,0:T(8,128)S(1)}, u32[]{:S(2)}, u32[]{:S(2)}) collective-permute-start(f32[240,128]{1,0:T(8,128)S(1)} %get-tuple-element.23), channel_id=1, source_target_pairs={{0,4},{1,5},{2,6},{3,7},{4,0},{5,1},{6,2},{7,3},{8,12},{9,13},{10,... | collective-permute-start | bytes 368648 | tf_op jit(solution)/shard_map/ppermute | solution.py:403
  5.1 0.4 %collective-permute-start.1 = (f32[240,128]{1,0:T(8,128)S(1)}, f32[240,128]{1,0:T(8,128)S(1)}, u32[]{:S(2)}, u32[]{:S(2)}) collective-permute-start(f32[240,128]{1,0:T(8,128)S(1)} %get-tuple-element.24), channel_id=1, source_target_pairs={{0,1},{1,0},{2,3},{3,2},{4,8},{5,9},{6,10},{7,11},{8,4},{9,5},{10,... | collective-permute-start | bytes 368648 | tf_op jit(solution)/shard_map/ppermute | solution.py:403
  5.5 0.6 %copies.1 = f32[32,1,128]{2,1,0:T(1,128)} custom-call(f32[1,128]{1,0:T(1,128)S(1)} %get-tuple-element.38.peak), custom_call_target="tpu_custom_call" | custom-call | tf_op jit(solution)/shard_map/copies/pallas_call | solution.py:455
  6.1 5.1 %all-to-all-start = ((f32[32,1,128]{2,1,0:T(1,128)}), f32[32,1,128]{2,1,0:T(1,128)S(1)}, u32[]{:S(2)}, u32[]{:S(2)}) async-start(f32[32,1,128]{2,1,0:T(1,128)} %copies.1), calls=%async_computation | async-start | bytes 32768 | tf_op jit(solution)/shard_map/all_to_all | solution.py:456
  11.3 0.0 collective-permute-done.rec_c
  11.3 0.0 collective-permute-done.1.rec_d
  11.3 0.2 spread.1
  11.5 1.6 %collective-permute-start.4 = (f32[128,128]{1,0:T(8,128)S(1)}, f32[128,128]{1,0:T(8,128)S(1)}, u32[]{:S(2)}, u32[]{:S(2)}) collective-permute-start(f32[128,128]{1,0:T(8,128)S(1)} %get-tuple-element.33), channel_id=1, source_target_pairs={{0,3},{1,2},{2,1},{3,0},{4,7},{5,6},{6,5},{7,4},{8,11},{9,10},{10,... | collective-permute-start | bytes 196616 | tf_op jit(solution)/shard_map/ppermute | solution.py:403
  13.0 0.4 %collective-permute-start.3 = (f32[7,72,128]{2,1,0:T(8,128)S(1)}, f32[7,72,128]{2,1,0:T(8,128)S(1)}, u32[]{:S(2)}, u32[]{:S(2)}) collective-permute-start(f32[7,72,128]{2,1,0:T(8,128)S(1)} %get-tuple-element.29), channel_id=1, source_target_pairs={{0,1},{1,0},{2,3},{3,2},{4,5},{5,4},{6,7},{7,6},{8,9},{9,8},{10,11... | collective-permute-start | bytes 774152 | tf_op jit(solution)/shard_map/ppermute | solution.py:403
  13.4 0.0 collective-permute-done.2.order.refs_0_
  13.4 1.4 %inner.1 = (f32[13,4,5,8,128]{4,3,2,1,0:T(8,128)S(1)}, f32[6,4,5,8,128]{4,3,2,1,0:T(8,128)S(1)}) custom-call(f32[7,4,40,128]{3,2,1,0:T(8,128)S(1)} %get-tuple-element.25.ext, f32[7,48,128]{2,1,0:T(8,128)S(1)} %collective-permute-done.2.order.refs_0_), custom_call_target="tpu_custom_call" | custom-call | flops 20000000000 | bytes 60000000 | tf_op jit(solution)/shard_map/inner/pallas_call | solution.py:466
  14.8 0.9 %collective-permute-done.4.refs_1_ = f32[128,128]{1,0:T(8,128)S(1)} collective-permute-done((f32[128,128]{1,0:T(8,128)S(1)}, f32[128,128]{1,0:T(8,128)S(1)}, u32[]{:S(2)}, u32[]{:S(2)}) %collective-permute-start.4) | collective-permute-done | bytes 65568 | tf_op jit(solution)/shard_map/ppermute | solution.py:403
  15.7 0.5 %rim_b.1 = (f32[7,4,8,128]{3,2,1,0:T(8,128)S(1)}, f32[6,4,8,128]{3,2,1,0:T(8,128)S(1)}, f32[6,5,8,128]{3,2,1,0:T(8,128)S(1)}) custom-call(f32[13,4,5,8,128]{4,3,2,1,0:T(8,128)S(1)} %get-tuple-element.27.q.base, f32[6,4,5,8,128]{4,3,2,1,0:T(8,128)S(1)} %get-tuple-element.28.inner.total, f32[7,48,128]{2,1,0:T(8,128)S(1)} %collective-permute-done.2.order.refs_0_, ...), custom_call_target="tpu_custom_call" | custom-call | flops 20000000000 | bytes 60000000 | tf_op jit(solution)/shard_map/rim_b/pallas_call | solution.py:473
  16.2 0.0 collective-permute-done.3.refs_0_
  16.2 0.5 %rim_a.1 = (f32[7,4,8,128]{3,2,1,0:T(8,128)S(1)}, f32[6,4,8,128]{3,2,1,0:T(8,128)S(1)}, f32[6,5,8,128]{3,2,1,0:T(8,128)S(1)}) custom-call(f32[13,4,5,8,128]{4,3,2,1,0:T(8,128)S(1)} %get-tuple-element.27.q.base, f32[6,4,5,8,128]{4,3,2,1,0:T(8,128)S(1)} %get-tuple-element.28.inner.total, f32[7,72,128]{2,1,0:T(8,128)S(1)} %collective-permute-done.3.refs_0_), custom_call_target="tpu_custom_call" | custom-call | flops 20000000000 | bytes 60000000 | tf_op jit(solution)/shard_map/rim_a/pallas_call | solution.py:470
  16.6 1.7 %all-to-all-done.peak = f32[32,1,128]{2,1,0:T(1,128)S(1)} async-done(((f32[32,1,128]{2,1,0:T(1,128)}), f32[32,1,128]{2,1,0:T(1,128)S(1)}, u32[]{:S(2)}, u32[]{:S(2)}) %all-to-all-start) | async-done | bytes 16416 | tf_op jit(solution)/shard_map/all_to_all | solution.py:456
  18.3 2.2 %second_section.1 = f32[6,128,128]{2,1,0:T(8,128)} custom-call(f32[13,4,5,8,128]{4,3,2,1,0:T(8,128)S(1)} %get-tuple-element.27.q.base, f32[6,4,5,8,128]{4,3,2,1,0:T(8,128)S(1)} %get-tuple-element.28.inner.total, f32[7,4,8,128]{3,2,1,0:T(8,128)S(1)} %get-tuple-element.30.edge_a, f32[6,4,8,128]{3,2,1,0:T(8,128)S(1)} %get-tuple-element.31.change_a, ...), custom_call_target="tpu_custom_call" | custom-call | tf_op jit(solution)/shard_map/second_section/pallas_call | solution.py:477
Async XLA Ops:
  1.2 12.2 %collective-permute-start.2 = (f32[7,48,128]{2,1,0:T(8,128)S(1)}, f32[7,48,128]{2,1,0:T(8,128)S(1)}, u32[]{:S(2)}, u32[]{:S(2)}) collective-permute-start(f32[7,48,128]{2,1,0:T(8,128)S(1)} %get-tuple-element.26), channel_id=1, source_target_pairs={{0,3},{1,2},{2,1},{3,0},{4,7},{5,6},{6,5},{7,4},{8,11},{9,10},{10,... | collective-permute-start | bytes 516104 | tf_op jit(solution)/shard_map/ppermute | solution.py:403
  3.6 7.6 %collective-permute-start = (f32[240,128]{1,0:T(8,128)S(1)}, f32[240,128]{1,0:T(8,128)S(1)}, u32[]{:S(2)}, u32[]{:S(2)}) collective-permute-start(f32[240,128]{1,0:T(8,128)S(1)} %get-tuple-element.23), channel_id=1, source_target_pairs={{0,4},{1,5},{2,6},{3,7},{4,0},{5,1},{6,2},{7,3},{8,12},{9,13},{10,... | collective-permute-start | bytes 368648 | tf_op jit(solution)/shard_map/ppermute | solution.py:403
  5.1 6.1 %collective-permute-start.1 = (f32[240,128]{1,0:T(8,128)S(1)}, f32[240,128]{1,0:T(8,128)S(1)}, u32[]{:S(2)}, u32[]{:S(2)}) collective-permute-start(f32[240,128]{1,0:T(8,128)S(1)} %get-tuple-element.24), channel_id=1, source_target_pairs={{0,1},{1,0},{2,3},{3,2},{4,8},{5,9},{6,10},{7,11},{8,4},{9,5},{10,... | collective-permute-start | bytes 368648 | tf_op jit(solution)/shard_map/ppermute | solution.py:403
  6.1 12.2 %all-to-all-start = ((f32[32,1,128]{2,1,0:T(1,128)}), f32[32,1,128]{2,1,0:T(1,128)S(1)}, u32[]{:S(2)}, u32[]{:S(2)}) async-start(f32[32,1,128]{2,1,0:T(1,128)} %copies.1), calls=%async_computation | async-start | bytes 32768 | tf_op jit(solution)/shard_map/all_to_all | solution.py:456
  11.5 4.2 %collective-permute-start.4 = (f32[128,128]{1,0:T(8,128)S(1)}, f32[128,128]{1,0:T(8,128)S(1)}, u32[]{:S(2)}, u32[]{:S(2)}) collective-permute-start(f32[128,128]{1,0:T(8,128)S(1)} %get-tuple-element.33), channel_id=1, source_target_pairs={{0,3},{1,2},{2,1},{3,0},{4,7},{5,6},{6,5},{7,4},{8,11},{9,10},{10,... | collective-permute-start | bytes 196616 | tf_op jit(solution)/shard_map/ppermute | solution.py:403
  13.0 3.1 %collective-permute-start.3 = (f32[7,72,128]{2,1,0:T(8,128)S(1)}, f32[7,72,128]{2,1,0:T(8,128)S(1)}, u32[]{:S(2)}, u32[]{:S(2)}) collective-permute-start(f32[7,72,128]{2,1,0:T(8,128)S(1)} %get-tuple-element.29), channel_id=1, source_target_pairs={{0,1},{1,0},{2,3},{3,2},{4,5},{5,4},{6,7},{7,6},{8,9},{9,8},{10,11... | collective-permute-start | bytes 774152 | tf_op jit(solution)/shard_map/ppermute | solution.py:403
